TPU v7x, 32 devices: a whole 2x2x4 slice. The times are simulated.
32 devices in a mesh: ctx: 8 (over z, y), fsdp: 4 (over x, core).
Axes of the slice: x: 2, y: 2, z: 4, core: 2. Of those that a mesh axis runs over, the one named last changes fastest.
Arguments:
- tokens: bfloat16 [4, 3584, 1024], P('fsdp', 'ctx'), may hold values from -6 to 6
- cotangent: bfloat16 [4, 3584, 1024], P('fsdp', 'ctx'), may hold values from -6 to 6
- block_table: int32 [16], replicated, may hold values from 0 to 15, as said below
- mixer_gain: float32 [1024], replicated, may hold values from 0.5 to 1.5
- in_proj: bfloat16 [1024, 3352], P('fsdp'), may hold values from -0.1875 to 0.1875
- conv_weight: float32 [4, 1792], replicated, may hold values from -0.5 to 0.5
- conv_bias: float32 [1792], replicated, may hold values from -0.5 to 0.5
- step_bias: float32 [24], replicated, may hold values from -3 to 0
- decay_log: float32 [24], replicated, may hold values from -20 to 0, as said below
- skip_gain: float32 [24], replicated, may hold values from 0.5 to 1.5
- gated_gain: float32 [1536], replicated, may hold values from 0.5 to 1.5
- out_proj: bfloat16 [1536, 1024], P('fsdp'), may hold values from -0.15625 to 0.15625
- attention_in: bfloat16 [1024, 768], P('fsdp'), may hold values from -0.1875 to 0.1875
- attention_out: bfloat16 [512, 1024], P('fsdp'), may hold values from -6 to 6
- feed_gain: float32 [1024], replicated, may hold values from 0.5 to 1.5
- gate_up: bfloat16 [1024, 4096], P('fsdp'), may hold values from -0.1875 to 0.1875
- down_proj: bfloat16 [2048, 1024], P('fsdp'), may hold values from -0.125 to 0.125
Outputs:
- output: bfloat16 [4, 3584, 1024], P('fsdp', 'ctx')
- input_grad: float32 [4, 3584, 1024], P('fsdp', 'ctx')
- grad_mixer_gain: float32 [1024], replicated
- grad_in_proj: float32 [1024, 3352], P(('ctx', 'fsdp'))
- grad_conv_weight: float32 [4, 1792], replicated
- grad_conv_bias: float32 [1792], replicated
- grad_step_bias: float32 [24], replicated
- grad_decay_log: float32 [24], replicated
- grad_skip_gain: float32 [24], replicated
- grad_gated_gain: float32 [1536], replicated
- grad_out_proj: float32 [1536, 1024], P(('ctx', 'fsdp'))
- grad_attention_in: float32 [1024, 768], P(('ctx', 'fsdp'))
- grad_attention_out: float32 [512, 1024], P(('ctx', 'fsdp'))
- grad_feed_gain: float32 [1024], replicated
- grad_gate_up: float32 [1024, 4096], P(('ctx', 'fsdp'))
- grad_down_proj: float32 [2048, 1024], P(('ctx', 'fsdp'))
Inputs may be any that keep to these rules, and one draw needn't show every extreme that they name: `block_table`: entries 2 d and 2 d + 1 hold the blocks d and 15 - d, in an order drawn for each d. exp(decay_log) lies between 0.2 / 224 and 4 / 224.
All inputs are finite; a program needn't handle non-finite values.
Results may differ from a plain program's by a relative error of at most 0.014.
The roundings to bfloat16 on the way count: a program that leaves them out, or rounds other values in their place, can miss the bound.
Values may be sent and summed in bfloat16 or wider, within the bound.
No kernel may reach another device: no remote copies, remote signals or barrier semaphores. Data moves between devices by JAX's collectives and lax.ppermute only.
A program may use at most 256 MiB of HBM per device.

v0:
```python
import jax
import jax.numpy as jnp
from jax import lax
from jax.sharding import PartitionSpec as P

DI = 1536
MH = 24
MP = 64
NS = 128
KCONV = 4
QUERY_HEADS = 8
KEY_VALUE_HEADS = 2
HEAD_WIDTH = 64
FF = 2048
CONV = 1792


highest = lax.Precision.HIGHEST
epsilon = 1e-05
rope_base = 100000000000.0
score_scale = 0.125
masked_fill_value = -1e30


def extended_2(array, sides, width):
    for axis, dim in sides:
        devices, length = (lax.axis_size(axis), array.shape[dim])
        up = [(i, (i + 1) % devices) for i in range(devices - 1)]
        down = [(j, i) for i, j in up]
        last = lax.slice_in_dim(array, length - width, length, axis=dim)
        initial = lax.slice_in_dim(array, 0, width, axis=dim)
        before = lax.ppermute(last, axis, up)
        after = lax.ppermute(initial, axis, down)
        array = jnp.concatenate([before, array, after], axis=dim)
    return array


def entering(array, axis, combine, identity):
    devices, mine = (lax.axis_size(axis), lax.axis_index(axis))
    everything = jax.tree.map(
        lambda part, kind: lax.all_gather(part.astype(kind), axis),
        array,
        (jnp.bfloat16, jnp.bfloat16),
    )
    start = jax.tree.map(
        lambda part, zero: jnp.broadcast_to(jnp.asarray(zero, part.dtype), part.shape),
        array,
        identity,
    )

    def lap(k, before):
        reached = k < mine
        new = combine(
            before, jax.tree.map(lambda part, own: part[k].astype(own.dtype), everything, array)
        )
        return jax.tree.map(lambda a, b: jnp.where(reached, a, b), new, before)

    return lax.fori_loop(0, devices, lap, start)


def prefix(array, axis, join, neutral, backward):
    count = lax.axis_size(axis)
    place = lax.axis_index(axis)
    ahead = count - 1 - place if backward else place
    gathered = jax.tree.map(
        lambda a, kind: lax.all_gather(a.astype(kind), axis),
        array,
        jax.tree.map(lambda a: jnp.bfloat16 if a.dtype == jnp.float32 else a.dtype, array),
    )
    state = jax.tree.map(lambda a, e: jnp.zeros_like(a) + jnp.asarray(e, a.dtype), array, neutral)

    def one(lap, state):
        source = count - 1 - lap if backward else lap
        return join(
            state,
            jax.tree.map(
                lambda a, own: lax.dynamic_index_in_dim(a, source, 0, False).astype(own.dtype),
                gathered,
                array,
            ),
        )

    return lax.fori_loop(0, ahead, one, state)


def norm_scale(value_rows):
    return lax.rsqrt(jnp.mean(value_rows * value_rows, axis=-1, keepdims=True) + epsilon)


def norm_backward(grad_norm, value_rows, scale):
    return scale * (
        grad_norm
        - value_rows * scale * scale * jnp.mean(grad_norm * value_rows, axis=-1, keepdims=True)
    )


def matmul(left, right):
    return jnp.dot(left, right, preferred_element_type=jnp.float32)


def row_contract(left, right):
    return lax.dot_general(
        left, right, (((0,), (0,)), ((), ())), preferred_element_type=jnp.float32
    )


def backward_product(grad_rows, weight):
    return lax.dot_general(
        grad_rows, weight, (((1,), (1,)), ((), ())), preferred_element_type=jnp.float32
    )


def rotary_embedding(value_rows, token_positions, direction):
    half_size = value_rows.shape[-1] // 2
    freqs = jnp.exp(
        -(jnp.arange(half_size, dtype=jnp.float32) * (2.0 / value_rows.shape[-1]))
        * jnp.log(rope_base)
    )
    angles = token_positions.astype(jnp.float32)[:, None] * freqs[None, :]
    cosine = jnp.cos(angles)[:, None, :]
    sine = direction * jnp.sin(angles)[:, None, :]
    first_half = value_rows[..., :half_size]
    second_half = value_rows[..., half_size:]
    return jnp.concatenate(
        [first_half * cosine - second_half * sine, second_half * cosine + first_half * sine],
        axis=-1,
    )


def conv_block(previous, raw_rows, conv_weight, conv_bias):
    extended = jnp.concatenate([previous, raw_rows], axis=0)
    row_count = raw_rows.shape[0]
    running = conv_bias[None, :] + conv_weight[0][None, :] * extended[0:row_count]
    for offset in range(1, conv_weight.shape[0]):
        running = running + conv_weight[offset][None, :] * extended[offset : offset + row_count]
    return jax.nn.silu(running)


def scan_local(inputs, b_rows, c_rows, step_size, decay_rate, skip_gain):
    log_decay = step_size * decay_rate[None, :]
    cumulative = jnp.cumsum(log_decay, axis=0)
    row_count = inputs.shape[0]
    causal = jnp.arange(row_count)[:, None] >= jnp.arange(row_count)[None, :]
    log_gap = cumulative.T[:, :, None] - cumulative.T[:, None, :]
    decays = jnp.exp(jnp.where(causal[None], log_gap, masked_fill_value))
    pair_scores = jnp.dot(c_rows, b_rows.T, precision=highest)
    weighted = decays * pair_scores[None]
    scaled_in = inputs * step_size[:, :, None]
    partial_out = (
        jnp.einsum("hts,shp->thp", weighted, scaled_in, precision=highest)
        + skip_gain[None, :, None] * inputs
    )
    tail_decay = jnp.exp(cumulative[-1][None, :] - cumulative)
    update = jnp.einsum("sh,shp,sn->hpn", tail_decay, scaled_in, b_rows, precision=highest)
    return (partial_out, cumulative, update)


def scan_carry(state_in, c_rows, cumulative):
    return (
        jnp.einsum("hpn,tn->thp", state_in, c_rows, precision=highest)
        * jnp.exp(cumulative)[:, :, None]
    )


def scan_block(inputs, b_rows, c_rows, step_size, decay_rate, skip_gain, state_in):
    partial_out, cumulative, update = scan_local(
        inputs, b_rows, c_rows, step_size, decay_rate, skip_gain
    )
    result = partial_out + scan_carry(state_in, c_rows, cumulative)
    state_out = jnp.exp(cumulative[-1])[:, None, None] * state_in + update
    return (result, state_out)


def combine_affine(earlier, later):
    return (earlier[0] * later[0], later[0][:, None, None] * earlier[1] + later[1])


def local(
    tokens,
    cotangent,
    block_table,
    mixer_gain,
    in_proj,
    conv_weight,
    conv_bias,
    step_bias,
    decay_log,
    skip_gain,
    gated_gain,
    out_proj,
    attention_in,
    attention_out,
    feed_gain,
    gate_up,
    down_proj,
):
    ctx_count = lax.axis_size("ctx")
    my_index = lax.axis_index("ctx")
    is_last = my_index == ctx_count - 1
    device_rows = tokens.shape[1]
    half_rows = device_rows // 2
    lag_rows = KCONV - 1
    slot_first = lax.dynamic_index_in_dim(block_table, 2 * my_index, keepdims=False)
    swapped = slot_first != my_index

    def arrange(value_rows):
        first_half = value_rows[:half_rows]
        second_half = value_rows[half_rows:]
        return jnp.concatenate(
            [
                jnp.where(swapped, second_half, first_half),
                jnp.where(swapped, first_half, second_half),
            ],
            axis=0,
        )

    block_ids = jnp.concatenate(
        [
            jnp.full((half_rows,), my_index, jnp.int32),
            jnp.full((half_rows,), 2 * ctx_count - 1 - my_index, jnp.int32),
        ]
    )
    token_positions = block_ids * half_rows + jnp.tile(jnp.arange(half_rows, dtype=jnp.int32), 2)
    hidden = arrange(tokens[0]).astype(jnp.float32)
    out_grad = arrange(cotangent[0]).astype(jnp.float32)
    full_in, full_qkv, full_out, full_output_weight, full_gu, full_down = (
        lax.all_gather(in_proj, "fsdp", axis=0, tiled=True),
        lax.all_gather(attention_in, "fsdp", axis=0, tiled=True),
        lax.all_gather(out_proj, "fsdp", axis=0, tiled=True),
        lax.all_gather(attention_out, "fsdp", axis=0, tiled=True),
        lax.all_gather(gate_up, "fsdp", axis=0, tiled=True),
        lax.all_gather(down_proj, "fsdp", axis=0, tiled=True),
    )
    scale_one = norm_scale(hidden)
    normed_one = (hidden * scale_one * mixer_gain).astype(jnp.bfloat16)
    projected = matmul(normed_one, full_in)
    query_key_value_rows = matmul(normed_one, full_qkv)
    gate_z = projected[:, :DI]
    raw_conv = projected[:, DI : DI + CONV]
    step_raw = projected[:, DI + CONV :]
    early_tail = raw_conv[half_rows - lag_rows : half_rows]
    edges = jnp.concatenate([raw_conv[device_rows - lag_rows :], early_tail], axis=0)
    rimmed = extended_2(edges.astype(jnp.bfloat16), (("ctx", 0),), KCONV - 1).astype(edges.dtype)
    prev_early = rimmed[:lag_rows]
    prev_late = jnp.where(is_last, early_tail, rimmed[rimmed.shape[0] - lag_rows :])
    raw_early = raw_conv[:half_rows]
    raw_late = raw_conv[half_rows:]
    mixed = jnp.concatenate(
        [
            conv_block(prev_early, raw_early, conv_weight, conv_bias),
            conv_block(prev_late, raw_late, conv_weight, conv_bias),
        ],
        axis=0,
    )
    inputs = mixed[:, :DI].reshape(device_rows, MH, MP)
    b_rows = mixed[:, DI : DI + NS]
    c_rows = mixed[:, DI + NS :]
    step_size = jax.nn.softplus(step_raw + step_bias[None, :])
    decay_rate = -jnp.exp(decay_log)
    early_rows = slice(0, half_rows)
    late_rows = slice(half_rows, device_rows)
    part_early, cum_early, update_early = scan_local(
        inputs[early_rows],
        b_rows[early_rows],
        c_rows[early_rows],
        step_size[early_rows],
        decay_rate,
        skip_gain,
    )
    part_late, cum_late, update_late = scan_local(
        inputs[late_rows],
        b_rows[late_rows],
        c_rows[late_rows],
        step_size[late_rows],
        decay_rate,
        skip_gain,
    )
    fade_early = jnp.exp(cum_early[-1])
    fade_late = jnp.exp(cum_late[-1])
    identity = (jnp.ones((MH,), jnp.float32), jnp.zeros((MH, MP, NS), jnp.float32))
    before_early = entering((fade_early, update_early), "ctx", combine_affine, identity)
    state_early = before_early[1]
    after_early = fade_early[:, None, None] * state_early + update_early
    seeded = jnp.where(is_last, fade_late[:, None, None] * after_early + update_late, update_late)
    before_late = prefix((fade_late, seeded), "ctx", combine_affine, identity, True)
    state_late = jnp.where(is_last, after_early, before_late[1])
    scan_out = jnp.concatenate(
        [
            part_early + scan_carry(state_early, c_rows[early_rows], cum_early),
            part_late + scan_carry(state_late, c_rows[late_rows], cum_late),
        ],
        axis=0,
    ).reshape(device_rows, DI)
    silu_z = jax.nn.silu(gate_z)
    gated = scan_out * silu_z
    scale_gated = norm_scale(gated)
    gated_low = (gated * scale_gated * gated_gain).astype(jnp.bfloat16)
    mamba_out = matmul(gated_low, full_out)
    query_matrix = rotary_embedding(
        query_key_value_rows[:, : QUERY_HEADS * HEAD_WIDTH].reshape(
            device_rows, QUERY_HEADS, HEAD_WIDTH
        ),
        token_positions,
        1.0,
    ).astype(jnp.bfloat16)
    query_matrix = query_matrix.reshape(
        device_rows, KEY_VALUE_HEADS, QUERY_HEADS // KEY_VALUE_HEADS, HEAD_WIDTH
    )
    key_rows_narrow = rotary_embedding(
        query_key_value_rows[
            :, QUERY_HEADS * HEAD_WIDTH : (QUERY_HEADS + KEY_VALUE_HEADS) * HEAD_WIDTH
        ].reshape(device_rows, KEY_VALUE_HEADS, HEAD_WIDTH),
        token_positions,
        1.0,
    )
    key_rows_narrow = key_rows_narrow.astype(jnp.bfloat16)
    pairs = jnp.concatenate(
        [
            key_rows_narrow.reshape(device_rows, KEY_VALUE_HEADS * HEAD_WIDTH),
            query_key_value_rows[:, (QUERY_HEADS + KEY_VALUE_HEADS) * HEAD_WIDTH :].astype(
                jnp.bfloat16
            ),
        ],
        axis=1,
    )
    all_pairs = lax.all_gather(pairs, "ctx", axis=0, tiled=True)
    seq_rows = all_pairs.shape[0]
    pairwise_columns = 2 * KEY_VALUE_HEADS * HEAD_WIDTH
    by_device = all_pairs.reshape(ctx_count, 2, half_rows, pairwise_columns)
    ordered = jnp.concatenate(
        [
            by_device[:, 0].reshape(ctx_count * half_rows, pairwise_columns),
            by_device[::-1, 1].reshape(ctx_count * half_rows, pairwise_columns),
        ],
        axis=0,
    )
    key_tile_block = min(512, seq_rows)
    required_rows = ((2 * ctx_count - my_index) * half_rows + key_tile_block - 1) // key_tile_block

    def block_scores(start):
        pairwise_block = lax.dynamic_slice_in_dim(ordered, start, key_tile_block, 0)
        pos_block = start + jnp.arange(key_tile_block, dtype=jnp.int32)
        key_portion = pairwise_block[:, : KEY_VALUE_HEADS * HEAD_WIDTH].reshape(
            key_tile_block, KEY_VALUE_HEADS, HEAD_WIDTH
        )
        value_portion = pairwise_block[:, KEY_VALUE_HEADS * HEAD_WIDTH :].reshape(
            key_tile_block, KEY_VALUE_HEADS, HEAD_WIDTH
        )
        raw_scores = (
            jnp.einsum(
                "qgrd,kgd->grqk", query_matrix, key_portion, preferred_element_type=jnp.float32
            )
            * score_scale
        )
        allowed = pos_block[None, :] <= token_positions[:, None]
        return (raw_scores, allowed, key_portion, value_portion)

    def max_step(index, carry):
        top_score, total = carry
        raw_scores, allowed, _, _ = block_scores(index * key_tile_block)
        masked = jnp.where(allowed, raw_scores, masked_fill_value)
        fresh = jnp.maximum(top_score, jnp.max(masked, axis=-1))
        total = total * jnp.exp(top_score - fresh) + jnp.sum(
            jnp.where(allowed, jnp.exp(masked - fresh[..., None]), 0.0), axis=-1
        )
        return (fresh, total)

    initial_maximum = jnp.full(
        (KEY_VALUE_HEADS, QUERY_HEADS // KEY_VALUE_HEADS, device_rows),
        masked_fill_value,
        jnp.float32,
    )
    initial_sum = jnp.zeros(
        (KEY_VALUE_HEADS, QUERY_HEADS // KEY_VALUE_HEADS, device_rows), jnp.float32
    )
    top_score, total = lax.fori_loop(0, required_rows, max_step, (initial_maximum, initial_sum))
    log_total = top_score + jnp.log(total)

    def output_increment(index, accum):
        raw_scores, allowed, _, value_portion = block_scores(index * key_tile_block)
        probs = jnp.where(allowed, jnp.exp(raw_scores - log_total[..., None]), 0.0).astype(
            jnp.bfloat16
        )
        return accum + jnp.einsum(
            "grqk,kgd->qgrd", probs, value_portion, preferred_element_type=jnp.float32
        )

    attn_float = lax.fori_loop(
        0,
        required_rows,
        output_increment,
        jnp.zeros(
            (device_rows, KEY_VALUE_HEADS, QUERY_HEADS // KEY_VALUE_HEADS, HEAD_WIDTH), jnp.float32
        ),
    )
    attn_low = attn_float.reshape(device_rows, QUERY_HEADS * HEAD_WIDTH).astype(jnp.bfloat16)
    attn_out = matmul(attn_low, full_output_weight)
    second = hidden + mamba_out + attn_out
    scale_two = norm_scale(second)
    normed_two = (second * scale_two * feed_gain).astype(jnp.bfloat16)
    gate_rows = matmul(normed_two, full_gu)
    gate_part = gate_rows[:, :FF]
    up_part = gate_rows[:, FF:]
    sig_gate = jax.nn.sigmoid(gate_part)
    silu_gate = gate_part * sig_gate
    activated = (silu_gate * up_part).astype(jnp.bfloat16)
    result = second + matmul(activated, full_down)
    down_grad = out_grad.astype(jnp.bfloat16)
    grad_down = row_contract(activated, down_grad)
    act_grad = backward_product(down_grad, full_down)
    gate_grad = act_grad * up_part * sig_gate * (1.0 + gate_part * (1.0 - sig_gate))
    up_grad = act_grad * silu_gate
    gu_grad = jnp.concatenate([gate_grad, up_grad], axis=1).astype(jnp.bfloat16)
    grad_gu = row_contract(normed_two, gu_grad)
    normed_two_grad = backward_product(gu_grad, full_gu)
    grad_feed = jnp.sum(normed_two_grad * second * scale_two, axis=0)
    resid_grad = out_grad + norm_backward(normed_two_grad * feed_gain, second, scale_two)
    branch_gradient = resid_grad.astype(jnp.bfloat16)
    grad_out = row_contract(gated_low, branch_gradient)
    grad_o = row_contract(attn_low, branch_gradient)
    gated_grad = backward_product(branch_gradient, full_out)
    attn_grad = (
        backward_product(branch_gradient, full_output_weight)
        .astype(jnp.bfloat16)
        .reshape(device_rows, KEY_VALUE_HEADS, QUERY_HEADS // KEY_VALUE_HEADS, HEAD_WIDTH)
    )
    row_dot = jnp.einsum("qgrd,qgrd->grq", attn_grad.astype(jnp.float32), attn_float)

    def grad_step(index, carry):
        query_accum, pair_buffer = carry
        start = index * key_tile_block
        raw_scores, allowed, key_portion, value_portion = block_scores(start)
        probs = jnp.where(allowed, jnp.exp(raw_scores - log_total[..., None]), 0.0)
        prob_grad = jnp.einsum(
            "qgrd,kgd->grqk", attn_grad, value_portion, preferred_element_type=jnp.float32
        )
        score_grad = (probs * (prob_grad - row_dot[..., None])).astype(jnp.bfloat16)
        query_accum = query_accum + score_scale * jnp.einsum(
            "grqk,kgd->qgrd", score_grad, key_portion, preferred_element_type=jnp.float32
        )
        key_gradient = score_scale * jnp.einsum(
            "grqk,qgrd->kgd", score_grad, query_matrix, preferred_element_type=jnp.float32
        )
        value_gradient = jnp.einsum(
            "grqk,qgrd->kgd",
            probs.astype(jnp.bfloat16),
            attn_grad,
            preferred_element_type=jnp.float32,
        )
        fresh_rows = jnp.concatenate(
            [
                key_gradient.reshape(key_tile_block, KEY_VALUE_HEADS * HEAD_WIDTH),
                value_gradient.reshape(key_tile_block, KEY_VALUE_HEADS * HEAD_WIDTH),
            ],
            axis=1,
        )
        return (query_accum, lax.dynamic_update_slice_in_dim(pair_buffer, fresh_rows, start, 0))

    query_grad, pair_ordered = lax.fori_loop(
        0,
        required_rows,
        grad_step,
        (
            jnp.zeros(
                (device_rows, KEY_VALUE_HEADS, QUERY_HEADS // KEY_VALUE_HEADS, HEAD_WIDTH),
                jnp.float32,
            ),
            jnp.zeros((seq_rows, pairwise_columns), jnp.float32),
        ),
    )
    early_back = pair_ordered[: ctx_count * half_rows].reshape(
        ctx_count, half_rows, pairwise_columns
    )
    late_back = pair_ordered[ctx_count * half_rows :].reshape(
        ctx_count, half_rows, pairwise_columns
    )[::-1]
    pair_terms = jnp.stack([early_back, late_back], axis=1).reshape(seq_rows, pairwise_columns)
    pairwise_gradient = lax.psum_scatter(
        pair_terms.astype(jnp.bfloat16), "ctx", scatter_dimension=0, tiled=True
    ).astype(jnp.float32)
    query_pre = rotary_embedding(
        query_grad.reshape(device_rows, QUERY_HEADS, HEAD_WIDTH), token_positions, -1.0
    )
    key_unrotated = rotary_embedding(
        pairwise_gradient[:, : KEY_VALUE_HEADS * HEAD_WIDTH].reshape(
            device_rows, KEY_VALUE_HEADS, HEAD_WIDTH
        ),
        token_positions,
        -1.0,
    )
    qkv_grad = jnp.concatenate(
        [
            query_pre.reshape(device_rows, QUERY_HEADS * HEAD_WIDTH),
            key_unrotated.reshape(device_rows, KEY_VALUE_HEADS * HEAD_WIDTH),
            pairwise_gradient[:, KEY_VALUE_HEADS * HEAD_WIDTH :],
        ],
        axis=1,
    ).astype(jnp.bfloat16)
    grad_qkv = row_contract(normed_one, qkv_grad)
    normed_one_grad = backward_product(qkv_grad, full_qkv)
    grad_gated = jnp.sum(gated_grad * gated * scale_gated, axis=0)
    pre_grad = norm_backward(gated_grad * gated_gain, gated, scale_gated)
    sig_z = jax.nn.sigmoid(gate_z)
    z_grad = pre_grad * scan_out * sig_z * (1.0 + gate_z * (1.0 - sig_z))
    scan_grad = (pre_grad * silu_z).reshape(device_rows, MH, MP)

    def direct_part(grad_block, c_block, cum_block):
        return jnp.einsum(
            "thp,tn->hpn", grad_block * jnp.exp(cum_block)[:, :, None], c_block, precision=highest
        )

    direct_early = direct_part(scan_grad[early_rows], c_rows[early_rows], cum_early)
    direct_late = direct_part(scan_grad[late_rows], c_rows[late_rows], cum_late)
    after_late_g = prefix((fade_late, direct_late), "ctx", combine_affine, identity, False)
    carry_late = after_late_g[1]
    into_late = direct_late + fade_late[:, None, None] * carry_late
    seeded_grad = jnp.where(
        is_last, direct_early + fade_early[:, None, None] * into_late, direct_early
    )
    after_early_g = prefix((fade_early, seeded_grad), "ctx", combine_affine, identity, True)
    carry_early = jnp.where(is_last, into_late, after_early_g[1])

    def block_grads(rows_slice, state_in, carry_out):
        primal = (
            inputs[rows_slice],
            b_rows[rows_slice],
            c_rows[rows_slice],
            step_size[rows_slice],
            decay_rate,
            skip_gain,
            state_in,
        )
        _, pullback = jax.vjp(scan_block, *primal)
        return pullback((scan_grad[rows_slice], carry_out))

    grads_early = block_grads(early_rows, state_early, carry_early)
    grads_late = block_grads(late_rows, state_late, carry_late)
    grad_decay = (grads_early[4] + grads_late[4]) * decay_rate
    grad_skip = grads_early[5] + grads_late[5]
    mixed_early_grad = jnp.concatenate(
        [grads_early[0].reshape(half_rows, DI), grads_early[1], grads_early[2]], axis=1
    )
    mixed_late_grad = jnp.concatenate(
        [grads_late[0].reshape(half_rows, DI), grads_late[1], grads_late[2]], axis=1
    )
    step_grad = jnp.concatenate([grads_early[3], grads_late[3]], axis=0)
    step_raw_grad = step_grad * jax.nn.sigmoid(step_raw + step_bias[None, :])
    grad_step = jnp.sum(step_raw_grad, axis=0)
    _, conv_pull_early = jax.vjp(conv_block, prev_early, raw_early, conv_weight, conv_bias)
    prev_early_grad, raw_early_grad, weight_early_grad, bias_early_grad = conv_pull_early(
        mixed_early_grad
    )
    _, conv_pull_late = jax.vjp(conv_block, prev_late, raw_late, conv_weight, conv_bias)
    prev_late_grad, raw_late_grad, weight_late_grad, bias_late_grad = conv_pull_late(
        mixed_late_grad
    )
    backs = jnp.concatenate([prev_early_grad, prev_late_grad], axis=0)
    returned = extended_2(backs.astype(jnp.bfloat16), (("ctx", 0),), KCONV - 1).astype(backs.dtype)
    early_tail_grad = returned[returned.shape[0] - lag_rows :] + jnp.where(
        is_last, prev_late_grad, 0.0
    )
    late_tail_grad = returned[:lag_rows]
    raw_early_grad = raw_early_grad.at[half_rows - lag_rows :].add(early_tail_grad)
    raw_late_grad = raw_late_grad.at[half_rows - lag_rows :].add(late_tail_grad)
    raw_grad = jnp.concatenate([raw_early_grad, raw_late_grad], axis=0)
    proj_grad = jnp.concatenate([z_grad, raw_grad, step_raw_grad], axis=1).astype(jnp.bfloat16)
    grad_in = row_contract(normed_one, proj_grad)
    normed_one_grad = normed_one_grad + backward_product(proj_grad, full_in)
    grad_mixer = jnp.sum(normed_one_grad * hidden * scale_one, axis=0)
    input_grad = resid_grad + norm_backward(normed_one_grad * mixer_gain, hidden, scale_one)
    grad_mats = (grad_in, grad_qkv, grad_out, grad_o, grad_gu, grad_down)
    reduced = (
        lax.psum_scatter(grad_mats[0], ("ctx", "fsdp"), scatter_dimension=0, tiled=True),
        lax.psum_scatter(grad_mats[1], ("ctx", "fsdp"), scatter_dimension=0, tiled=True),
        lax.psum_scatter(grad_mats[2], ("ctx", "fsdp"), scatter_dimension=0, tiled=True),
        lax.psum_scatter(grad_mats[3], ("ctx", "fsdp"), scatter_dimension=0, tiled=True),
        lax.psum_scatter(grad_mats[4], ("ctx", "fsdp"), scatter_dimension=0, tiled=True),
        lax.psum_scatter(grad_mats[5], ("ctx", "fsdp"), scatter_dimension=0, tiled=True),
    )
    smalls = lax.psum(
        (
            grad_mixer,
            grad_gated,
            grad_feed,
            weight_early_grad + weight_late_grad,
            bias_early_grad + bias_late_grad,
            grad_step,
            grad_decay,
            grad_skip,
        ),
        ("ctx", "fsdp"),
    )
    return (
        arrange(result).astype(jnp.bfloat16)[None],
        arrange(input_grad)[None],
        smalls[0],
        reduced[0],
        smalls[3],
        smalls[4],
        smalls[5],
        smalls[6],
        smalls[7],
        smalls[1],
        reduced[2],
        reduced[1],
        reduced[3],
        smalls[2],
        reduced[4],
        reduced[5],
    )


def solution(mesh):
    return jax.shard_map(
        local,
        mesh=mesh,
        in_specs=(
            P("fsdp", "ctx", None),
            P("fsdp", "ctx", None),
            P(),
            P(),
            P("fsdp", None),
            P(),
            P(),
            P(),
            P(),
            P(),
            P(),
            P("fsdp", None),
            P("fsdp", None),
            P("fsdp", None),
            P(),
            P("fsdp", None),
            P("fsdp", None),
        ),
        out_specs=(
            P("fsdp", "ctx", None),
            P("fsdp", "ctx", None),
            P(),
            P(("ctx", "fsdp"), None),
            P(),
            P(),
            P(),
            P(),
            P(),
            P(),
            P(("ctx", "fsdp"), None),
            P(("ctx", "fsdp"), None),
            P(("ctx", "fsdp"), None),
            P(),
            P(("ctx", "fsdp"), None),
            P(("ctx", "fsdp"), None),
        ),
        check_vma=False,
    )
```

profile of v0, /device:TPU:0, one launch (start us, length us, event | category | flops | bytes accessed | tf_op | source)
XLA Modules:
  0.0 1525.2 jit_solution(12425185214468284308)
XLA Ops:
  10.6 52.3 %all-gather.18.cloned.1.call-done = bf16[1024,3352]{0,1:T(8,128)(2,1)} async-done(((bf16[256,3352]{0,1:T(8,128)(2,1)}), bf16[1024,3352]{0,1:T(8,128)(2,1)}) %all-gather.18.cloned.1.call-update) | async-done | bytes 6864912 | tf_op jit(solution)/shard_map/all_gather | solution.py:227
  62.9 6.0 fusion.234
  73.9 4.5 collective-permute-start
  82.6 7.3 fusion.90
  106.3 19.5 %all-gather.4 = bf16[8,1,24]{2,1,0:T(2,128)(2,1)S(1)} all-gather(bf16[1,1,24]{2,1,0:T(2,128)(2,1)S(1)} %bitcast.516), channel_id=1, replica_groups=mesh['ctx'=8,'fsdp'=4] {'ctx'}, dimensions={0}, use_global_device_ids=true | all-gather | bytes 432 | tf_op jit(solution)/shard_map/all_gather | solution.py:41
  129.2 29.7 %all-gather.32.cloned.1.call-done = bf16[192,64,128]{2,1,0:T(8,128)(2,1)} async-done(((bf16[24,64,128]{2,1,0:T(8,128)(2,1)}), bf16[192,64,128]{2,1,0:T(8,128)(2,1)}) %all-gather.32.cloned.1.call-update) | async-done | bytes 3145744 | tf_op jit(solution)/shard_map/all_gather | solution.py:41
  159.0 9.9 while.96
  177.8 28.7 %all-gather.24.cloned.1.call-done = bf16[3584,256]{1,0:T(8,128)(2,1)} async-done(((bf16[448,256]{1,0:T(8,128)(2,1)}), bf16[3584,256]{1,0:T(8,128)(2,1)}) %all-gather.24.cloned.1.call-update) | async-done | bytes 1835024 | tf_op jit(solution)/shard_map/all_gather | solution.py:326
  214.3 31.9 %while.91 = (s32[]{:T(128)}, f32[2,4,448]{2,1,0:T(4,128)S(1)}, f32[2,4,448]{2,1,0:T(4,128)S(1)}, s32[]{:T(128)}, s32[448]{0:T(512)S(1)}, /*index=5*/bf16[3584,25...) while((s32[]{:T(128)}, f32[2,4,448]{2,1,0:T(4,128)S(1)}, ...), condition=%wide.region_13.14_spmd, body=%wide.region_10.13_spmd.sunk | while | flops 249798144 | bytes 16412587 | solution.py:376
  247.4 42.2 %while.92 = (s32[]{:T(128)}, f32[448,2,4,64]{0,3,2,1:T(8,128)}, s32[]{:T(128)}, bf16[3584,256]{0,1:T(8,128)(2,1)S(1)}, s32[448]{0:T(512)S(1)}, /*index=5*/bf16[4...) while((s32[]{:T(128)}, f32[448,2,4,64]{0,3,2,1:T(8,128)}, ...), condition=%wide.region_15.16_spmd, body=%wide.region_14.15_spmd.sunk | while | flops 477561344 | bytes 3559363 | solution.py:388
  248.3 5.1 fusion.335
  254.3 5.1 fusion.335
  260.3 5.1 fusion.335
  266.3 5.1 fusion.335
  272.4 5.1 fusion.335
  278.4 5.1 fusion.335
  284.4 5.1 fusion.335
  292.5 16.9 %all-gather.5 = bf16[8,1,24]{2,1,0:T(2,128)(2,1)S(1)} all-gather(bf16[1,1,24]{2,1,0:T(2,128)(2,1)S(1)} %bitcast.517), channel_id=1, replica_groups=mesh['ctx'=8,'fsdp'=4] {'ctx'}, dimensions={0}, use_global_device_ids=true | all-gather | bytes 432 | tf_op jit(solution)/shard_map/all_gather | solution.py:66
  316.5 7.6 fusion.92
  324.3 9.2 while.90
  337.2 6.4 fusion.91
  349.9 4.9 multiply_reduce_fusion.4
  354.9 5.6 fusion.229
  363.5 11.9 all-gather.28.cloned.1.call-done
  375.4 9.5 fusion.227
  384.9 26.6 %all-gather.30.cloned.1.call-done = bf16[2048,1024]{1,0:T(8,128)(2,1)} async-done(((bf16[512,1024]{1,0:T(8,128)(2,1)}), bf16[2048,1024]{1,0:T(8,128)(2,1)}) %all-gather.30.cloned.1.call-update) | async-done | bytes 4194320 | tf_op jit(solution)/shard_map/all_gather | solution.py:232
  411.5 9.2 multiply_convert_fusion.1
  420.7 8.8 multiply_reduce_fusion.5
  455.3 71.4 %while.93 = (s32[]{:T(128)}, f32[448,2,4,64]{0,3,2,1:T(8,128)S(1)}, bf16[3584,256]{1,0:T(8,128)(2,1)}, s32[]{:T(128)}, bf16[3584,256]{0,1:T(8,128)(2,1)}, /*inde...) while((s32[]{:T(128)}, f32[448,2,4,64]{0,3,2,1:T(8,128)S(1)}, ...), condition=%wide.region_19.20_spmd, body=%wide.region_18.19_spmd.sunk | while | flops 1194099200 | bytes 40189916 | solution.py:459
  542.8 50.6 %reduce-scatter.22.cloned.1.call-done = bf16[448,256]{1,0:T(8,128)(2,1)} async-done(((bf16[3584,256]{1,0:T(8,128)(2,1)}), bf16[448,256]{1,0:T(8,128)(2,1)}) %reduce-scatter.22.cloned.1.call-update) | async-done | bytes 229392
  604.1 6.3 fusion.228
  611.5 7.1 fusion.174
  629.4 4.8 fusion.114
  634.3 11.9 fusion.43
  652.4 6.8 multiply_reduce_fusion.16
  667.4 13.4 while.95
  686.2 8.2 multiply_reduce_fusion.17
  711.2 6.0 multiply_reduce_fusion.15
  720.0 4.7 collective-permute-start.2
  734.1 11.3 fusion.168
  746.9 10.3 fusion.67
  758.4 5.0 convolution_add_fusion.1
  771.9 38.5 %all-reduce.25 = (f32[1024]{0:T(1024)}, f32[4,1792]{1,0:T(4,128)}, f32[1792]{0:T(1024)}, f32[24]{0:T(128)}, f32[24]{0:T(128)}, /*index=5*/f32[24]{0:T(128)}, f32[1536]{0:T(1024)}, f32[1024]{0:T(1024)}) all-reduce(f32[1024]{0:T(1024)S(1)} %get-tuple-element.661, ...), channel_id=1, replica_groups=mesh['ctx'=8,'fsdp'=4] {'ctx','fsdp'}, use_global_device_ids=true, to_apply=%region_46.47 | all-reduce | flops 12616 | bytes 100928 | tf_op jit(solution)/shard_map/psum | solution.py:580
  814.1 82.9 %reduce-scatter.14.cloned.1.call-done = f32[32,768]{1,0:T(8,128)} async-done(((f32[1024,768]{1,0:T(8,128)}), f32[32,768]{1,0:T(8,128)}) %reduce-scatter.14.cloned.1.call-update) | async-done | bytes 98320 | tf_op jit(solution)/shard_map/reduce_scatter | solution.py:574
  897.0 119.5 %reduce-scatter.12.cloned.1.call-done = f32[48,1024]{1,0:T(8,128)} async-done(((f32[1536,1024]{1,0:T(8,128)}), f32[48,1024]{1,0:T(8,128)}) %reduce-scatter.12.cloned.1.call-update) | async-done | bytes 196624 | tf_op jit(solution)/shard_map/reduce_scatter | solution.py:575
  1016.5 151.1 %reduce-scatter.20.cloned.1.call-done = f32[64,1024]{1,0:T(8,128)} async-done(((f32[2048,1024]{1,0:T(8,128)}), f32[64,1024]{1,0:T(8,128)}) %reduce-scatter.20.cloned.1.call-update) | async-done | bytes 262160 | tf_op jit(solution)/shard_map/reduce_scatter | solution.py:578
  1167.6 166.2 %reduce-scatter.10.cloned.1.call-done = f32[32,3352]{1,0:T(8,128)} async-done(((f32[1024,3352]{1,0:T(8,128)}), f32[32,3352]{1,0:T(8,128)}) %reduce-scatter.10.cloned.1.call-update) | async-done | bytes 429072 | tf_op jit(solution)/shard_map/reduce_scatter | solution.py:573
  1333.8 184.3 %reduce-scatter.18.cloned.1.call-done = f32[32,4096]{1,0:T(8,128)} async-done(((f32[1024,4096]{1,0:T(8,128)}), f32[32,4096]{1,0:T(8,128)}) %reduce-scatter.18.cloned.1.call-update) | async-done | bytes 524304 | tf_op jit(solution)/shard_map/reduce_scatter | solution.py:577
  (787 shorter events, 338.3 us)
Async XLA Ops:
  7.2 55.7 %all-gather.18.cloned.1.call-start = ((), (), s32[]{:S(2)}) async-start(), calls=%async_computation.7 | async-start | bytes 8581120 | tf_op jit(solution)/shard_map/all_gather | solution.py:227
  8.0 54.9 %copy-start.85 = (f32[1024]{0:T(1024)S(1)}, f32[1024]{0:T(1024)}, u32[]{:S(2)}) copy-start(f32[1024]{0:T(1024)} %param.38) | copy-start | bytes 12292
  8.0 91.5 %all-gather.22.cloned.1.call-start = ((), (), s32[]{:S(2)}) async-start(), calls=%async_computation.9 | async-start | bytes 1966080 | tf_op jit(solution)/shard_map/all_gather | solution.py:228
  8.7 150.2 %all-gather.32.cloned.1.call-start = ((), (), s32[]{:S(2)}) async-start(), calls=%async_computation.20 | async-start | bytes 3538944 | tf_op jit(solution)/shard_map/all_gather | solution.py:41
  10.1 58.7 %copy-start.29 = (bf16[224,1024]{1,0:T(8,128)(2,1)}, bf16[224,1024]{1,0:T(8,128)(2,1)S(1)}, u32[]{:S(2)}) copy-start(bf16[224,1024]{1,0:T(8,128)(2,1)S(1)} %get-tuple-element.840) | copy-start | bytes 1376260
  10.1 58.7 %copy-start.32 = (bf16[224,1024]{1,0:T(8,128)(2,1)}, bf16[224,1024]{1,0:T(8,128)(2,1)S(1)}, u32[]{:S(2)}) copy-start(bf16[224,1024]{1,0:T(8,128)(2,1)S(1)} %get-tuple-element.841) | copy-start | bytes 1376260
  10.4 89.1 %copy-start.105 = (f32[448]{0:T(512)}, f32[448]{0:T(512)S(1)}, u32[]{:S(2)}) copy-start(f32[448]{0:T(512)S(1)} %add_rsqrt_fusion.2) | copy-start | bytes 5380
  10.4 68.1 %copy-start.161 = (f32[24]{0:T(128)}, f32[24]{0:T(128)S(1)}, u32[]{:S(2)}) copy-start(f32[24]{0:T(128)S(1)} %exponential_negate_fusion) | copy-start | bytes 292
  10.5 72.0 %copy-start.115 = (f32[1792]{0:T(1024)}, f32[1792]{0:T(1024)S(1)}, u32[]{:S(2)}) copy-start(f32[1792]{0:T(1024)S(1)} %get-tuple-element.681) | copy-start | bytes 21508
  10.5 72.0 %copy-start.117 = (f32[1792]{0:T(1024)}, f32[1792]{0:T(1024)S(1)}, u32[]{:S(2)}) copy-start(f32[1792]{0:T(1024)S(1)} %get-tuple-element.682) | copy-start | bytes 21508
  10.5 72.0 %copy-start.119 = (f32[1792]{0:T(1024)}, f32[1792]{0:T(1024)S(1)}, u32[]{:S(2)}) copy-start(f32[1792]{0:T(1024)S(1)} %get-tuple-element.683) | copy-start | bytes 21508
  10.6 72.0 %copy-start.121 = (f32[1792]{0:T(1024)}, f32[1792]{0:T(1024)S(1)}, u32[]{:S(2)}) copy-start(f32[1792]{0:T(1024)S(1)} %get-tuple-element.684) | copy-start | bytes 21508
  72.6 9.0 collective-permute-start.1
  73.9 7.7 collective-permute-start
  90.0 35.9 %copy-start.16 = (f32[224,1792]{1,0:T(8,128)}, f32[224,1792]{1,0:T(8,128)S(1)}, u32[]{:S(2)}) copy-start(f32[224,1792]{1,0:T(8,128)S(1)} %get-tuple-element.855) | copy-start | bytes 4816900
  98.4 108.1 %all-gather.24.cloned.1.call-start = ((), (), s32[]{:S(2)}) async-start(), calls=%async_computation.10 | async-start | bytes 2064384 | tf_op jit(solution)/shard_map/all_gather | solution.py:326
  99.5 78.0 %copy-start.56 = (f32[448,32]{0,1:T(8,128)}, f32[448,32]{0,1:T(8,128)S(1)}, u32[]{:S(2)}) copy-start(f32[448,32]{0,1:T(8,128)S(1)} %get-tuple-element.871) | copy-start | bytes 172036
  104.3 219.8 %all-gather.34.cloned.1.call-start = ((), (), s32[]{:S(2)}) async-start(), calls=%async_computation.21 | async-start | bytes 3538944 | tf_op jit(solution)/shard_map/all_gather | solution.py:66
  106.1 62.7 %copy-start.65 = (f32[224,24]{0,1:T(8,128)}, f32[224,24]{0,1:T(8,128)S(1)}, u32[]{:S(2)}) copy-start(f32[224,24]{0,1:T(8,128)S(1)} %get-tuple-element.867) | copy-start | bytes 64516
  106.1 62.7 %copy-start.153 = (f32[24]{0:T(128)}, f32[24]{0:T(128)S(1)}, u32[]{:S(2)}) copy-start(f32[24]{0:T(128)S(1)} %exp.111) | copy-start | bytes 292
  129.2 39.6 %copy-start.6 = (f32[224,1536]{0,1:T(8,128)}, f32[224,1536]{0,1:T(8,128)S(1)}, u32[]{:S(2)}) copy-start(f32[224,1536]{0,1:T(8,128)S(1)} %copy.226) | copy-start | bytes 4128772
  172.0 182.9 %all-gather.20.cloned.1.call-start = ((), (), s32[]{:S(2)}) async-start(), calls=%async_computation.8 | async-start | bytes 3932160 | tf_op jit(solution)/shard_map/all_gather | solution.py:229
  172.6 187.9 %all-gather.26.cloned.1.call-start = ((), (), s32[]{:S(2)}) async-start(), calls=%async_computation.11 | async-start | bytes 1310720 | tf_op jit(solution)/shard_map/all_gather | solution.py:230
  173.3 202.1 %all-gather.28.cloned.1.call-start = ((), (), s32[]{:S(2)}) async-start(), calls=%async_computation.12 | async-start | bytes 10485760 | tf_op jit(solution)/shard_map/all_gather | solution.py:231
  174.1 237.4 %all-gather.30.cloned.1.call-start = ((), (), s32[]{:S(2)}) async-start(), calls=%async_computation.13 | async-start | bytes 5242880 | tf_op jit(solution)/shard_map/all_gather | solution.py:232
  174.8 358.1 %all-gather.36.cloned.1.call-start = ((), (), s32[]{:S(2)}) async-start(), calls=%async_computation.22 | async-start | bytes 3538944 | tf_op jit(solution)/shard_map/all_gather | solution.py:66
  247.4 44.9 %copy-start.72 = (f32[256,24]{0,1:T(8,128)S(1)}, f32[256,24]{0,1:T(8,128)}, u32[]{:S(2)}) copy-start(f32[256,24]{0,1:T(8,128)} %copy-done.71) | copy-start | bytes 73732
  289.5 25.8 %copy-start.149 = (f32[2,4,448]{2,1,0:T(4,128)}, f32[2,4,448]{2,1,0:T(4,128)S(1)}, u32[]{:S(2)}) copy-start(f32[2,4,448]{2,1,0:T(4,128)S(1)} %get-tuple-element.1460) | copy-start | bytes 43012
  354.8 80.9 %copy-start.139 = (f32[448]{0:T(512)}, f32[448]{0:T(512)S(1)}, u32[]{:S(2)}) copy-start(f32[448]{0:T(512)S(1)} %add_rsqrt_fusion.1) | copy-start | bytes 5380
  363.4 66.1 %copy-start.18 = (f32[448,1024]{1,0:T(8,128)}, f32[448,1024]{1,0:T(8,128)S(1)}, u32[]{:S(2)}) copy-start(f32[448,1024]{1,0:T(8,128)S(1)} %get-tuple-element.875) | copy-start | bytes 5505028
  363.5 66.1 %copy-start.107 = (f32[448]{0:T(512)}, f32[448]{0:T(512)S(1)}, u32[]{:S(2)}) copy-start(f32[448]{0:T(512)S(1)} %add_rsqrt_fusion) | copy-start | bytes 5380
  448.1 145.2 %reduce-scatter.22.cloned.1.call-start = ((), (), s32[]{:S(2)}) async-start(), calls=%async_computation.24 | async-start | bytes 2064384
  529.9 137.4 %all-gather.38.cloned.1.call-start = ((), (), s32[]{:S(2)}) async-start(), calls=%async_computation.23 | async-start | bytes 3538944 | tf_op jit(solution)/shard_map/all_gather | solution.py:66
  537.6 276.4 %reduce-scatter.16.cloned.1.call-start = ((), (), s32[]{:S(2)}) async-start(), calls=%async_computation.17 | async-start | bytes 2162688 | tf_op jit(solution)/shard_map/reduce_scatter | solution.py:576
  540.8 356.2 %reduce-scatter.14.cloned.1.call-start = ((), (), s32[]{:S(2)}) async-start(), calls=%async_computation.16 | async-start | bytes 3244032 | tf_op jit(solution)/shard_map/reduce_scatter | solution.py:574
  541.9 57.4 %copy-start.57 = (f32[448,32]{0,1:T(8,128)S(1)}, f32[448,32]{0,1:T(8,128)}, u32[]{:S(2)}) copy-start(f32[448,32]{0,1:T(8,128)} %copy-done.56) | copy-start | bytes 172036
  541.9 57.4 %copy-start.67 = (f32[448,32]{0,1:T(8,128)S(1)}, f32[448,32]{0,1:T(8,128)}, u32[]{:S(2)}) copy-start(f32[448,32]{0,1:T(8,128)} %get-tuple-element.869) | copy-start | bytes 172036
  541.9 57.5 %copy-start.30 = (bf16[224,1024]{1,0:T(8,128)(2,1)S(1)}, bf16[224,1024]{1,0:T(8,128)(2,1)}, u32[]{:S(2)}) copy-start(bf16[224,1024]{1,0:T(8,128)(2,1)} %copy-done.29) | copy-start | bytes 1376260
  541.9 57.5 %copy-start.33 = (bf16[224,1024]{1,0:T(8,128)(2,1)S(1)}, bf16[224,1024]{1,0:T(8,128)(2,1)}, u32[]{:S(2)}) copy-start(bf16[224,1024]{1,0:T(8,128)(2,1)} %copy-done.32) | copy-start | bytes 1376260
  541.9 57.5 %copy-start.86 = (f32[1024]{0:T(1024)S(1)}, f32[1024]{0:T(1024)}, u32[]{:S(2)}) copy-start(f32[1024]{0:T(1024)} %param.38) | copy-start | bytes 12292
  541.9 57.5 %copy-start.106 = (f32[448]{0:T(512)S(1)}, f32[448]{0:T(512)}, u32[]{:S(2)}) copy-start(f32[448]{0:T(512)} %copy-done.105) | copy-start | bytes 5380
  603.4 413.1 %reduce-scatter.12.cloned.1.call-start = ((), (), s32[]{:S(2)}) async-start(), calls=%async_computation.15 | async-start | bytes 6488064 | tf_op jit(solution)/shard_map/reduce_scatter | solution.py:575
  610.4 557.2 %reduce-scatter.20.cloned.1.call-start = ((), (), s32[]{:S(2)}) async-start(), calls=%async_computation.19 | async-start | bytes 8650752 | tf_op jit(solution)/shard_map/reduce_scatter | solution.py:578
  618.7 715.2 %reduce-scatter.10.cloned.1.call-start = ((), (), s32[]{:S(2)}) async-start(), calls=%async_computation.14 | async-start | bytes 14598144 | tf_op jit(solution)/shard_map/reduce_scatter | solution.py:573
  718.6 11.8 collective-permute-start.3
  720.0 10.4 collective-permute-start.2
  745.4 772.7 %reduce-scatter.18.cloned.1.call-start = ((), (), s32[]{:S(2)}) async-start(), calls=%async_computation.18 | async-start | bytes 17301504 | tf_op jit(solution)/shard_map/reduce_scatter | solution.py:577
  769.3 41.2 %copy-start.37 = (f32[448,1024]{1,0:T(8,128)S(1)}, f32[448,1024]{1,0:T(8,128)}, u32[]{:S(2)}) copy-start(f32[448,1024]{1,0:T(8,128)} %get-tuple-element.790) | copy-start | bytes 5505028
  (150 other events, 855.5 us)
Sparse Core Ops, SparseCore 0:
  9.6 53.2 all-gather.17
  64.4 19.6 all-gather.21
  98.5 60.4 all-gather.31
  161.6 44.8 all-gather.23
  209.1 59.4 all-gather.33
  270.0 27.1 all-gather.19
  298.8 16.7 all-gather.25
  317.1 58.2 all-gather.27
  377.0 34.4 all-gather.29
  448.2 60.4 all-gather.35
  530.0 63.2 reduce-scatter.21
  596.2 59.2 all-gather.37
  658.5 135.0 reduce-scatter.15
  799.4 97.5 reduce-scatter.13
  903.0 113.4 reduce-scatter.11
  1019.3 148.2 reduce-scatter.19
  1175.0 158.7 reduce-scatter.9
  1336.7 181.4 reduce-scatter.17
where the time goes:
time: 1540 us; the launch traced here: 1530 us
  waiting for transfers between devices  908 us (59%)
  matrix products  301 us (20%)
  other arithmetic  121 us (8%)
  local copies, waits for them, and re-layouts  87 us (6%)
  blocking collectives  75 us (5%)
  between operations  17.6 us (1%)
    reduce_scatter x1, waiting for transfers between devices, local(): lax.psum_scatter(grad_mats[4], ('ctx', 'fsdp'), scatter_dimension=0, tile...  184 us
    reduce_scatter x1, waiting for transfers between devices, local(): lax.psum_scatter(grad_mats[0], ('ctx', 'fsdp'), scatter_dimension=0, tile...  166 us
    reduce_scatter x1, waiting for transfers between devices, local(): lax.psum_scatter(grad_mats[5], ('ctx', 'fsdp'), scatter_dimension=0, tile...  151 us
    reduce_scatter x1, waiting for transfers between devices, local(): lax.psum_scatter(grad_mats[2], ('ctx', 'fsdp'), scatter_dimension=0, tile...  120 us
    reduce_scatter x1, waiting for transfers between devices, local(): lax.psum_scatter(grad_mats[1], ('ctx', 'fsdp'), scatter_dimension=0, tile...  82.9 us
    unnamed x19, waiting for transfers between devices  54.7 us
    all_gather x1, waiting for transfers between devices, local(): lax.all_gather(in_proj, 'fsdp', axis=0, tiled=True)  52.3 us
    dot_general x6, matrix products, scan_local(): jnp.einsum('hts,shp->thp', weighted, scaled_in, precision=highest)  45.7 us
  transfers between devices with their start and end apart: 22, of which 11 were waited for; matrix products, arithmetic and copies ran while one was open for 30% of the time, Pallas kernels for 0%

commit v1 on v0

v1 whole, which is shorter than its diff:
```python
import math

import jax
import jax.numpy as jnp
from jax import lax
from jax.experimental import pallas as pl
from jax.experimental.pallas import tpu as pltpu
from jax.sharding import PartitionSpec as P

DI = 1536
MH = 24
MP = 64
NS = 128
KCONV = 4
QUERY_HEADS = 8
KEY_VALUE_HEADS = 2
HEAD_WIDTH = 64
GROUP = QUERY_HEADS // KEY_VALUE_HEADS
FF = 2048
CONV = 1792
PAIRS = MH // 2

highest = lax.Precision.HIGHEST
epsilon = 1e-05
rope_base = 100000000000.0
score_scale = 0.125
masked_fill_value = -1e30
bf16 = jnp.bfloat16
f32 = jnp.float32


def xor_pairs(count, distance):
    return [(i, i ^ distance) for i in range(count)]


def swap(array, axis, distance):
    return lax.ppermute(array, axis, xor_pairs(lax.axis_size(axis), distance))


def norm_scale(value_rows):
    return lax.rsqrt(jnp.mean(value_rows * value_rows, axis=-1, keepdims=True) + epsilon)


def norm_backward(grad_norm, value_rows, scale):
    return scale * (
        grad_norm
        - value_rows * scale * scale * jnp.mean(grad_norm * value_rows, axis=-1, keepdims=True)
    )


def matmul(left, right):
    return jnp.dot(left, right, preferred_element_type=f32)


def row_contract(left, right):
    return lax.dot_general(left, right, (((0,), (0,)), ((), ())), preferred_element_type=f32)


def backward_product(grad_rows, weight):
    return lax.dot_general(grad_rows, weight, (((1,), (1,)), ((), ())), preferred_element_type=f32)


def edge_exchange(array, width):
    devices, length = lax.axis_size("ctx"), array.shape[0]
    up = [(i, i + 1) for i in range(devices - 1)]
    down = [(j, i) for i, j in up]
    before = lax.ppermute(array[length - width :], "ctx", up)
    after = lax.ppermute(array[:width], "ctx", down)
    return before, after


def gather_weight_fast(weight):
    fs = lax.axis_index("fsdp")
    rows, cols = weight.shape
    half = rows // 2
    y_bit, x_bit, c_bit = lax.axis_index("ctx") % 2, fs // 2, fs % 2
    mine = lax.dynamic_slice_in_dim(weight, y_bit * half, half, 0)
    first = swap(mine, "fsdp", 2)
    second = swap(first, "ctx", 1)
    buf = jnp.zeros((2, 2, 2, half, cols), weight.dtype)
    zero = jnp.int32(0)

    def put(buf, piece, x, c, h):
        piece = piece.reshape(1, 1, -1, half, cols)
        return lax.dynamic_update_slice(buf, piece, (x, c, h, zero, zero))

    buf = put(buf, weight, x_bit, c_bit, zero)
    buf = put(buf, swap(weight, "fsdp", 1), x_bit, 1 - c_bit, zero)
    buf = put(buf, first, 1 - x_bit, c_bit, y_bit)
    buf = put(buf, swap(first, "fsdp", 1), 1 - x_bit, 1 - c_bit, y_bit)
    buf = put(buf, second, 1 - x_bit, c_bit, 1 - y_bit)
    buf = put(buf, swap(second, "fsdp", 1), 1 - x_bit, 1 - c_bit, 1 - y_bit)
    return buf.reshape(4 * rows, cols)


def gather_weight(weight, fast):
    if fast and lax.axis_size("fsdp") == 4 and lax.axis_size("ctx") % 2 == 0:
        return gather_weight_fast(weight)
    return lax.all_gather(weight, "fsdp", axis=0, tiled=True)


def gather_ctx(piece):
    count = lax.axis_size("ctx")
    outer = jnp.stack([piece] + [swap(piece, "ctx", k) for k in range(2, count, 2)])
    both = jnp.stack([outer, swap(outer, "ctx", 1)], axis=1)
    return both.reshape((count,) + piece.shape)


def reduce_ctx(stacked):
    count = lax.axis_size("ctx")
    parts = stacked.reshape((count // 2, 2) + stacked.shape[1:])
    parts = (parts[:, 0].astype(f32) + swap(parts[:, 1], "ctx", 1).astype(f32)).astype(bf16)
    total = parts[0].astype(f32)
    for k in range(2, count, 2):
        total = total + swap(parts[k // 2], "ctx", k).astype(f32)
    return total


def pick(array, index, dim):
    return lax.dynamic_index_in_dim(array, index, dim, keepdims=False)


def exchange_sum(array, dim, axis, stride, size):
    own = (lax.axis_index(axis) // stride) % size
    total = pick(array, own, dim).astype(f32)
    for k in range(1, size):
        total = total + swap(pick(array, own ^ k, dim), axis, k * stride).astype(f32)
    return total


def rows_by_owner(grad):
    ctx_count, fs_count = lax.axis_size("ctx"), lax.axis_size("fsdp")
    rows, cols = grad.shape
    return grad.astype(bf16).reshape(
        ctx_count // 2, 2, fs_count // 2, 2, rows // (ctx_count * fs_count), cols
    )


def sum_core(views):
    core = lax.axis_index("fsdp") % 2
    keep, send = (
        jnp.concatenate([pick(view, side, 3) for view in views], axis=3) for side in (core, 1 - core)
    )
    return (keep.astype(f32) + swap(send, "fsdp", 1).astype(f32)).astype(bf16)


def sum_first(parts):
    half, wide = parts.shape[0] // 2, parts.shape[2]
    low = exchange_sum(parts[:half], 2, "fsdp", 2, wide).astype(bf16)
    high = exchange_sum(parts[half:], 1, "ctx", 1, 2).astype(bf16)
    return low, high


def sum_second(low, high):
    low = exchange_sum(low, 1, "ctx", 1, 2).astype(bf16)
    high = exchange_sum(high, 1, "fsdp", 2, high.shape[1]).astype(bf16)
    return jnp.concatenate([low, high], axis=0)


def sum_last(parts):
    return exchange_sum(parts, 0, "ctx", 2, parts.shape[0])


def tie(*arrays):
    return lax.optimization_barrier(arrays)


def all_sum(array):
    for axis in ("fsdp", "ctx"):
        distance = 1
        while distance < lax.axis_size(axis):
            array = array + swap(array, axis, distance)
            distance *= 2
    return array


def pair_table(ctx_count, mine):
    step = jnp.arange(2 * ctx_count + 1, dtype=jnp.int32)
    late = step > mine
    key_block = jnp.where(late, step - (mine + 1), step)
    own = jnp.where(late, 2 * ctx_count - 1 - mine, mine)
    key_late = key_block >= ctx_count
    device = jnp.where(key_late, 2 * ctx_count - 1 - key_block, key_block)
    place = (device ^ mine) * 2 + key_late.astype(jnp.int32)
    return jnp.stack(
        [
            late.astype(jnp.int32),
            place,
            (key_block == 0).astype(jnp.int32),
            (key_block == own).astype(jnp.int32),
        ]
    )


def turn(x, cosine, sine):
    lane = lax.broadcasted_iota(jnp.int32, x.shape, 1) % HEAD_WIDTH
    swapped = jnp.where(
        lane < HEAD_WIDTH // 2,
        pltpu.roll(x, 2 * HEAD_WIDTH - HEAD_WIDTH // 2, 1),
        pltpu.roll(x, HEAD_WIDTH // 2, 1),
    )
    return x * cosine + swapped * sine


def side_by_side(rows):
    turned = [rows[:, 2 * HEAD_WIDTH * p : 2 * HEAD_WIDTH * (p + 1)].T for p in range(QUERY_HEADS // 2)]
    heads = [turned[h // 2][h % 2 * HEAD_WIDTH : (h % 2 + 1) * HEAD_WIDTH] for h in range(QUERY_HEADS)]
    return [
        jnp.concatenate(heads[g * GROUP : (g + 1) * GROUP], axis=1).astype(bf16)
        for g in range(KEY_VALUE_HEADS)
    ]


def head_pair(groups, pair):
    half = groups[0].shape[1] // GROUP
    heads = []
    for h in (2 * pair, 2 * pair + 1):
        k = h % GROUP
        heads.append(groups[h // GROUP][:, k * half : (k + 1) * half])
    return jnp.concatenate(heads, axis=0).T


def prepare_kernel(qkv_ref, cos_ref, sin_ref, q_ref, pair_ref):
    width = 2 * HEAD_WIDTH
    cosine, sine = cos_ref[...], sin_ref[...]
    queries = []
    for p in range(QUERY_HEADS // 2):
        turned = turn(qkv_ref[:, width * p : width * (p + 1)], cosine, sine)
        queries.append(turned.astype(bf16).astype(f32) * score_scale)
    for g, part in enumerate(side_by_side(jnp.concatenate(queries, axis=1))):
        q_ref[0, g] = part
    start = QUERY_HEADS * HEAD_WIDTH
    pair_ref[:, :width] = turn(qkv_ref[:, start : start + width], cosine, sine).astype(bf16)
    pair_ref[:, width:] = qkv_ref[:, start + width :].astype(bf16)


def prepare(qkv_rows, cosine, sine):
    half = qkv_rows.shape[0] // 2
    kv = KEY_VALUE_HEADS * HEAD_WIDTH
    turn_spec = pl.BlockSpec((half, 2 * HEAD_WIDTH), lambda b: (b, 0))
    return pl.pallas_call(
        prepare_kernel,
        grid=(2,),
        in_specs=[pl.BlockSpec((half, qkv_rows.shape[1]), lambda b: (b, 0)), turn_spec, turn_spec],
        out_specs=[
            pl.BlockSpec((1, KEY_VALUE_HEADS, HEAD_WIDTH, GROUP * half), lambda b: (b, 0, 0, 0)),
            pl.BlockSpec((half, 2 * kv), lambda b: (b, 0)),
        ],
        out_shape=[
            jax.ShapeDtypeStruct((2, KEY_VALUE_HEADS, HEAD_WIDTH, GROUP * half), bf16),
            jax.ShapeDtypeStruct((2 * half, 2 * kv), bf16),
        ],
        compiler_params=pltpu.CompilerParams(vmem_limit_bytes=24 * 2**20),
        cost_estimate=pl.CostEstimate(flops=2**22, bytes_accessed=2**22, transcendentals=0),
        name="prepare",
    )(qkv_rows, cosine, sine)


def attn_forward_kernel(tab, q_ref, kv_ref, row_ref, o_ref, ot_ref, lse_ref, m_s, l_s, acc_s):
    step = pl.program_id(0)
    diag = tab[3, step]

    @pl.when(tab[2, step] == 1)
    def _():
        m_s[...] = jnp.full(m_s.shape, masked_fill_value, f32)
        l_s[...] = jnp.zeros(l_s.shape, f32)
        acc_s[...] = jnp.zeros(acc_s.shape, f32)

    keys, queries = kv_ref.shape[1], q_ref.shape[3]
    limit = row_ref[...] + (1 - diag) * keys
    allowed = lax.broadcasted_iota(jnp.int32, (keys, queries), 0) <= limit
    kv = kv_ref[0]
    values_t = kv[:, KEY_VALUE_HEADS * HEAD_WIDTH :].astype(f32).T.astype(bf16)
    for g in range(KEY_VALUE_HEADS):
        head = slice(g * HEAD_WIDTH, (g + 1) * HEAD_WIDTH)
        scores = matmul(kv[:, head], q_ref[0, g])
        scores = jnp.where(allowed, scores, masked_fill_value)
        old = m_s[g]
        new = jnp.maximum(old, jnp.max(scores, axis=0, keepdims=True))
        probs = jnp.exp(scores - new)
        fade = jnp.exp(old - new)
        m_s[g] = new
        l_s[g] = l_s[g] * fade + jnp.sum(probs, axis=0, keepdims=True)
        acc_s[g] = acc_s[g] * fade + matmul(values_t[head], probs.astype(bf16))

    @pl.when(diag == 1)
    def _():
        outs = []
        for g in range(KEY_VALUE_HEADS):
            outs.append(acc_s[g] / l_s[g])
            ot_ref[0, g] = outs[g]
            lse_ref[0, g] = m_s[g] + jnp.log(l_s[g])
        for p in range(QUERY_HEADS // 2):
            o_ref[:, 2 * HEAD_WIDTH * p : 2 * HEAD_WIDTH * (p + 1)] = head_pair(outs, p).astype(bf16)


def attn_specs(half):
    width = GROUP * half
    query = pl.BlockSpec((1, KEY_VALUE_HEADS, HEAD_WIDTH, width), lambda j, t: (t[0, j], 0, 0, 0))
    row = pl.BlockSpec((1, KEY_VALUE_HEADS, 1, width), lambda j, t: (t[0, j], 0, 0, 0))
    pair = pl.BlockSpec((1, half, 2 * KEY_VALUE_HEADS * HEAD_WIDTH), lambda j, t: (t[1, j], 0, 0))
    natural = pl.BlockSpec((half, QUERY_HEADS * HEAD_WIDTH), lambda j, t: (t[0, j], 0))
    return query, row, pair, natural


def attn_forward(table, q_t, all_pairs, query_row):
    steps = table.shape[1]
    half, width = all_pairs.shape[1], q_t.shape[3]
    query, row, pair, natural = attn_specs(half)
    return pl.pallas_call(
        attn_forward_kernel,
        grid_spec=pltpu.PrefetchScalarGridSpec(
            num_scalar_prefetch=1,
            grid=(steps,),
            in_specs=[query, pair, pl.BlockSpec((1, width), lambda j, t: (0, 0))],
            out_specs=[natural, query, row],
            scratch_shapes=[
                pltpu.VMEM((KEY_VALUE_HEADS, 1, width), f32),
                pltpu.VMEM((KEY_VALUE_HEADS, 1, width), f32),
                pltpu.VMEM((KEY_VALUE_HEADS, HEAD_WIDTH, width), f32),
            ],
        ),
        out_shape=[
            jax.ShapeDtypeStruct((2 * half, QUERY_HEADS * HEAD_WIDTH), bf16),
            jax.ShapeDtypeStruct(q_t.shape, f32),
            jax.ShapeDtypeStruct((2, KEY_VALUE_HEADS, 1, width), f32),
        ],
        compiler_params=pltpu.CompilerParams(vmem_limit_bytes=40 * 2**20),
        cost_estimate=pl.CostEstimate(
            flops=steps * 4 * half * width * 2 * HEAD_WIDTH,
            bytes_accessed=2**23,
            transcendentals=steps * 2 * half * width,
        ),
        name="attn_forward",
    )(table, q_t, all_pairs, query_row)


def attn_backward_kernel(
    tab, q_ref, kv_ref, do_ref, ot_ref, lse_ref, cos_ref, sin_ref, row_ref,
    dq_ref, dkv_ref, do_s, dot_s, dq_s, dkv_s,
):
    step = pl.program_id(0)
    diag = tab[3, step]
    place = tab[1, step]

    @pl.when(step == 0)
    def _():
        dkv_s[...] = jnp.zeros(dkv_s.shape, f32)

    @pl.when(tab[2, step] == 1)
    def _():
        dq_s[...] = jnp.zeros(dq_s.shape, f32)
        for g, part in enumerate(side_by_side(do_ref[...].astype(f32))):
            do_s[g] = part
            dot_s[g] = jnp.sum(part.astype(f32) * ot_ref[0, g], axis=0, keepdims=True)

    keys, queries = kv_ref.shape[1], q_ref.shape[3]
    limit = row_ref[...] + (1 - diag) * keys
    allowed = lax.broadcasted_iota(jnp.int32, (keys, queries), 0) <= limit
    kv = kv_ref[0]
    kv_width = KEY_VALUE_HEADS * HEAD_WIDTH
    keys_t = kv[:, :kv_width].astype(f32).T.astype(bf16)
    grads = [None] * 4
    for g in range(KEY_VALUE_HEADS):
        head = slice(g * HEAD_WIDTH, (g + 1) * HEAD_WIDTH)
        v_head = slice(kv_width + g * HEAD_WIDTH, kv_width + (g + 1) * HEAD_WIDTH)
        q, d_out = q_ref[0, g], do_s[g]
        scores = matmul(kv[:, head], q)
        probs = jnp.exp(jnp.where(allowed, scores - lse_ref[0, g], masked_fill_value))
        d_probs = matmul(kv[:, v_head], d_out)
        d_scores = (probs * (d_probs - dot_s[g])).astype(bf16)
        dq_s[g] += matmul(keys_t[head], d_scores)
        grads[g] = backward_product(d_scores, q)
        grads[2 + g] = backward_product(probs.astype(bf16), d_out)
    dkv_s[place] += jnp.concatenate(grads, axis=1)

    @pl.when(diag == 1)
    def _():
        parts = [dq_s[g] for g in range(KEY_VALUE_HEADS)]
        for p in range(QUERY_HEADS // 2):
            turned = turn(head_pair(parts, p), cos_ref[...], -sin_ref[...]) * score_scale
            dq_ref[:, 2 * HEAD_WIDTH * p : 2 * HEAD_WIDTH * (p + 1)] = turned.astype(bf16)

    @pl.when(step == pl.num_programs(0) - 1)
    def _():
        dkv_ref[...] = dkv_s[...].astype(bf16)


def attn_backward(table, q_t, all_pairs, d_out, out_t, lse, cosine, sine, query_row):
    steps = table.shape[1]
    blocks, half, kv = all_pairs.shape
    width = q_t.shape[3]
    query, row, pair, natural = attn_specs(half)
    turn_spec = pl.BlockSpec((half, 2 * HEAD_WIDTH), lambda j, t: (t[0, j], 0))
    return pl.pallas_call(
        attn_backward_kernel,
        grid_spec=pltpu.PrefetchScalarGridSpec(
            num_scalar_prefetch=1,
            grid=(steps,),
            in_specs=[
                query, pair, natural, query, row, turn_spec, turn_spec,
                pl.BlockSpec((1, width), lambda j, t: (0, 0)),
            ],
            out_specs=[natural, pl.BlockSpec((blocks, half, kv), lambda j, t: (0, 0, 0))],
            scratch_shapes=[
                pltpu.VMEM((KEY_VALUE_HEADS, HEAD_WIDTH, width), bf16),
                pltpu.VMEM((KEY_VALUE_HEADS, 1, width), f32),
                pltpu.VMEM((KEY_VALUE_HEADS, HEAD_WIDTH, width), f32),
                pltpu.VMEM((blocks, half, kv), f32),
            ],
        ),
        out_shape=[
            jax.ShapeDtypeStruct((2 * half, QUERY_HEADS * HEAD_WIDTH), bf16),
            jax.ShapeDtypeStruct((blocks, half, kv), bf16),
        ],
        compiler_params=pltpu.CompilerParams(vmem_limit_bytes=56 * 2**20),
        cost_estimate=pl.CostEstimate(
            flops=steps * 10 * half * width * 2 * HEAD_WIDTH,
            bytes_accessed=2**24,
            transcendentals=steps * 2 * half * width,
        ),
        name="attn_backward",
    )(table, q_t, all_pairs, d_out, out_t, lse, cosine, sine, query_row)


def two_halves(values):
    high = values.astype(bf16)
    return high, (values - high.astype(f32)).astype(bf16)


def wide_product(left, right):
    return backward_product(
        jnp.concatenate([left[0], left[0], left[1]], axis=1),
        jnp.concatenate([right[0], right[1], right[0]], axis=1),
    )


def by_pair(columns, pair, left):
    return jnp.where(left, columns[:, 2 * pair : 2 * pair + 1], columns[:, 2 * pair + 1 : 2 * pair + 2])


def pair_lanes(pair):
    return slice(2 * MP * pair, 2 * MP * (pair + 1))


def scan_forward_kernel(m_ref, dt_ref, cum_ref, cumt_ref, skip_ref, part_ref, upd_ref, tail_s):
    half = m_ref.shape[0]
    left = lax.broadcasted_iota(jnp.int32, (half, 2 * MP), 1) < MP
    causal = lax.broadcasted_iota(jnp.int32, (half, half), 0) >= lax.broadcasted_iota(
        jnp.int32, (half, half), 1
    )
    b_rows = m_ref[:, DI : DI + NS].astype(bf16)
    scores = wide_product(two_halves(m_ref[:, DI + NS :]), two_halves(m_ref[:, DI : DI + NS]))
    dt, cum, cum_t = dt_ref[0], cum_ref[0], cumt_ref[0]
    tail = jnp.exp(cum[half - 1 : half, :] - cum)
    for pair in range(PAIRS):
        lanes = pair_lanes(pair)
        x = m_ref[:, lanes]
        scaled = x * by_pair(dt, pair, left)
        scaled_both = jnp.concatenate(two_halves(scaled), axis=1)
        outs = []
        for h in (2 * pair, 2 * pair + 1):
            gap = cum[:, h : h + 1] - cum_t[h : h + 1, :]
            weights = jnp.exp(jnp.where(causal, gap, masked_fill_value)) * scores
            high, rest = two_halves(weights)
            wide = matmul(high, scaled_both)
            outs.append(wide[:, : 2 * MP] + wide[:, 2 * MP :] + matmul(rest, scaled_both[:, : 2 * MP]))
        part_ref[:, lanes] = jnp.where(left, outs[0], outs[1]) + skip_ref[:, lanes] * x
        tail_s[:, lanes] = (scaled * by_pair(tail, pair, left)).astype(bf16)
    upd_ref[0] = row_contract(b_rows, tail_s[...]).astype(bf16)


def token_specs(half):
    per_block = pl.BlockSpec((1, half, MH), lambda b: (b, 0, 0))
    per_block_t = pl.BlockSpec((1, MH, half), lambda b: (b, 0, 0))
    return per_block, per_block_t


def scan_forward(mixed, dt, cum, cum_t, skip_row):
    half = mixed.shape[0] // 2
    per_block, per_block_t = token_specs(half)
    return pl.pallas_call(
        scan_forward_kernel,
        grid=(2,),
        in_specs=[
            pl.BlockSpec((half, CONV), lambda b: (b, 0)),
            per_block,
            per_block,
            per_block_t,
            pl.BlockSpec((1, DI), lambda b: (0, 0)),
        ],
        out_specs=[
            pl.BlockSpec((half, DI), lambda b: (b, 0)),
            pl.BlockSpec((1, NS, DI), lambda b: (b, 0, 0)),
        ],
        out_shape=[
            jax.ShapeDtypeStruct((2 * half, DI), f32),
            jax.ShapeDtypeStruct((2, NS, DI), bf16),
        ],
        scratch_shapes=[pltpu.VMEM((half, DI), bf16)],
        compiler_params=pltpu.CompilerParams(vmem_limit_bytes=48 * 2**20),
        cost_estimate=pl.CostEstimate(
            flops=2 * half * half * 128 * 2 * MH,
            bytes_accessed=16 * half * DI,
            transcendentals=2 * MH * half * half,
        ),
        name="scan_forward",
    )(mixed, dt, cum, cum_t, skip_row)


def state_kernel(order, upd_ref, fade_ref, out_ref):
    def one(i, state):
        place = order[0, i]
        out_ref[place] = state.astype(bf16)
        return state * fade_ref[pl.ds(order[1, i], 1), :] + upd_ref[place].astype(f32)

    lax.fori_loop(0, upd_ref.shape[0], one, jnp.zeros(upd_ref.shape[1:], f32))


def run_states(order, updates, fades):
    return pl.pallas_call(
        state_kernel,
        grid_spec=pltpu.PrefetchScalarGridSpec(
            num_scalar_prefetch=1,
            grid=(1,),
            in_specs=[
                pl.BlockSpec(updates.shape, lambda j, t: (0, 0, 0)),
                pl.BlockSpec(fades.shape, lambda j, t: (0, 0)),
            ],
            out_specs=pl.BlockSpec(updates.shape, lambda j, t: (0, 0, 0)),
        ),
        out_shape=jax.ShapeDtypeStruct(updates.shape, bf16),
        compiler_params=pltpu.CompilerParams(vmem_limit_bytes=24 * 2**20),
        name="run_states",
    )(order, updates, fades)


def exchange_states(order, updates, fades):
    count = lax.axis_size("ctx")
    share = NS // count
    parts = updates.reshape(2, count, share, DI).swapaxes(0, 1)
    pieces = lax.all_to_all(parts, "ctx", 0, 0).reshape(2 * count, share, DI)
    states = run_states(order, pieces, fades).reshape(count, 2, share, DI)
    back = lax.all_to_all(states, "ctx", 0, 0)
    return back.swapaxes(0, 1).reshape(2, NS, DI)


def gated_forward_kernel(part_ref, c_ref, cum_ref, state_ref, z_ref, gain_ref, y_ref, low_ref, g_s):
    half = part_ref.shape[0]
    left = lax.broadcasted_iota(jnp.int32, (half, 2 * MP), 1) < MP
    c_rows, c_rest = two_halves(c_ref[...])
    carried = matmul(c_rows, state_ref[0]) + matmul(c_rest, state_ref[0])
    decay = jnp.exp(cum_ref[0])
    square = jnp.zeros((half, 2 * MP), f32)
    for pair in range(PAIRS):
        lanes = pair_lanes(pair)
        y = part_ref[:, lanes] + carried[:, lanes] * by_pair(decay, pair, left)
        y_ref[:, lanes] = y
        gated = y * jax.nn.silu(z_ref[:, lanes])
        g_s[:, lanes] = gated
        square += gated * gated
    scale = lax.rsqrt(jnp.sum(square, axis=1, keepdims=True) * (1.0 / DI) + epsilon)
    low_ref[...] = (g_s[...] * scale * gain_ref[...]).astype(bf16)


def gated_forward(part, mixed, cum, states, projected, gain):
    half = part.shape[0] // 2
    per_block, _ = token_specs(half)
    wide = pl.BlockSpec((half, DI), lambda b: (b, 0))
    return pl.pallas_call(
        gated_forward_kernel,
        grid=(2,),
        in_specs=[
            wide,
            pl.BlockSpec((half, NS), lambda b: (b, (DI + NS) // NS)),
            per_block,
            pl.BlockSpec((1, NS, DI), lambda b: (b, 0, 0)),
            wide,
            pl.BlockSpec((1, DI), lambda b: (0, 0)),
        ],
        out_specs=[wide, wide],
        out_shape=[
            jax.ShapeDtypeStruct((2 * half, DI), f32),
            jax.ShapeDtypeStruct((2 * half, DI), bf16),
        ],
        scratch_shapes=[pltpu.VMEM((half, DI), f32)],
        compiler_params=pltpu.CompilerParams(vmem_limit_bytes=48 * 2**20),
        cost_estimate=pl.CostEstimate(
            flops=4 * half * NS * DI + 40 * half * DI,
            bytes_accessed=30 * half * DI,
            transcendentals=4 * half * DI,
        ),
        name="gated_forward",
    )(part, mixed, cum, states, projected, gain)


def gated_backward_kernel(
    gg_ref, y_ref, z_ref, gain_ref, c_ref, cum_ref, yg_ref, zg_ref, gain_g_ref, direct_ref, g_s, w_s
):
    half = gg_ref.shape[0]
    left = lax.broadcasted_iota(jnp.int32, (half, 2 * MP), 1) < MP
    decay = jnp.exp(cum_ref[0])
    square = jnp.zeros((half, 2 * MP), f32)
    cross = jnp.zeros((half, 2 * MP), f32)
    for pair in range(PAIRS):
        lanes = pair_lanes(pair)
        gated = y_ref[:, lanes] * jax.nn.silu(z_ref[:, lanes])
        g_s[:, lanes] = gated
        square += gated * gated
        cross += gg_ref[:, lanes] * gain_ref[:, lanes] * gated
    scale = lax.rsqrt(jnp.sum(square, axis=1, keepdims=True) * (1.0 / DI) + epsilon)
    mean = jnp.sum(cross, axis=1, keepdims=True) * (1.0 / DI)
    pull = scale * scale * scale * mean
    for pair in range(PAIRS):
        lanes = pair_lanes(pair)
        gated, grad, z = g_s[:, lanes], gg_ref[:, lanes], z_ref[:, lanes]
        gain_g_ref[0, :, lanes] = jnp.sum(grad * gated * scale, axis=0, keepdims=True)
        inner = scale * grad * gain_ref[:, lanes] - gated * pull
        sig = jax.nn.sigmoid(z)
        zg_ref[:, lanes] = (inner * y_ref[:, lanes] * sig * (1.0 + z * (1.0 - sig))).astype(bf16)
        grad_y = inner * z * sig
        yg_ref[:, lanes] = grad_y
        w_s[:, lanes] = (grad_y * by_pair(decay, pair, left)).astype(bf16)
    direct_ref[0] = row_contract(c_ref[...].astype(bf16), w_s[...]).astype(bf16)


def gated_backward(gated_grad, scan_out, projected, gain, mixed, cum):
    half = gated_grad.shape[0] // 2
    per_block, _ = token_specs(half)
    wide = pl.BlockSpec((half, DI), lambda b: (b, 0))
    return pl.pallas_call(
        gated_backward_kernel,
        grid=(2,),
        in_specs=[
            wide,
            wide,
            wide,
            pl.BlockSpec((1, DI), lambda b: (0, 0)),
            pl.BlockSpec((half, NS), lambda b: (b, (DI + NS) // NS)),
            per_block,
        ],
        out_specs=[
            wide,
            wide,
            pl.BlockSpec((1, 1, DI), lambda b: (b, 0, 0)),
            pl.BlockSpec((1, NS, DI), lambda b: (b, 0, 0)),
        ],
        out_shape=[
            jax.ShapeDtypeStruct((2 * half, DI), f32),
            jax.ShapeDtypeStruct((2 * half, DI), bf16),
            jax.ShapeDtypeStruct((2, 1, DI), f32),
            jax.ShapeDtypeStruct((2, NS, DI), bf16),
        ],
        scratch_shapes=[pltpu.VMEM((half, DI), f32), pltpu.VMEM((half, DI), bf16)],
        compiler_params=pltpu.CompilerParams(vmem_limit_bytes=48 * 2**20),
        cost_estimate=pl.CostEstimate(
            flops=4 * half * NS * DI + 60 * half * DI,
            bytes_accessed=40 * half * DI,
            transcendentals=8 * half * DI,
        ),
        name="gated_backward",
    )(gated_grad, scan_out, projected, gain, mixed, cum)


def split_sum(values, spread):
    high, rest = two_halves(values)
    return matmul(high, spread) + matmul(rest, spread)


def scan_backward_kernel(
    m_ref, gy_ref, y_ref, dt_ref, cum_ref, cumt_ref, skip_ref, state_ref, carry_ref,
    dm_ref, dcum_ref, ddt_ref, dskip_ref, last_ref, tail_s, grow_s, blt_s,
):
    half = m_ref.shape[0]
    left = lax.broadcasted_iota(jnp.int32, (half, 2 * MP), 1) < MP
    upper = lax.broadcasted_iota(jnp.int32, (half, half), 0) <= lax.broadcasted_iota(
        jnp.int32, (half, half), 1
    )
    b_rows, b_rest = two_halves(m_ref[:, DI : DI + NS])
    c_rows, c_rest = two_halves(m_ref[:, DI + NS :])
    scores_t = wide_product((b_rows, b_rest), (c_rows, c_rest))
    dt, cum, cum_t = dt_ref[0], cum_ref[0], cumt_ref[0]
    grow = jnp.exp(cum)
    tail = jnp.exp(cum[half - 1 : half, :] - cum)
    fade = grow[half - 1 : half, :]
    carry_low = carry_ref[0]
    blt_s[...] = matmul(b_rows, carry_low)
    d_scores_t = jnp.zeros((half, half), f32)
    d_cum = jnp.zeros((half, 2 * MP), f32)
    d_dt = jnp.zeros((half, 2 * MP), f32)
    lane_head = lax.broadcasted_iota(jnp.int32, (2 * MP, 2 * MP), 0) // MP
    column = lax.broadcasted_iota(jnp.int32, (2 * MP, 2 * MP), 1)
    for pair in range(PAIRS):
        lanes = pair_lanes(pair)
        x, gy = m_ref[:, lanes], gy_ref[:, lanes]
        dt_pair = by_pair(dt, pair, left)
        scaled = x * dt_pair
        gy_low, gy_rest = two_halves(gy)
        scaled_two = two_halves(scaled)
        nothing = jnp.zeros_like(gy_low)
        outs = []
        for k, h in enumerate((2 * pair, 2 * pair + 1)):
            gap = cum_t[h : h + 1, :] - cum[:, h : h + 1]
            decays = jnp.exp(jnp.where(upper, gap, masked_fill_value))
            outs.append(matmul((decays * scores_t).astype(bf16), gy_low))
            mine = [jnp.where(left, v, nothing) if k == 0 else jnp.where(left, nothing, v) for v in scaled_two]
            d_scores_t += wide_product(mine, (gy_low, gy_rest)) * decays
        tail_pair = by_pair(tail, pair, left)
        from_tail = tail_pair * blt_s[:, lanes]
        d_scaled = jnp.where(left, outs[0], outs[1]) + from_tail
        dm_ref[:, lanes] = dt_pair * d_scaled + skip_ref[:, lanes] * gy
        spread = (lane_head + 2 * pair == column).astype(bf16)
        skipped = x * gy
        d_cum += split_sum(gy * y_ref[:, lanes] - skip_ref[:, lanes] * skipped - scaled * d_scaled, spread)
        d_dt += split_sum(x * d_scaled, spread)
        dskip_ref[0, :, lanes] = jnp.sum(skipped, axis=0, keepdims=True)
        held = jnp.sum(state_ref[0][:, lanes].astype(f32) * carry_low[:, lanes].astype(f32), axis=0, keepdims=True)
        last_ref[0, :, lanes] = jnp.sum(scaled * from_tail, axis=0, keepdims=True) + held * by_pair(
            fade, pair, left[0:1]
        )
        tail_s[0, :, lanes], tail_s[1, :, lanes] = two_halves(scaled * tail_pair)
        grow_s[0, :, lanes], grow_s[1, :, lanes] = two_halves(gy * by_pair(grow, pair, left))
    d_low, d_rest = two_halves(d_scores_t)
    dm_ref[:, DI : DI + NS] = (
        matmul(d_low, c_rows)
        + matmul(d_low, c_rest)
        + matmul(d_rest, c_rows)
        + backward_product(tail_s[0], carry_low)
        + backward_product(tail_s[1], carry_low)
    )
    dm_ref[:, DI + NS :] = (
        row_contract(d_low, b_rows)
        + row_contract(d_low, b_rest)
        + row_contract(d_rest, b_rows)
        + backward_product(grow_s[0], state_ref[0])
        + backward_product(grow_s[1], state_ref[0])
    )
    dcum_ref[0] = d_cum[:, :MH]
    ddt_ref[0] = d_dt[:, :MH]


def scan_backward(mixed, scan_grad, scan_out, dt, cum, cum_t, skip_row, states, carries):
    half = mixed.shape[0] // 2
    per_block, per_block_t = token_specs(half)
    wide = pl.BlockSpec((half, DI), lambda b: (b, 0))
    full = pl.BlockSpec((half, CONV), lambda b: (b, 0))
    state = pl.BlockSpec((1, NS, DI), lambda b: (b, 0, 0))
    row = pl.BlockSpec((1, 1, DI), lambda b: (b, 0, 0))
    return pl.pallas_call(
        scan_backward_kernel,
        grid=(2,),
        in_specs=[
            full, wide, wide, per_block, per_block, per_block_t,
            pl.BlockSpec((1, DI), lambda b: (0, 0)), state, state,
        ],
        out_specs=[full, per_block, per_block, row, row],
        out_shape=[
            jax.ShapeDtypeStruct((2 * half, CONV), f32),
            jax.ShapeDtypeStruct((2, half, MH), f32),
            jax.ShapeDtypeStruct((2, half, MH), f32),
            jax.ShapeDtypeStruct((2, 1, DI), f32),
            jax.ShapeDtypeStruct((2, 1, DI), f32),
        ],
        scratch_shapes=[
            pltpu.VMEM((2, half, DI), bf16),
            pltpu.VMEM((2, half, DI), bf16),
            pltpu.VMEM((half, DI), f32),
        ],
        compiler_params=pltpu.CompilerParams(vmem_limit_bytes=56 * 2**20),
        cost_estimate=pl.CostEstimate(
            flops=6 * half * half * 128 * 2 * MH,
            bytes_accessed=40 * half * DI,
            transcendentals=2 * MH * half * half,
        ),
        name="scan_backward",
    )(mixed, scan_grad, scan_out, dt, cum, cum_t, skip_row, states, carries)


def conv_block(previous, raw_rows, conv_weight, conv_bias):
    extended = jnp.concatenate([previous, raw_rows], axis=0)
    row_count = raw_rows.shape[0]
    running = conv_bias[None, :] + conv_weight[0][None, :] * extended[0:row_count]
    for offset in range(1, conv_weight.shape[0]):
        running = running + conv_weight[offset][None, :] * extended[offset : offset + row_count]
    return jax.nn.silu(running)


def local(
    tokens,
    cotangent,
    block_table,
    mixer_gain,
    in_proj,
    conv_weight,
    conv_bias,
    step_bias,
    decay_log,
    skip_gain,
    gated_gain,
    out_proj,
    attention_in,
    attention_out,
    feed_gain,
    gate_up,
    down_proj,
):
    ctx_count = lax.axis_size("ctx")
    my_index = lax.axis_index("ctx")
    is_last = my_index == ctx_count - 1
    device_rows = tokens.shape[1]
    half_rows = device_rows // 2
    lag_rows = KCONV - 1
    kv_width = KEY_VALUE_HEADS * HEAD_WIDTH
    slot_first = lax.dynamic_index_in_dim(block_table, 2 * my_index, keepdims=False)
    swapped = slot_first != my_index

    def arrange(value_rows):
        first_half = value_rows[:half_rows]
        second_half = value_rows[half_rows:]
        return jnp.concatenate(
            [
                jnp.where(swapped, second_half, first_half),
                jnp.where(swapped, first_half, second_half),
            ],
            axis=0,
        )

    block_ids = jnp.concatenate(
        [
            jnp.full((half_rows,), my_index, jnp.int32),
            jnp.full((half_rows,), 2 * ctx_count - 1 - my_index, jnp.int32),
        ]
    )
    token_positions = block_ids * half_rows + jnp.tile(jnp.arange(half_rows, dtype=jnp.int32), 2)
    freqs = jnp.exp(
        -(jnp.arange(HEAD_WIDTH // 2, dtype=f32) * (2.0 / HEAD_WIDTH)) * jnp.log(rope_base)
    )
    angles = token_positions.astype(f32)[:, None] * freqs[None, :]
    sign = jnp.where(jnp.arange(2 * HEAD_WIDTH) % HEAD_WIDTH < HEAD_WIDTH // 2, -1.0, 1.0)
    cosine, sine = tie(jnp.tile(jnp.cos(angles), (1, 4)), jnp.tile(jnp.sin(angles), (1, 4)) * sign)
    hidden = arrange(tokens[0]).astype(f32)
    out_grad = arrange(cotangent[0]).astype(f32)

    full_qkv = gather_weight(attention_in, True)
    full_in = gather_weight(in_proj, True)
    full_in, out_proj, attention_out, gate_up, down_proj = lax.optimization_barrier(
        (full_in, out_proj, attention_out, gate_up, down_proj)
    )
    full_out = gather_weight(out_proj, False)
    full_output_weight = gather_weight(attention_out, False)
    full_gu = gather_weight(gate_up, False)
    full_down = gather_weight(down_proj, False)

    scale_one = norm_scale(hidden)
    normed_one = (hidden * scale_one * mixer_gain).astype(bf16)

    qkv_rows = matmul(normed_one, full_qkv)
    q_t, pairs = prepare(qkv_rows, cosine, sine)
    all_pairs = gather_ctx(pairs).reshape(2 * ctx_count, half_rows, 2 * kv_width)
    table = pair_table(ctx_count, my_index)
    query_row = jnp.tile(jnp.arange(half_rows, dtype=jnp.int32), GROUP)[None]
    attn_low, attn_t, log_total = attn_forward(table, q_t, all_pairs, query_row)

    projected = matmul(normed_one, full_in)
    raw_conv = projected[:, DI : DI + CONV]
    step_raw = projected[:, DI + CONV :]
    early_tail = raw_conv[half_rows - lag_rows : half_rows]
    edges = jnp.concatenate([raw_conv[device_rows - lag_rows :], early_tail], axis=0)
    before, after = edge_exchange(edges.astype(bf16), lag_rows)
    prev_early = before.astype(f32)
    prev_late = jnp.where(is_last, early_tail, after.astype(f32))
    raw_early = raw_conv[:half_rows]
    raw_late = raw_conv[half_rows:]
    mixed = jnp.concatenate(
        [
            conv_block(prev_early, raw_early, conv_weight, conv_bias),
            conv_block(prev_late, raw_late, conv_weight, conv_bias),
        ],
        axis=0,
    )
    step_size = jax.nn.softplus(step_raw + step_bias[None, :])
    decay_rate = -jnp.exp(decay_log)
    dt = step_size.reshape(2, half_rows, MH)
    lower = jnp.tril(jnp.ones((half_rows, half_rows), f32))
    cum = jnp.einsum("ts,bsh->bth", lower, dt * decay_rate, precision=highest)
    cum_t = cum.swapaxes(1, 2)
    skip_row = jnp.repeat(skip_gain, MP)[None]
    part, updates = scan_forward(mixed, dt, cum, cum_t, skip_row)

    fades = gather_ctx(jnp.exp(cum[:, half_rows - 1]))
    fades = jnp.repeat(fades.reshape(2 * ctx_count, MH), MP, axis=1)
    block = jnp.arange(2 * ctx_count, dtype=jnp.int32)
    block_late = block >= ctx_count
    block_device = jnp.where(block_late, 2 * ctx_count - 1 - block, block)
    order = jnp.stack([block_device, block_device ^ my_index]) * 2 + block_late.astype(jnp.int32)
    states = exchange_states(order, updates, fades)
    gain_row = gated_gain[None]
    scan_out, gated_low = gated_forward(part, mixed, cum, states, projected, gain_row)

    mamba_out = matmul(gated_low, full_out)
    attn_out = matmul(attn_low, full_output_weight)
    second = hidden + mamba_out + attn_out
    scale_two = norm_scale(second)
    normed_two = (second * scale_two * feed_gain).astype(bf16)
    gate_rows = matmul(normed_two, full_gu)
    gate_part = gate_rows[:, :FF]
    up_part = gate_rows[:, FF:]
    sig_gate = jax.nn.sigmoid(gate_part)
    silu_gate = gate_part * sig_gate
    activated = (silu_gate * up_part).astype(bf16)
    result = second + matmul(activated, full_down)

    down_grad = out_grad.astype(bf16)
    down_part = row_contract(activated, down_grad)
    act_grad = backward_product(down_grad, full_down)
    gate_grad = act_grad * up_part * sig_gate * (1.0 + gate_part * (1.0 - sig_gate))
    up_grad = act_grad * silu_gate
    gu_grad = jnp.concatenate([gate_grad, up_grad], axis=1).astype(bf16)
    gu_part = rows_by_owner(row_contract(normed_two, gu_grad))
    d_model = hidden.shape[1]
    sum_1 = sum_core(
        [gu_part[..., k : k + d_model] for k in range(0, 2 * FF, d_model)] + [rows_by_owner(down_part)]
    )
    normed_two_grad = backward_product(gu_grad, full_gu)
    grad_feed = jnp.sum(normed_two_grad * second * scale_two, axis=0)
    resid_grad = out_grad + norm_backward(normed_two_grad * feed_gain, second, scale_two)
    branch_gradient = resid_grad.astype(bf16)
    gated_grad = backward_product(branch_gradient, full_out)
    scan_grad, z_grad, gain_parts, direct = gated_backward(
        gated_grad, scan_out, projected, gain_row, mixed, cum
    )
    grad_gated = jnp.sum(gain_parts[:, 0], axis=0)
    carries = exchange_states(order[:, ::-1], direct, fades)

    attn_grad = backward_product(branch_gradient, full_output_weight).astype(bf16)
    attn_grad, sum_1 = tie(attn_grad, sum_1)
    sum_1 = sum_first(sum_1)
    z_wide = row_contract(normed_one, z_grad[:, :d_model])
    z_rest = rows_by_owner(row_contract(normed_one, z_grad[:, d_model:]))
    rest_rows = z_rest.shape[4] // 2
    sum_2 = sum_core(
        [
            rows_by_owner(row_contract(gated_low, branch_gradient)),
            rows_by_owner(row_contract(attn_low, branch_gradient)),
            rows_by_owner(z_wide),
            jnp.concatenate([z_rest[..., :rest_rows, :], z_rest[..., rest_rows:, :]], axis=5),
        ]
    )
    dq, d_pairs = attn_backward(
        table, q_t, all_pairs, attn_grad, attn_t, log_total, cosine, sine, query_row
    )
    pair_grad = reduce_ctx(d_pairs.reshape(ctx_count, device_rows, 2 * kv_width))
    key_grad = pair_grad[:, :kv_width]
    quarter = HEAD_WIDTH // 2
    key_swapped = jnp.concatenate(
        [key_grad[:, k * quarter : (k + 1) * quarter] for k in (1, 0, 3, 2)], axis=1
    )
    qkv_grad = jnp.concatenate(
        [dq, (key_grad * cosine - key_swapped * sine).astype(bf16), pair_grad[:, kv_width:].astype(bf16)],
        axis=1,
    )

    scan_grad, sum_1, sum_2 = tie(scan_grad, sum_1, sum_2)
    sum_1 = sum_second(*sum_1)
    sum_2 = sum_first(sum_2)
    mixed_grad, d_cum, d_dt, skip_parts, last_parts = scan_backward(
        mixed, scan_grad, scan_out, dt, cum, cum_t, skip_row, states, carries
    )
    mixed_grad, sum_1, sum_2 = tie(mixed_grad, sum_1, sum_2)
    sum_1 = sum_last(sum_1)
    sum_2 = sum_second(*sum_2)
    grad_skip = jnp.sum(skip_parts.reshape(2, MH, MP), axis=(0, 2))
    last = jnp.sum(last_parts.reshape(2, MH, MP), axis=2)
    log_grad = jnp.einsum("ts,bth->bsh", lower, d_cum, precision=highest) + last[:, None, :]
    grad_decay = jnp.sum(log_grad * dt, axis=(0, 1)) * decay_rate
    step_grad = (d_dt + log_grad * decay_rate).reshape(device_rows, MH)
    step_raw_grad = step_grad * jax.nn.sigmoid(step_raw + step_bias[None, :])
    grad_step = jnp.sum(step_raw_grad, axis=0)
    _, conv_pull_early = jax.vjp(conv_block, prev_early, raw_early, conv_weight, conv_bias)
    prev_early_grad, raw_early_grad, weight_early_grad, bias_early_grad = conv_pull_early(
        mixed_grad[:half_rows]
    )
    _, conv_pull_late = jax.vjp(conv_block, prev_late, raw_late, conv_weight, conv_bias)
    prev_late_grad, raw_late_grad, weight_late_grad, bias_late_grad = conv_pull_late(
        mixed_grad[half_rows:]
    )
    backs = jnp.concatenate([prev_early_grad, prev_late_grad], axis=0)
    before_g, after_g = edge_exchange(backs.astype(bf16), lag_rows)
    early_tail_grad = after_g.astype(f32) + jnp.where(is_last, prev_late_grad, 0.0)
    late_tail_grad = before_g.astype(f32)
    raw_early_grad = raw_early_grad.at[half_rows - lag_rows :].add(early_tail_grad)
    raw_late_grad = raw_late_grad.at[half_rows - lag_rows :].add(late_tail_grad)
    raw_grad = jnp.concatenate([raw_early_grad, raw_late_grad], axis=0)
    raw_grad, sum_1, sum_2 = tie(raw_grad.astype(bf16), sum_1, sum_2)
    sum_2 = sum_last(sum_2)
    tail_width = CONV + MH
    tail_grad = jnp.concatenate(
        [raw_grad, step_raw_grad.astype(bf16), jnp.zeros((device_rows, -tail_width % 128), bf16), qkv_grad],
        axis=1,
    )
    sum_3 = sum_core([rows_by_owner(row_contract(normed_one, tail_grad))])
    sum_3 = sum_last(sum_second(*sum_first(sum_3)))
    normed_one_grad = (
        backward_product(qkv_grad, full_qkv)
        + backward_product(z_grad, full_in[:, :DI])
        + backward_product(tail_grad[:, :tail_width], full_in[:, DI:])
    )
    grad_mixer = jnp.sum(normed_one_grad * hidden * scale_one, axis=0)
    input_grad = resid_grad + norm_backward(normed_one_grad * mixer_gain, hidden, scale_one)

    small = (
        grad_mixer,
        grad_gated,
        grad_feed,
        (weight_early_grad + weight_late_grad).reshape(-1),
        bias_early_grad + bias_late_grad,
        grad_step,
        grad_decay,
        grad_skip,
    )
    each = d_model // (ctx_count * lax.axis_size("fsdp"))
    gu_blocks = 2 * FF // d_model
    grad_gu = jnp.concatenate([sum_1[k * each : (k + 1) * each] for k in range(gu_blocks)], axis=1)
    grad_down = sum_1[gu_blocks * each :]
    cuts = []
    for rows in (each * DI // d_model, each * QUERY_HEADS * HEAD_WIDTH // d_model, each, each // 2):
        cuts.append(sum_2[:rows])
        sum_2 = sum_2[rows:]
    grad_out, grad_o = cuts[:2]
    grad_in = jnp.concatenate(
        [
            cuts[2],
            jnp.concatenate([cuts[3][:, : d_model // 2], cuts[3][:, d_model // 2 :]], axis=0),
            sum_3[:, :tail_width],
        ],
        axis=1,
    )
    grad_qkv = sum_3[:, tail_width + -tail_width % 128 :]
    flat = jnp.concatenate(small)
    size = flat.shape[0]
    flat = jnp.pad(flat, (0, -size % 1024)).reshape(-1, 128)
    flat = all_sum(flat).reshape(-1)
    sums, start = [], 0
    for piece in small:
        sums.append(flat[start : start + piece.shape[0]])
        start += piece.shape[0]
    return (
        arrange(result).astype(bf16)[None],
        arrange(input_grad)[None],
        sums[0],
        grad_in,
        sums[3].reshape(conv_weight.shape),
        sums[4],
        sums[5],
        sums[6],
        sums[7],
        sums[1],
        grad_out,
        grad_qkv,
        grad_o,
        sums[2],
        grad_gu,
        grad_down,
    )


def solution(mesh):
    rows = P("fsdp", None)
    spread = P(("ctx", "fsdp"), None)
    tokens = P("fsdp", "ctx", None)
    return jax.shard_map(
        local,
        mesh=mesh,
        in_specs=(
            tokens, tokens, P(), P(), rows, P(), P(), P(), P(), P(), P(), rows, rows, rows, P(), rows, rows,
        ),
        out_specs=(
            tokens, tokens, P(), spread, P(), P(), P(), P(), P(), P(), spread, spread, spread, P(), spread, spread,
        ),
        check_vma=False,
    )
```

time: 1540 us -> 677 us (0.44)
  waiting for transfers between devices: 908 us -> 172 us
  matrix products: 301 us -> 82.8 us
  starting transfers between devices: 13.2 us -> 118 us
  Pallas kernels: 0 us -> 94.4 us
  blocking collectives: 75 us -> 0 us
  other arithmetic: 121 us -> 70.2 us
  local copies, waits for them, and re-layouts: 87 us -> 115 us
    reduce_scatter x6 -> x0, waiting for transfers between devices: 704 us -> none  [the longest x1 184 us: local(): lax.psum_scatter(grad_mats[4], ('ctx', 'fsdp'), scatter_dimension=0, tile...]
    dot_general x79 -> x8, matrix products: 229 us -> 31.9 us  [the longest x6 31 us: matmul(): return jnp.dot(left, right, preferred_element_type=f32)]
    ppermute x4 -> x55, waiting for transfers between devices: 0.01 us -> 166 us  [the longest x51 164 us: swap(): return lax.ppermute(array, axis, xor_pairs(lax.axis_size(axis), distance))]
    all_gather x11 -> x4, waiting for transfers between devices: 149 us -> 0.01 us  [gather_weight(): return lax.all_gather(weight, 'fsdp', axis=0, tiled=True)]
    pallas_call x0 -> x9, Pallas kernels: none -> 94.4 us  [the longest x1 34.5 us: attn_backward(): pl.pallas_call(attn_backward_kernel, grid_spec=pltpu.PrefetchScalarGridSp...]
    ppermute x4 -> x55, starting transfers between devices: 11.8 us -> 98 us  [the longest x51 87.7 us: swap(): return lax.ppermute(array, axis, xor_pairs(lax.axis_size(axis), distance))]
    unnamed x19 -> x4, waiting for transfers between devices: 54.7 us -> 1.41 us
    psum x1 -> x0, blocking collectives: 38.5 us -> none  [local(): lax.psum((grad_mixer, grad_gated, grad_feed, weight_early_grad + weight_l...]
  transfers between devices with their start and end apart: 22 -> 63, of which waited for: 11 -> 30; matrix products, arithmetic and copies ran while one was open for 30% -> 28% of each run, Pallas kernels for 0% -> 12%
where the time goes in v1:
time: 677 us; the launch traced here: 669 us
  waiting for transfers between devices  172 us (25%)
  starting transfers between devices  118 us (17%)
  local copies, waits for them, and re-layouts  115 us (17%)
  Pallas kernels  94.4 us (14%)
  matrix products  82.8 us (12%)
  other arithmetic  70.2 us (10%)
  between operations  17 us (3%)
    ppermute x51, waiting for transfers between devices, swap(): return lax.ppermute(array, axis, xor_pairs(lax.axis_size(axis), distance))  164 us
    ppermute x51, starting transfers between devices, swap(): return lax.ppermute(array, axis, xor_pairs(lax.axis_size(axis), distance))  87.7 us
    pallas_call x1, Pallas kernels, attn_backward(): pl.pallas_call(attn_backward_kernel, grid_spec=pltpu.PrefetchScalarGridSp...  34.5 us
    dot_general x7, matrix products, backward_product(): lax.dot_general(grad_rows, weight, (((1,), (1,)), ((), ())), preferred_el...  32.8 us
    dot_general x6, matrix products, matmul(): return jnp.dot(left, right, preferred_element_type=f32)  31 us
    unnamed x264, local copies, waits for them, and re-layouts  23.8 us
    pallas_call x1, Pallas kernels, attn_forward(): pl.pallas_call(attn_forward_kernel, grid_spec=pltpu.PrefetchScalarGridSpe...  20.2 us
    dot_general x7, matrix products, row_contract(): lax.dot_general(left, right, (((0,), (0,)), ((), ())), preferred_element_...  18.1 us
  transfers between devices with their start and end apart: 63, of which 30 were waited for; matrix products, arithmetic and copies ran while one was open for 28% of the time, Pallas kernels for 12%

profile of v1, /device:TPU:0, one launch (start us, length us, event | category | flops | bytes accessed | tf_op | source)
XLA Modules:
  0.0 669.0 jit_solution(3063124282517338060)
XLA Ops:
  11.6 19.2 %collective-permute-done.1 = bf16[128,3352]{0,1:T(8,128)(2,1)} collective-permute-done((bf16[128,3352]{0,1:T(8,128)(2,1)S(1)}, bf16[128,3352]{0,1:T(8,128)(2,1)}, u32[]{:S(2)}, u32[]{:S(2)}) %collective-permute-start.1) | collective-permute-done | bytes 858144 | tf_op jit(solution)/shard_map/ppermute | solution.py:37
  41.8 10.8 %collective-permute-done.3 = bf16[128,3352]{0,1:T(8,128)(2,1)} collective-permute-done((bf16[128,3352]{0,1:T(8,128)(2,1)}, bf16[128,3352]{0,1:T(8,128)(2,1)}, u32[]{:S(2)}, u32[]{:S(2)}) %collective-permute-start.3) | collective-permute-done | bytes 858144 | tf_op jit(solution)/shard_map/ppermute | solution.py:37
  77.2 4.9 collective-permute-done.14
  84.2 6.6 fusion.111.z_ref
  101.0 5.7 fusion.36
  108.6 7.6 %scan_forward.1 = (f32[448,1536]{1,0:T(8,128)S(1)}, bf16[2,128,1536]{2,1,0:T(8,128)(2,1)S(1)}) custom-call(f32[448,1792]{1,0:T(8,128)} %pad_maximum_fusion.2.m_ref.c_ref, f32[2,224,24]{2,1,0:T(8,128)S(1)} %bitcast.300, f32[2,224,24]{2,1,0:T(8,128)S(1)} %bitcast.294, f32[2,24,224]{2,1,0:T(8,128)S(1)} %fusion.69.cumt_ref, ...), custom_call_target="tpu_custom_call" | custom-call | flops 616562688 | bytes 5505024 | tf_op jit(solution)/shard_map/scan_forward/pallas_call | solution.py:482
  118.7 5.7 all-to-all-start
  133.1 3.9 collective-permute-start.18
  141.4 6.3 collective-permute-done.9
  147.6 13.7 %collective-permute-start.16 = (bf16[448,256]{1,0:T(8,128)(2,1)S(1)}, bf16[448,256]{1,0:T(8,128)(2,1)S(1)}, u32[]{:S(2)}, u32[]{:S(2)}) collective-permute-start(bf16[448,256]{1,0:T(8,128)(2,1)S(1)} %get-tuple-element.88), channel_id=1, source_target_pairs={{0,8},{4,12},{8,0},{12,4},{16,24},{20,28},{24,16},{28,20},{1,9},{5... | collective-permute-start | bytes 688136 | tf_op jit(solution)/shard_map/ppermute | solution.py:37
  169.7 4.6 all-to-all-start.1
  179.8 23.6 %collective-permute-done.19 = bf16[4,448,256]{2,1,0:T(8,128)(2,1)S(1)} collective-permute-done((bf16[4,448,256]{2,1,0:T(8,128)(2,1)}, bf16[4,448,256]{2,1,0:T(8,128)(2,1)S(1)}, u32[]{:S(2)}, u32[]{:S(2)}) %collective-permute-start.19) | collective-permute-done | bytes 917536 | tf_op jit(solution)/shard_map/ppermute | solution.py:37
  204.6 20.2 %attn_forward.1 = (bf16[448,512]{1,0:T(8,128)(2,1)S(1)}, f32[2,2,64,896]{3,2,1,0:T(8,128)S(1)}, f32[2,2,1,896]{3,2,1,0:T(1,128)S(1)}) custom-call(s32[4,17]{1,0:T(4,128)S(1)} %pad_add_fusion.3.tab, bf16[2,2,64,896]{3,2,1,0:T(8,128)(2,1)S(1)} %copy-done.21, bf16[16,224,256]{2,1,0:T(8,128)(2,1)S(1)} %bitcast.305, s32[1,896]{1,0:T(1,128)S(1)} %broadcast_in_dim_tile.5.row_ref), custom_call_target="tpu_custom_call" | custom-call | flops 1746927616 | bytes 8388608 | tf_op jit(solution)/shard_map/attn_forward/pallas_call | solution.py:310
  227.6 4.3 gated_forward.1
  233.4 5.2 fusion.128
  238.6 3.8 multiply_reduce_fusion.2
  242.4 11.0 %fusion.104 = f32[448,4096]{1,0:T(8,128)} fusion(bf16[1024,4096]{1,0:T(8,128)(2,1)} %all-gather.9.cloned.1.call-done, f32[448,1024]{1,0:T(8,128)} %get-tuple-element.252, f32[1024]{0:T(1024)S(1)} %copy-done.105, f32[448]{0:T(512)S(1)} %add_rsqrt_fusion), kind=kOutput, calls=%fused_computation.343 | convolution fusion | flops 3759472640 | bytes 17569536 | tf_op jit(solution)/shard_map/dot_general | solution.py:52
  253.4 8.7 %multiply_convert_fusion.1 = (bf16[448,2048]{1,0:T(8,128)(2,1)S(1)}, bf16[448,2048]{1,0:T(8,128)(2,1)S(1)}, bf16[448,2048]{1,0:T(8,128)(2,1)}) fusion(f32[448,4096]{1,0:T(8,128)} %fusion.104, bf16[2048,1024]{1,0:T(8,128)(2,1)} %all-gather.11.cloned.1.call-done, bf16[224,1024]{1,0:T(8,128)(2,1)S(1)} %copy-done.71, bf16[224,1024]{1,0:T(8,128)(2,1)S(1)} %copy-done.69), kind=kOutput, calls=%fused_computation.13 | convolution fusion | flops 1894645760 | bytes 17956864 | tf_op jit(solution)/shard_map/dot_general | solution.py:60
  262.1 5.6 convolution_convert_fusion
  284.4 7.3 %multiply_reduce_fusion = (f32[1024]{0:T(1024)}, f32[448]{0:T(512)S(1)}, f32[448,1024]{1,0:T(8,128)S(1)}) fusion(f32[448,1024]{1,0:T(8,128)S(1)} %copy-done.45, f32[448]{0:T(512)S(1)} %add_rsqrt_fusion, f32[1024]{0:T(1024)S(1)} %copy-done.105, bf16[1024,4096]{1,0:T(8,128)(2,1)} %all-gather.9.cloned.1.call-done, bf16[448,2048]{1,0:T(8,128)(2,1)S(1)} %copy-done.125, ...), kind=kOutput, calls=%fused_computation.61 | convolution fusion | flops 3768187392 | bytes 15740416 | tf_op jit(solution)/shard_map/dot_general | solution.py:60
  297.5 6.0 gated_backward.1
  317.8 4.6 all-to-all-start.2
  334.0 4.7 fusion.6
  338.8 4.5 all-to-all-done.2
  345.0 4.6 all-to-all-start.3
  349.7 10.7 %add_convert_fusion = bf16[4,2,2,192,1024]{4,3,0,2,1:T(8,128)(2,1)} fusion(bf16[4,2,2,192,1024]{4,3,0,2,1:T(8,128)(2,1)} %collective-permute-done.20, bf16[4,2,2,192,1024]{4,3,0,2,1:T(8,128)(2,1)} %copy-done.30), kind=kLoop, calls=%fused_computation | loop fusion | flops 12582912 | bytes 18874368 | tf_op jit(solution)/shard_map/convert_element_type | solution.py:144
  360.3 34.5 %attn_backward.1 = (bf16[448,512]{1,0:T(8,128)(2,1)}, bf16[16,224,256]{2,1,0:T(8,128)(2,1)}) custom-call(s32[4,17]{1,0:T(4,128)} %copy-done.15, bf16[2,2,64,896]{3,2,1,0:T(8,128)(2,1)} %copy-done.20, bf16[16,224,256]{2,1,0:T(8,128)(2,1)} %bitcast.306, bf16[448,512]{1,0:T(8,128)(2,1)} %convolution_convert_fusion.7.do_ref, f32[2,2,64,896]{3,2,1,0:T(8,128)} %copy-done.22, ...), custom_call_target="tpu_custom_call" | custom-call | flops 4367319040 | bytes 16777216 | tf_op jit(solution)/shard_map/attn_backward/pallas_call | solution.py:395
  406.9 4.0 fusion.118
  413.0 7.6 %collective-permute-done.21 = bf16[4,448,256]{2,1,0:T(8,128)(2,1)} collective-permute-done((bf16[4,448,256]{2,1,0:T(8,128)(2,1)}, bf16[4,448,256]{2,1,0:T(8,128)(2,1)}, u32[]{:S(2)}, u32[]{:S(2)}) %collective-permute-start.21) | collective-permute-done | bytes 917536 | tf_op jit(solution)/shard_map/ppermute | solution.py:37
  422.1 3.9 collective-permute-start.24
  426.6 4.5 add_convert_fusion.1
  432.5 9.6 %collective-permute-done.23 = bf16[448,256]{1,0:T(8,128)(2,1)S(1)} collective-permute-done((bf16[448,256]{1,0:T(8,128)(2,1)S(1)}, bf16[448,256]{1,0:T(8,128)(2,1)S(1)}, u32[]{:S(2)}, u32[]{:S(2)}) %collective-permute-start.23) | collective-permute-done | bytes 229408 | tf_op jit(solution)/shard_map/ppermute | solution.py:37
  443.5 9.1 %collective-permute-done.26 = bf16[2,2,192,1024]{3,2,0,1:T(8,128)(2,1)S(1)} collective-permute-done((bf16[2,2,192,1024]{3,2,0,1:T(8,128)(2,1)S(1)}, bf16[2,2,192,1024]{3,2,0,1:T(8,128)(2,1)S(1)}, u32[]{:S(2)}, u32[]{:S(2)}) %collective-permute-start.26) | collective-permute-done | bytes 1572896 | tf_op jit(solution)/shard_map/ppermute | solution.py:37
  454.0 17.0 %scan_backward.1 = (f32[448,1792]{1,0:T(8,128)}, f32[2,224,24]{2,1,0:T(8,128)}, f32[2,224,24]{2,1,0:T(8,128)}, f32[2,1,1536]{2,1,0:T(1,128)}, f32[2,1,1536]{2,1,0:T(1,128)}) custom-call(f32[448,1792]{1,0:T(8,128)} %pad_maximum_fusion.2.m_ref.c_ref, f32[448,1536]{1,0:T(8,128)} %copy-done.6, f32[448,1536]{1,0:T(8,128)} %copy-done, f32[2,224,24]{2,1,0:T(8,128)} %bitcast.301, ...), custom_call_target="tpu_custom_call" | custom-call | flops 1849688064 | bytes 13762560 | tf_op jit(solution)/shard_map/scan_backward/pallas_call | solution.py:749
  486.5 7.1 %collective-permute-done.29 = bf16[2,192,1024]{2,1,0:T(8,128)(2,1)} collective-permute-done((bf16[2,192,1024]{2,1,0:T(8,128)(2,1)}, bf16[2,192,1024]{2,1,0:T(8,128)(2,1)}, u32[]{:S(2)}, u32[]{:S(2)}) %collective-permute-start.29) | collective-permute-done | bytes 786464 | tf_op jit(solution)/shard_map/ppermute | solution.py:37
  498.1 12.6 %collective-permute-done.30 = bf16[2,2,112,1024]{3,2,0,1:T(8,128)(2,1)} collective-permute-done((bf16[2,2,112,1024]{3,2,0,1:T(8,128)(2,1)}, bf16[2,2,112,1024]{3,2,0,1:T(8,128)(2,1)}, u32[]{:S(2)}, u32[]{:S(2)}) %collective-permute-start.30) | collective-permute-done | bytes 917536 | tf_op jit(solution)/shard_map/ppermute | solution.py:37
  514.2 4.5 multiply_reduce_fusion.10
  525.7 5.3 collective-permute-start.36
  534.4 3.9 collective-permute-start.33
  542.0 12.8 %collective-permute-start.37 = (bf16[2,112,1024]{2,1,0:T(8,128)(2,1)}, bf16[2,112,1024]{2,1,0:T(8,128)(2,1)}, u32[]{:S(2)}, u32[]{:S(2)}) collective-permute-start(bf16[2,112,1024]{2,1,0:T(8,128)(2,1)} %dynamic-slice_bitcast_fusion.9), channel_id=1, source_target_pairs={{0,4},{4,0},{8,12},{12,8},{16,20},{20,16},{24,28},{28,24},{1,5},{5... | collective-permute-start | bytes 1376264 | tf_op jit(solution)/shard_map/ppermute | solution.py:37
  558.6 4.1 collective-permute-done.35
  567.8 4.4 fusion.1
  577.5 4.7 concatenate.127
  582.2 5.3 convolution_convert_fusion.1
  591.4 6.2 collective-permute-start.45
  625.8 9.3 %collective-permute-done.48 = bf16[2,2,32,2688]{3,2,0,1:T(8,128)(2,1)S(1)} collective-permute-done((bf16[2,2,32,2688]{3,2,0,1:T(8,128)(2,1)}, bf16[2,2,32,2688]{3,2,0,1:T(8,128)(2,1)S(1)}, u32[]{:S(2)}, u32[]{:S(2)}) %collective-permute-start.48) | collective-permute-done | bytes 688160 | tf_op jit(solution)/shard_map/ppermute | solution.py:37
  635.7 6.0 collective-permute-done.50
  645.5 3.7 collective-permute-done.51
  (590 shorter events, 258.0 us)
Async XLA Ops:
  7.2 226.2 %all-gather.5.cloned.1.call-start = ((), (), s32[]{:S(2)}) async-start(), calls=%async_computation.4 | async-start | bytes 3932160 | tf_op jit(solution)/shard_map/all_gather | solution.py:99
  8.6 22.2 %collective-permute-start.1 = (bf16[128,3352]{0,1:T(8,128)(2,1)S(1)}, bf16[128,3352]{0,1:T(8,128)(2,1)}, u32[]{:S(2)}, u32[]{:S(2)}) collective-permute-start(bf16[128,3352]{0,1:T(8,128)(2,1)S(1)} %constant_dynamic-slice_fusion.19), channel_id=1, source_target_pairs={{0,2},{1,3},{2,0},{3,1},{4,6},{5,7},{6,4},{7,5},{8,10},{9,11},{10,... | collective-permute-start | bytes 2574344 | tf_op jit(solution)/shard_map/ppermute | solution.py:37
  11.6 43.2 %collective-permute-start = (bf16[256,3352]{0,1:T(8,128)(2,1)}, bf16[256,3352]{0,1:T(8,128)(2,1)}, u32[]{:S(2)}, u32[]{:S(2)}) collective-permute-start(bf16[256,3352]{0,1:T(8,128)(2,1)} %param.25), channel_id=1, source_target_pairs={{0,1},{1,0},{2,3},{3,2},{4,5},{5,4},{6,7},{7,6},{8,9},{9,8},{10,11... | collective-permute-start | bytes 5148680 | tf_op jit(solution)/shard_map/ppermute | solution.py:37
  30.8 9.4 %collective-permute-start.2 = (bf16[128,3352]{0,1:T(8,128)(2,1)}, bf16[128,3352]{0,1:T(8,128)(2,1)}, u32[]{:S(2)}, u32[]{:S(2)}) collective-permute-start(bf16[128,3352]{0,1:T(8,128)(2,1)} %collective-permute-done.1), channel_id=1, source_target_pairs={{0,1},{1,0},{2,3},{3,2},{4,5},{5,4},{6,7},{7,6},{8,9},{9,8},{10,11... | collective-permute-start | bytes 2574344 | tf_op jit(solution)/shard_map/ppermute | solution.py:37
  30.8 21.8 %collective-permute-start.3 = (bf16[128,3352]{0,1:T(8,128)(2,1)}, bf16[128,3352]{0,1:T(8,128)(2,1)}, u32[]{:S(2)}, u32[]{:S(2)}) collective-permute-start(bf16[128,3352]{0,1:T(8,128)(2,1)} %collective-permute-done.1), channel_id=1, source_target_pairs={{0,4},{4,0},{8,12},{12,8},{16,20},{20,16},{24,28},{28,24},{1,5},{5... | collective-permute-start | bytes 2574344 | tf_op jit(solution)/shard_map/ppermute | solution.py:37
  64.5 174.1 %all-gather.7.cloned.1.call-start = ((), (), s32[]{:S(2)}) async-start(), calls=%async_computation.5 | async-start | bytes 1310720 | tf_op jit(solution)/shard_map/all_gather | solution.py:99
  65.2 177.2 %all-gather.9.cloned.1.call-start = ((), (), s32[]{:S(2)}) async-start(), calls=%async_computation.6 | async-start | bytes 10485760 | tf_op jit(solution)/shard_map/all_gather | solution.py:99
  66.0 187.4 %all-gather.11.cloned.1.call-start = ((), (), s32[]{:S(2)}) async-start(), calls=%async_computation.7 | async-start | bytes 5242880 | tf_op jit(solution)/shard_map/all_gather | solution.py:99
  66.0 16.1 %collective-permute-start.11 = (bf16[256,768]{1,0:T(8,128)(2,1)}, bf16[256,768]{1,0:T(8,128)(2,1)}, u32[]{:S(2)}, u32[]{:S(2)}) collective-permute-start(bf16[256,768]{1,0:T(8,128)(2,1)} %param.33), channel_id=1, source_target_pairs={{0,1},{1,0},{2,3},{3,2},{4,5},{5,4},{6,7},{7,6},{8,9},{9,8},{10,11... | collective-permute-start | bytes 1179656 | tf_op jit(solution)/shard_map/ppermute | solution.py:37
  77.1 47.2 %collective-permute-start.13 = (bf16[128,768]{1,0:T(8,128)(2,1)}, bf16[128,768]{1,0:T(8,128)(2,1)}, u32[]{:S(2)}, u32[]{:S(2)}) collective-permute-start(bf16[128,768]{1,0:T(8,128)(2,1)} %collective-permute-done.12), channel_id=1, source_target_pairs={{0,1},{1,0},{2,3},{3,2},{4,5},{5,4},{6,7},{7,6},{8,9},{9,8},{10,11... | collective-permute-start | bytes 589832 | tf_op jit(solution)/shard_map/ppermute | solution.py:37
  82.1 45.5 %collective-permute-start.15 = (bf16[128,768]{1,0:T(8,128)(2,1)}, bf16[128,768]{1,0:T(8,128)(2,1)}, u32[]{:S(2)}, u32[]{:S(2)}) collective-permute-start(bf16[128,768]{1,0:T(8,128)(2,1)} %collective-permute-done.14), channel_id=1, source_target_pairs={{0,1},{1,0},{2,3},{3,2},{4,5},{5,4},{6,7},{7,6},{8,9},{9,8},{10,11... | collective-permute-start | bytes 589832 | tf_op jit(solution)/shard_map/ppermute | solution.py:37
  118.7 49.2 %all-to-all-start = ((bf16[8,2,16,1536]{3,2,1,0:T(8,128)(2,1)}), bf16[8,2,16,1536]{3,2,1,0:T(8,128)(2,1)S(1)}, u32[]{:S(2)}, u32[]{:S(2)}) async-start(bf16[8,2,16,1536]{3,2,1,0:T(8,128)(2,1)} %bitcast.321), calls=%async_computation | async-start | bytes 1572864 | tf_op jit(solution)/shard_map/all_to_all | solution.py:542
  133.1 41.2 %collective-permute-start.18 = (bf16[448,256]{1,0:T(8,128)(2,1)S(1)}, bf16[448,256]{1,0:T(8,128)(2,1)S(1)}, u32[]{:S(2)}, u32[]{:S(2)}) collective-permute-start(bf16[448,256]{1,0:T(8,128)(2,1)S(1)} %get-tuple-element.88), channel_id=1, source_target_pairs={{0,24},{4,28},{8,16},{12,20},{16,8},{20,12},{24,0},{28,4},{1,25},{... | collective-permute-start | bytes 688136 | tf_op jit(solution)/shard_map/ppermute | solution.py:37
  136.9 10.7 %collective-permute-start.9 = (f32[2,24]{1,0:T(2,128)S(1)}, f32[2,24]{1,0:T(2,128)S(1)}, u32[]{:S(2)}, u32[]{:S(2)}) collective-permute-start(f32[2,24]{1,0:T(2,128)S(1)} %bitcast.346), channel_id=1, source_target_pairs={{0,24},{4,28},{8,16},{12,20},{16,8},{20,12},{24,0},{28,4},{1,25},{... | collective-permute-start | bytes 584 | tf_op jit(solution)/shard_map/ppermute | solution.py:37
  137.0 37.2 %collective-permute-start.17 = (bf16[448,256]{1,0:T(8,128)(2,1)S(1)}, bf16[448,256]{1,0:T(8,128)(2,1)S(1)}, u32[]{:S(2)}, u32[]{:S(2)}) collective-permute-start(bf16[448,256]{1,0:T(8,128)(2,1)S(1)} %get-tuple-element.88), channel_id=1, source_target_pairs={{0,16},{4,20},{8,24},{12,28},{16,0},{20,4},{24,8},{28,12},{1,17},{... | collective-permute-start | bytes 688136 | tf_op jit(solution)/shard_map/ppermute | solution.py:37
  138.1 25.9 %collective-permute-start.8 = (f32[2,24]{1,0:T(2,128)S(1)}, f32[2,24]{1,0:T(2,128)S(1)}, u32[]{:S(2)}, u32[]{:S(2)}) collective-permute-start(f32[2,24]{1,0:T(2,128)S(1)} %bitcast.347), channel_id=1, source_target_pairs={{0,16},{4,20},{8,24},{12,28},{16,0},{20,4},{24,8},{28,12},{1,17},{... | collective-permute-start | bytes 584 | tf_op jit(solution)/shard_map/ppermute | solution.py:37
  140.0 24.0 %collective-permute-start.7 = (f32[2,24]{1,0:T(2,128)S(1)}, f32[2,24]{1,0:T(2,128)S(1)}, u32[]{:S(2)}, u32[]{:S(2)}) collective-permute-start(f32[2,24]{1,0:T(2,128)S(1)} %bitcast.348), channel_id=1, source_target_pairs={{0,8},{4,12},{8,0},{12,4},{16,24},{20,28},{24,16},{28,20},{1,9},{5... | collective-permute-start | bytes 584 | tf_op jit(solution)/shard_map/ppermute | solution.py:37
  147.6 26.6 %collective-permute-start.16 = (bf16[448,256]{1,0:T(8,128)(2,1)S(1)}, bf16[448,256]{1,0:T(8,128)(2,1)S(1)}, u32[]{:S(2)}, u32[]{:S(2)}) collective-permute-start(bf16[448,256]{1,0:T(8,128)(2,1)S(1)} %get-tuple-element.88), channel_id=1, source_target_pairs={{0,8},{4,12},{8,0},{12,4},{16,24},{20,28},{24,16},{28,20},{1,9},{5... | collective-permute-start | bytes 688136 | tf_op jit(solution)/shard_map/ppermute | solution.py:37
  169.7 56.7 %all-to-all-start.1 = ((bf16[8,2,16,1536]{3,2,1,0:T(8,128)(2,1)}), bf16[8,2,16,1536]{3,2,1,0:T(8,128)(2,1)}, u32[]{:S(2)}, u32[]{:S(2)}) async-start(bf16[8,2,16,1536]{3,2,1,0:T(8,128)(2,1)} %bitcast.24), calls=%async_computation.1 | async-start | bytes 1572864 | tf_op jit(solution)/shard_map/all_to_all | solution.py:544
  175.3 28.1 %collective-permute-start.19 = (bf16[4,448,256]{2,1,0:T(8,128)(2,1)}, bf16[4,448,256]{2,1,0:T(8,128)(2,1)S(1)}, u32[]{:S(2)}, u32[]{:S(2)}) collective-permute-start(bf16[4,448,256]{2,1,0:T(8,128)(2,1)} %get-tuple-element.220), channel_id=1, source_target_pairs={{0,4},{4,0},{8,12},{12,8},{16,20},{20,16},{24,28},{28,24},{1,5},{5... | collective-permute-start | bytes 2752520 | tf_op jit(solution)/shard_map/ppermute | solution.py:37
  283.1 66.6 %collective-permute-start.20 = (bf16[4,2,2,192,1024]{4,3,0,2,1:T(8,128)(2,1)}, bf16[4,2,2,192,1024]{4,3,0,2,1:T(8,128)(2,1)}, u32[]{:S(2)}, u32[]{:S(2)}) collective-permute-start(bf16[4,2,2,192,1024]{4,3,0,2,1:T(8,128)(2,1)} %bitcast_dynamic-update-slice_fusion), channel_id=1, source_target_pairs={{0,1},{1,0},{2,3},{3,2},{4,5},{5,4},{6,7},{7,6},{8,9},{9,8},{10,11... | collective-permute-start | bytes 18874376 | tf_op jit(solution)/shard_map/ppermute | solution.py:37
  316.9 109.1 %collective-permute-start.27 = (bf16[4,2,2,112,1024]{4,3,0,2,1:T(8,128)(2,1)}, bf16[4,2,2,112,1024]{4,3,0,2,1:T(8,128)(2,1)}, u32[]{:S(2)}, u32[]{:S(2)}) collective-permute-start(bf16[4,2,2,112,1024]{4,3,0,2,1:T(8,128)(2,1)} %pad_maximum_fusion.1), channel_id=1, source_target_pairs={{0,1},{1,0},{2,3},{3,2},{4,5},{5,4},{6,7},{7,6},{8,9},{9,8},{10,11... | collective-permute-start | bytes 11010056 | tf_op jit(solution)/shard_map/ppermute | solution.py:37
  317.8 25.5 %all-to-all-start.2 = ((bf16[8,2,16,1536]{3,2,1,0:T(8,128)(2,1)}), bf16[8,2,16,1536]{3,2,1,0:T(8,128)(2,1)S(1)}, u32[]{:S(2)}, u32[]{:S(2)}) async-start(bf16[8,2,16,1536]{3,2,1,0:T(8,128)(2,1)} %bitcast.322), calls=%async_computation.2 | async-start | bytes 1572864 | tf_op jit(solution)/shard_map/all_to_all | solution.py:542
  345.0 59.8 %all-to-all-start.3 = ((bf16[8,2,16,1536]{3,2,1,0:T(8,128)(2,1)}), bf16[8,2,16,1536]{3,2,1,0:T(8,128)(2,1)}, u32[]{:S(2)}, u32[]{:S(2)}) async-start(bf16[8,2,16,1536]{3,2,1,0:T(8,128)(2,1)} %bitcast.85), calls=%async_computation.3 | async-start | bytes 1572864 | tf_op jit(solution)/shard_map/all_to_all | solution.py:544
  397.0 23.6 %collective-permute-start.21 = (bf16[4,448,256]{2,1,0:T(8,128)(2,1)}, bf16[4,448,256]{2,1,0:T(8,128)(2,1)}, u32[]{:S(2)}, u32[]{:S(2)}) collective-permute-start(bf16[4,448,256]{2,1,0:T(8,128)(2,1)} %slice_bitcast_fusion), channel_id=1, source_target_pairs={{0,4},{4,0},{8,12},{12,8},{16,20},{20,16},{24,28},{28,24},{1,5},{5... | collective-permute-start | bytes 2752520 | tf_op jit(solution)/shard_map/ppermute | solution.py:37
  411.1 42.2 %collective-permute-start.25 = (bf16[2,2,192,1024]{3,2,0,1:T(8,128)(2,1)S(1)}, bf16[2,2,192,1024]{3,2,0,1:T(8,128)(2,1)S(1)}, u32[]{:S(2)}, u32[]{:S(2)}) collective-permute-start(bf16[2,2,192,1024]{3,2,0,1:T(8,128)(2,1)S(1)} %dynamic-slice_bitcast_fusion.1), channel_id=1, source_target_pairs={{0,2},{1,3},{2,0},{3,1},{4,6},{5,7},{6,4},{7,5},{8,10},{9,11},{10,... | collective-permute-start | bytes 4718600 | tf_op jit(solution)/shard_map/ppermute | solution.py:37
  412.8 39.8 %collective-permute-start.26 = (bf16[2,2,192,1024]{3,2,0,1:T(8,128)(2,1)S(1)}, bf16[2,2,192,1024]{3,2,0,1:T(8,128)(2,1)S(1)}, u32[]{:S(2)}, u32[]{:S(2)}) collective-permute-start(bf16[2,2,192,1024]{3,2,0,1:T(8,128)(2,1)S(1)} %dynamic-slice_bitcast_fusion), channel_id=1, source_target_pairs={{0,4},{4,0},{8,12},{12,8},{16,20},{20,16},{24,28},{28,24},{1,5},{5... | collective-permute-start | bytes 4718600 | tf_op jit(solution)/shard_map/ppermute | solution.py:37
  422.1 10.4 %collective-permute-start.24 = (bf16[448,256]{1,0:T(8,128)(2,1)S(1)}, bf16[448,256]{1,0:T(8,128)(2,1)S(1)}, u32[]{:S(2)}, u32[]{:S(2)}) collective-permute-start(bf16[448,256]{1,0:T(8,128)(2,1)S(1)} %get-tuple-element.213), channel_id=1, source_target_pairs={{0,24},{4,28},{8,16},{12,20},{16,8},{20,12},{24,0},{28,4},{1,25},{... | collective-permute-start | bytes 688136 | tf_op jit(solution)/shard_map/ppermute | solution.py:37
  426.0 16.1 %collective-permute-start.23 = (bf16[448,256]{1,0:T(8,128)(2,1)S(1)}, bf16[448,256]{1,0:T(8,128)(2,1)S(1)}, u32[]{:S(2)}, u32[]{:S(2)}) collective-permute-start(bf16[448,256]{1,0:T(8,128)(2,1)S(1)} %get-tuple-element.214), channel_id=1, source_target_pairs={{0,16},{4,20},{8,24},{12,28},{16,0},{20,4},{24,8},{28,12},{1,17},{... | collective-permute-start | bytes 688136 | tf_op jit(solution)/shard_map/ppermute | solution.py:37
  426.0 16.1 %collective-permute-start.22 = (bf16[448,256]{1,0:T(8,128)(2,1)S(1)}, bf16[448,256]{1,0:T(8,128)(2,1)S(1)}, u32[]{:S(2)}, u32[]{:S(2)}) collective-permute-start(bf16[448,256]{1,0:T(8,128)(2,1)S(1)} %get-tuple-element.212), channel_id=1, source_target_pairs={{0,8},{4,12},{8,0},{12,4},{16,24},{20,28},{24,16},{28,20},{1,9},{5... | collective-permute-start | bytes 688136 | tf_op jit(solution)/shard_map/ppermute | solution.py:37
  472.9 20.8 %collective-permute-start.29 = (bf16[2,192,1024]{2,1,0:T(8,128)(2,1)}, bf16[2,192,1024]{2,1,0:T(8,128)(2,1)}, u32[]{:S(2)}, u32[]{:S(2)}) collective-permute-start(bf16[2,192,1024]{2,1,0:T(8,128)(2,1)} %dynamic-slice_bitcast_fusion.4), channel_id=1, source_target_pairs={{0,2},{1,3},{2,0},{3,1},{4,6},{5,7},{6,4},{7,5},{8,10},{9,11},{10,... | collective-permute-start | bytes 2359304 | tf_op jit(solution)/shard_map/ppermute | solution.py:37
  475.4 20.8 %collective-permute-start.28 = (bf16[2,192,1024]{2,1,0:T(8,128)(2,1)}, bf16[2,192,1024]{2,1,0:T(8,128)(2,1)}, u32[]{:S(2)}, u32[]{:S(2)}) collective-permute-start(bf16[2,192,1024]{2,1,0:T(8,128)(2,1)} %dynamic-slice_bitcast_fusion.5), channel_id=1, source_target_pairs={{0,4},{4,0},{8,12},{12,8},{16,20},{20,16},{24,28},{28,24},{1,5},{5... | collective-permute-start | bytes 2359304 | tf_op jit(solution)/shard_map/ppermute | solution.py:37
  480.7 30.1 %collective-permute-start.30 = (bf16[2,2,112,1024]{3,2,0,1:T(8,128)(2,1)}, bf16[2,2,112,1024]{3,2,0,1:T(8,128)(2,1)}, u32[]{:S(2)}, u32[]{:S(2)}) collective-permute-start(bf16[2,2,112,1024]{3,2,0,1:T(8,128)(2,1)} %dynamic-slice_bitcast_fusion.3), channel_id=1, source_target_pairs={{0,2},{1,3},{2,0},{3,1},{4,6},{5,7},{6,4},{7,5},{8,10},{9,11},{10,... | collective-permute-start | bytes 2752520 | tf_op jit(solution)/shard_map/ppermute | solution.py:37
  482.3 30.6 %collective-permute-start.31 = (bf16[2,2,112,1024]{3,2,0,1:T(8,128)(2,1)}, bf16[2,2,112,1024]{3,2,0,1:T(8,128)(2,1)S(1)}, u32[]{:S(2)}, u32[]{:S(2)}) collective-permute-start(bf16[2,2,112,1024]{3,2,0,1:T(8,128)(2,1)} %dynamic-slice_bitcast_fusion.2), channel_id=1, source_target_pairs={{0,4},{4,0},{8,12},{12,8},{16,20},{20,16},{24,28},{28,24},{1,5},{5... | collective-permute-start | bytes 2752520 | tf_op jit(solution)/shard_map/ppermute | solution.py:37
  523.3 11.1 %collective-permute-start.32 = (bf16[3,1792]{1,0:T(4,128)(2,1)S(1)}, bf16[3,1792]{1,0:T(4,128)(2,1)S(1)}, u32[]{:S(2)}, u32[]{:S(2)}) collective-permute-start(bf16[3,1792]{1,0:T(4,128)(2,1)S(1)} %split.21), channel_id=1, source_target_pairs={{4,0},{8,4},{12,8},{16,12},{20,16},{24,20},{28,24},{5,1},{9,5},{13... | collective-permute-start | bytes 32264 | tf_op jit(solution)/shard_map/ppermute | solution.py:68
  525.7 33.0 %collective-permute-start.36 = (bf16[192,1024]{1,0:T(8,128)(2,1)}, bf16[192,1024]{1,0:T(8,128)(2,1)}, u32[]{:S(2)}, u32[]{:S(2)}) collective-permute-start(bf16[192,1024]{1,0:T(8,128)(2,1)} %get-tuple-element.201), channel_id=1, source_target_pairs={{0,24},{4,28},{8,16},{12,20},{16,8},{20,12},{24,0},{28,4},{1,25},{... | collective-permute-start | bytes 1179656 | tf_op jit(solution)/shard_map/ppermute | solution.py:37
  531.0 31.7 %collective-permute-start.35 = (bf16[192,1024]{1,0:T(8,128)(2,1)}, bf16[192,1024]{1,0:T(8,128)(2,1)}, u32[]{:S(2)}, u32[]{:S(2)}) collective-permute-start(bf16[192,1024]{1,0:T(8,128)(2,1)} %get-tuple-element.202), channel_id=1, source_target_pairs={{0,16},{4,20},{8,24},{12,28},{16,0},{20,4},{24,8},{28,12},{1,17},{... | collective-permute-start | bytes 1179656 | tf_op jit(solution)/shard_map/ppermute | solution.py:37
  531.0 31.7 %collective-permute-start.34 = (bf16[192,1024]{1,0:T(8,128)(2,1)}, bf16[192,1024]{1,0:T(8,128)(2,1)}, u32[]{:S(2)}, u32[]{:S(2)}) collective-permute-start(bf16[192,1024]{1,0:T(8,128)(2,1)} %get-tuple-element.200), channel_id=1, source_target_pairs={{0,8},{4,12},{8,0},{12,4},{16,24},{20,28},{24,16},{28,20},{1,9},{5... | collective-permute-start | bytes 1179656 | tf_op jit(solution)/shard_map/ppermute | solution.py:37
  532.3 32.8 %collective-permute-start.38 = (bf16[2,112,1024]{2,1,0:T(8,128)(2,1)}, bf16[2,112,1024]{2,1,0:T(8,128)(2,1)}, u32[]{:S(2)}, u32[]{:S(2)}) collective-permute-start(bf16[2,112,1024]{2,1,0:T(8,128)(2,1)} %dynamic-slice_bitcast_fusion.8), channel_id=1, source_target_pairs={{0,2},{1,3},{2,0},{3,1},{4,6},{5,7},{6,4},{7,5},{8,10},{9,11},{10,... | collective-permute-start | bytes 1376264 | tf_op jit(solution)/shard_map/ppermute | solution.py:37
  542.0 24.4 %collective-permute-start.37 = (bf16[2,112,1024]{2,1,0:T(8,128)(2,1)}, bf16[2,112,1024]{2,1,0:T(8,128)(2,1)}, u32[]{:S(2)}, u32[]{:S(2)}) collective-permute-start(bf16[2,112,1024]{2,1,0:T(8,128)(2,1)} %dynamic-slice_bitcast_fusion.9), channel_id=1, source_target_pairs={{0,4},{4,0},{8,12},{12,8},{16,20},{20,16},{24,28},{28,24},{1,5},{5... | collective-permute-start | bytes 1376264 | tf_op jit(solution)/shard_map/ppermute | solution.py:37
  576.9 22.1 %collective-permute-start.39 = (f32[104,128]{1,0:T(8,128)}, f32[104,128]{1,0:T(8,128)S(1)}, u32[]{:S(2)}, u32[]{:S(2)}) collective-permute-start(f32[104,128]{1,0:T(8,128)} %pad_bitcast_fusion), channel_id=1, source_target_pairs={{0,1},{1,0},{2,3},{3,2},{4,5},{5,4},{6,7},{7,6},{8,9},{9,8},{10,11... | collective-permute-start | bytes 159752 | tf_op jit(solution)/shard_map/ppermute | solution.py:37
  588.5 31.8 %collective-permute-start.47 = (bf16[4,2,2,32,2688]{4,3,0,2,1:T(8,128)(2,1)S(1)}, bf16[4,2,2,32,2688]{4,3,0,2,1:T(8,128)(2,1)S(1)}, u32[]{:S(2)}, u32[]{:S(2)}) collective-permute-start(bf16[4,2,2,32,2688]{4,3,0,2,1:T(8,128)(2,1)S(1)} %bitcast.325), channel_id=1, source_target_pairs={{0,1},{1,0},{2,3},{3,2},{4,5},{5,4},{6,7},{7,6},{8,9},{9,8},{10,11... | collective-permute-start | bytes 8257544 | tf_op jit(solution)/shard_map/ppermute | solution.py:37
  589.1 25.9 %collective-permute-start.46 = (bf16[112,1024]{1,0:T(8,128)(2,1)S(1)}, bf16[112,1024]{1,0:T(8,128)(2,1)S(1)}, u32[]{:S(2)}, u32[]{:S(2)}) collective-permute-start(bf16[112,1024]{1,0:T(8,128)(2,1)S(1)} %get-tuple-element.210), channel_id=1, source_target_pairs={{0,24},{4,28},{8,16},{12,20},{16,8},{20,12},{24,0},{28,4},{1,25},{... | collective-permute-start | bytes 688136 | tf_op jit(solution)/shard_map/ppermute | solution.py:37
  591.4 23.6 %collective-permute-start.45 = (bf16[112,1024]{1,0:T(8,128)(2,1)S(1)}, bf16[112,1024]{1,0:T(8,128)(2,1)S(1)}, u32[]{:S(2)}, u32[]{:S(2)}) collective-permute-start(bf16[112,1024]{1,0:T(8,128)(2,1)S(1)} %get-tuple-element.211), channel_id=1, source_target_pairs={{0,16},{4,20},{8,24},{12,28},{16,0},{20,4},{24,8},{28,12},{1,17},{... | collective-permute-start | bytes 688136 | tf_op jit(solution)/shard_map/ppermute | solution.py:37
  597.6 17.4 %collective-permute-start.44 = (bf16[112,1024]{1,0:T(8,128)(2,1)S(1)}, bf16[112,1024]{1,0:T(8,128)(2,1)S(1)}, u32[]{:S(2)}, u32[]{:S(2)}) collective-permute-start(bf16[112,1024]{1,0:T(8,128)(2,1)S(1)} %get-tuple-element.209), channel_id=1, source_target_pairs={{0,8},{4,12},{8,0},{12,4},{16,24},{20,28},{24,16},{28,20},{1,9},{5... | collective-permute-start | bytes 688136 | tf_op jit(solution)/shard_map/ppermute | solution.py:37
  622.0 13.1 %collective-permute-start.48 = (bf16[2,2,32,2688]{3,2,0,1:T(8,128)(2,1)}, bf16[2,2,32,2688]{3,2,0,1:T(8,128)(2,1)S(1)}, u32[]{:S(2)}, u32[]{:S(2)}) collective-permute-start(bf16[2,2,32,2688]{3,2,0,1:T(8,128)(2,1)} %dynamic-slice_bitcast_fusion.7), channel_id=1, source_target_pairs={{0,2},{1,3},{2,0},{3,1},{4,6},{5,7},{6,4},{7,5},{8,10},{9,11},{10,... | collective-permute-start | bytes 2064392 | tf_op jit(solution)/shard_map/ppermute | solution.py:37
  625.4 16.3 %collective-permute-start.50 = (bf16[2,2,32,2688]{3,2,0,1:T(8,128)(2,1)S(1)}, bf16[2,2,32,2688]{3,2,0,1:T(8,128)(2,1)S(1)}, u32[]{:S(2)}, u32[]{:S(2)}) collective-permute-start(bf16[2,2,32,2688]{3,2,0,1:T(8,128)(2,1)S(1)} %dynamic-slice_bitcast_fusion.6), channel_id=1, source_target_pairs={{0,4},{4,0},{8,12},{12,8},{16,20},{20,16},{24,28},{28,24},{1,5},{5... | collective-permute-start | bytes 2064392 | tf_op jit(solution)/shard_map/ppermute | solution.py:37
  635.4 10.1 %collective-permute-start.49 = (bf16[2,32,2688]{2,1,0:T(8,128)(2,1)S(1)}, bf16[2,32,2688]{2,1,0:T(8,128)(2,1)S(1)}, u32[]{:S(2)}, u32[]{:S(2)}) collective-permute-start(bf16[2,32,2688]{2,1,0:T(8,128)(2,1)S(1)} %dynamic-slice_bitcast_fusion.14), channel_id=1, source_target_pairs={{0,4},{4,0},{8,12},{12,8},{16,20},{20,16},{24,28},{28,24},{1,5},{5... | collective-permute-start | bytes 1032200 | tf_op jit(solution)/shard_map/ppermute | solution.py:37
  (144 other events, 2030.4 us)
Sparse Core Ops, SparseCore 0:
  64.6 30.0 all-gather.4
  96.3 17.1 all-gather.6
  115.0 58.2 all-gather.8
  174.8 34.4 all-gather.10

commit v2 on v1

--- a/solution.py
+++ b/solution.py
@@ -69,63 +69,60 @@
     return before, after
 
 
-def gather_weight_fast(weight):
+def swap_blocks(array, wanted, size):
+    blocks = [array[:, k : k + size] for k in range(0, array.shape[1], size)]
+    return jnp.where(wanted, jnp.concatenate([blocks[k ^ 1] for k in range(len(blocks))], axis=1), array)
+
+
+def by_distance(rows):
     fs = lax.axis_index("fsdp")
-    rows, cols = weight.shape
-    half = rows // 2
-    y_bit, x_bit, c_bit = lax.axis_index("ctx") % 2, fs // 2, fs % 2
-    mine = lax.dynamic_slice_in_dim(weight, y_bit * half, half, 0)
-    first = swap(mine, "fsdp", 2)
-    second = swap(first, "ctx", 1)
-    buf = jnp.zeros((2, 2, 2, half, cols), weight.dtype)
-    zero = jnp.int32(0)
-
-    def put(buf, piece, x, c, h):
-        piece = piece.reshape(1, 1, -1, half, cols)
-        return lax.dynamic_update_slice(buf, piece, (x, c, h, zero, zero))
-
-    buf = put(buf, weight, x_bit, c_bit, zero)
-    buf = put(buf, swap(weight, "fsdp", 1), x_bit, 1 - c_bit, zero)
-    buf = put(buf, first, 1 - x_bit, c_bit, y_bit)
-    buf = put(buf, swap(first, "fsdp", 1), 1 - x_bit, 1 - c_bit, y_bit)
-    buf = put(buf, second, 1 - x_bit, c_bit, 1 - y_bit)
-    buf = put(buf, swap(second, "fsdp", 1), 1 - x_bit, 1 - c_bit, 1 - y_bit)
-    return buf.reshape(4 * rows, cols)
-
-
-def gather_weight(weight, fast):
-    if fast and lax.axis_size("fsdp") == 4 and lax.axis_size("ctx") % 2 == 0:
-        return gather_weight_fast(weight)
+    size = rows.shape[1] // 4
+    return swap_blocks(swap_blocks(rows, fs // 2 == 1, 2 * size), fs % 2 == 1, size)
+
+
+def gather_plain(weight):
     return lax.all_gather(weight, "fsdp", axis=0, tiled=True)
 
 
-def gather_ctx(piece):
-    count = lax.axis_size("ctx")
-    outer = jnp.stack([piece] + [swap(piece, "ctx", k) for k in range(2, count, 2)])
-    both = jnp.stack([outer, swap(outer, "ctx", 1)], axis=1)
-    return both.reshape((count,) + piece.shape)
-
-
-def reduce_ctx(stacked):
-    count = lax.axis_size("ctx")
-    parts = stacked.reshape((count // 2, 2) + stacked.shape[1:])
-    parts = (parts[:, 0].astype(f32) + swap(parts[:, 1], "ctx", 1).astype(f32)).astype(bf16)
-    total = parts[0].astype(f32)
-    for k in range(2, count, 2):
-        total = total + swap(parts[k // 2], "ctx", k).astype(f32)
-    return total
+def gather_whole(weight):
+    far = swap(weight, "fsdp", 2)
+    return [weight, swap(weight, "fsdp", 1), far, swap(far, "fsdp", 1)]
+
+
+def gather_outer(piece):
+    return [piece] + [swap(piece, "ctx", k) for k in range(2, lax.axis_size("ctx"), 2)]
 
 
 def pick(array, index, dim):
     return lax.dynamic_index_in_dim(array, index, dim, keepdims=False)
 
 
-def exchange_sum(array, dim, axis, stride, size):
+def sum_all(flat):
+    rows, cols = flat.shape[4:]
+    return lax.psum_scatter(
+        flat.reshape(-1, cols), ("ctx", "fsdp"), scatter_dimension=0, tiled=True
+    ).astype(f32)
+
+
+def column_blocks(array, width):
+    return [array[..., k : k + width] for k in range(0, array.shape[-1], width)]
+
+
+def beside(rows, blocks):
+    each = rows.shape[0] // blocks
+    return jnp.concatenate([rows[k * each : (k + 1) * each] for k in range(blocks)], axis=1)
+
+
+def exchange(array, dim, axis, stride, size):
     own = (lax.axis_index(axis) // stride) % size
-    total = pick(array, own, dim).astype(f32)
+    terms = [pick(array, own, dim)]
     for k in range(1, size):
-        total = total + swap(pick(array, own ^ k, dim), axis, k * stride).astype(f32)
-    return total
+        terms.append(swap(pick(array, own ^ k, dim), axis, k * stride))
+    return terms
+
+
+def add_up(terms):
+    return sum(term.astype(f32) for term in terms)
 
 
 def rows_by_owner(grad):
@@ -144,34 +141,29 @@
     return (keep.astype(f32) + swap(send, "fsdp", 1).astype(f32)).astype(bf16)
 
 
-def sum_first(parts):
-    half, wide = parts.shape[0] // 2, parts.shape[2]
-    low = exchange_sum(parts[:half], 2, "fsdp", 2, wide).astype(bf16)
-    high = exchange_sum(parts[half:], 1, "ctx", 1, 2).astype(bf16)
-    return low, high
-
-
-def sum_second(low, high):
-    low = exchange_sum(low, 1, "ctx", 1, 2).astype(bf16)
-    high = exchange_sum(high, 1, "fsdp", 2, high.shape[1]).astype(bf16)
-    return jnp.concatenate([low, high], axis=0)
-
-
-def sum_last(parts):
-    return exchange_sum(parts, 0, "ctx", 2, parts.shape[0])
-
-
 def tie(*arrays):
     return lax.optimization_barrier(arrays)
 
 
-def all_sum(array):
-    for axis in ("fsdp", "ctx"):
-        distance = 1
-        while distance < lax.axis_size(axis):
-            array = array + swap(array, axis, distance)
-            distance *= 2
+def all_sum(array, axis, distance, limit):
+    while distance < limit:
+        array = array + swap(array, axis, distance)
+        distance *= 2
     return array
+
+
+def tail_sums(parts, small):
+    ctx_count, fs_count = lax.axis_size("ctx"), lax.axis_size("fsdp")
+    half, wide = parts.shape[0] // 2, fs_count // 2
+    low = exchange(parts[:half], 2, "fsdp", 2, wide)
+    high = exchange(parts[half:], 1, "ctx", 1, 2)
+    small, *terms = tie(all_sum(small, "fsdp", 1, fs_count), *low, *high)
+    low, high = (add_up(part).astype(bf16) for part in (terms[:wide], terms[wide:]))
+    low = exchange(low, 1, "ctx", 1, 2)
+    high = exchange(high, 1, "fsdp", 2, wide)
+    small, *terms = tie(all_sum(small, "ctx", 1, 2), *low, *high)
+    both = jnp.concatenate([add_up(part).astype(bf16) for part in (terms[:2], terms[2:])], axis=0)
+    return add_up(exchange(both, 0, "ctx", 2, ctx_count // 2)), all_sum(small, "ctx", 2, ctx_count)
 
 
 def pair_table(ctx_count, mine):
@@ -510,9 +502,9 @@
 
 def state_kernel(order, upd_ref, fade_ref, out_ref):
     def one(i, state):
-        place = order[0, i]
+        place = order[i]
         out_ref[place] = state.astype(bf16)
-        return state * fade_ref[pl.ds(order[1, i], 1), :] + upd_ref[place].astype(f32)
+        return state * fade_ref[pl.ds(place, 1), :] + upd_ref[place].astype(f32)
 
     lax.fori_loop(0, upd_ref.shape[0], one, jnp.zeros(upd_ref.shape[1:], f32))
 
@@ -535,13 +527,16 @@
     )(order, updates, fades)
 
 
-def exchange_states(order, updates, fades):
+def send_updates(updates):
     count = lax.axis_size("ctx")
     share = NS // count
     parts = updates.reshape(2, count, share, DI).swapaxes(0, 1)
-    pieces = lax.all_to_all(parts, "ctx", 0, 0).reshape(2 * count, share, DI)
-    states = run_states(order, pieces, fades).reshape(count, 2, share, DI)
-    back = lax.all_to_all(states, "ctx", 0, 0)
+    return lax.all_to_all(parts, "ctx", 0, 0).reshape(2 * count, share, DI)
+
+
+def return_states(states):
+    count = lax.axis_size("ctx")
+    back = lax.all_to_all(states.reshape(count, 2, NS // count, DI), "ctx", 0, 0)
     return back.swapaxes(0, 1).reshape(2, NS, DI)
 
 
@@ -776,6 +771,25 @@
     )(mixed, scan_grad, scan_out, dt, cum, cum_t, skip_row, states, carries)
 
 
+def branch_columns(gated, attended):
+    shards = lax.axis_size("fsdp")
+    one, two = gated.shape[1] // shards, attended.shape[1] // shards
+    pieces = []
+    for k in range(shards):
+        pieces += [gated[:, k * one : (k + 1) * one], attended[:, k * two : (k + 1) * two]]
+    return jnp.concatenate(pieces, axis=1)
+
+
+def branch_split(columns, one, two):
+    shards = lax.axis_size("fsdp")
+    one, two = one // shards, two // shards
+    starts = [k * (one + two) for k in range(shards)]
+    return (
+        jnp.concatenate([columns[:, k : k + one] for k in starts], axis=1),
+        jnp.concatenate([columns[:, k + one : k + one + two] for k in starts], axis=1),
+    )
+
+
 def conv_block(previous, raw_rows, conv_weight, conv_bias):
     extended = jnp.concatenate([previous, raw_rows], axis=0)
     row_count = raw_rows.shape[0]
@@ -841,29 +855,34 @@
     hidden = arrange(tokens[0]).astype(f32)
     out_grad = arrange(cotangent[0]).astype(f32)
 
-    full_qkv = gather_weight(attention_in, True)
-    full_in = gather_weight(in_proj, True)
-    full_in, out_proj, attention_out, gate_up, down_proj = lax.optimization_barrier(
-        (full_in, out_proj, attention_out, gate_up, down_proj)
-    )
-    full_out = gather_weight(out_proj, False)
-    full_output_weight = gather_weight(attention_out, False)
-    full_gu = gather_weight(gate_up, False)
-    full_down = gather_weight(down_proj, False)
-
     scale_one = norm_scale(hidden)
     normed_one = (hidden * scale_one * mixer_gain).astype(bf16)
 
-    qkv_rows = matmul(normed_one, full_qkv)
+    mixer_in, gate_in = in_proj[:, DI:], in_proj[:, :DI]
+    branch_rows = jnp.concatenate([out_proj, attention_out], axis=0)
+    if lax.axis_size("fsdp") == 4 and ctx_count % 2 == 0:
+        qkv_parts = gather_whole(attention_in)
+        mixer_in, qkv_parts[2] = tie(mixer_in, qkv_parts[2])
+        in_parts = gather_whole(mixer_in)
+        full_qkv, full_in = jnp.concatenate(qkv_parts), jnp.concatenate(in_parts)
+        order_rows = by_distance
+    else:
+        full_qkv, full_in = gather_plain(attention_in), gather_plain(mixer_in)
+        order_rows = lambda rows: rows
+    full_gate_in = gather_plain(gate_in)
+    full_branch = gather_plain(branch_rows)
+    full_gu = gather_plain(gate_up)
+    full_down = gather_plain(down_proj)
+    normed_turned = order_rows(normed_one)
+
+    qkv_rows = matmul(normed_turned, full_qkv)
     q_t, pairs = prepare(qkv_rows, cosine, sine)
-    all_pairs = gather_ctx(pairs).reshape(2 * ctx_count, half_rows, 2 * kv_width)
+    outer_pairs = gather_outer(pairs)
     table = pair_table(ctx_count, my_index)
     query_row = jnp.tile(jnp.arange(half_rows, dtype=jnp.int32), GROUP)[None]
-    attn_low, attn_t, log_total = attn_forward(table, q_t, all_pairs, query_row)
-
-    projected = matmul(normed_one, full_in)
-    raw_conv = projected[:, DI : DI + CONV]
-    step_raw = projected[:, DI + CONV :]
+    projected = matmul(normed_turned, full_in)
+    raw_conv = projected[:, :CONV]
+    step_raw = projected[:, CONV:]
     early_tail = raw_conv[half_rows - lag_rows : half_rows]
     edges = jnp.concatenate([raw_conv[device_rows - lag_rows :], early_tail], axis=0)
     before, after = edge_exchange(edges.astype(bf16), lag_rows)
@@ -878,6 +897,9 @@
         ],
         axis=0,
     )
+    mixed, *outer_pairs = tie(mixed, *outer_pairs)
+    outer_pairs = jnp.stack(outer_pairs)
+    inner_pairs = swap(outer_pairs, "ctx", 1)
     step_size = jax.nn.softplus(step_raw + step_bias[None, :])
     decay_rate = -jnp.exp(decay_log)
     dt = step_size.reshape(2, half_rows, MH)
@@ -885,21 +907,27 @@
     cum = jnp.einsum("ts,bsh->bth", lower, dt * decay_rate, precision=highest)
     cum_t = cum.swapaxes(1, 2)
     skip_row = jnp.repeat(skip_gain, MP)[None]
+    fades = jnp.broadcast_to(jnp.exp(cum[:, half_rows - 1]), (ctx_count, 2, MH))
+    fades = lax.all_to_all(fades, "ctx", 0, 0)
+    fades = jnp.repeat(fades.reshape(2 * ctx_count, MH), MP, axis=1)
     part, updates = scan_forward(mixed, dt, cum, cum_t, skip_row)
 
-    fades = gather_ctx(jnp.exp(cum[:, half_rows - 1]))
-    fades = jnp.repeat(fades.reshape(2 * ctx_count, MH), MP, axis=1)
     block = jnp.arange(2 * ctx_count, dtype=jnp.int32)
     block_late = block >= ctx_count
     block_device = jnp.where(block_late, 2 * ctx_count - 1 - block, block)
-    order = jnp.stack([block_device, block_device ^ my_index]) * 2 + block_late.astype(jnp.int32)
-    states = exchange_states(order, updates, fades)
+    order = block_device * 2 + block_late.astype(jnp.int32)
+    updates, inner_pairs = tie(updates, inner_pairs)
+    all_pairs = jnp.stack([outer_pairs, inner_pairs], axis=1)
+    all_pairs = all_pairs.reshape(2 * ctx_count, half_rows, 2 * kv_width)
+    pieces = send_updates(updates)
+    gate_z, pieces = tie(matmul(normed_one, full_gate_in), pieces)
+    states = return_states(run_states(order, pieces, fades))
+    attn_low, attn_t, log_total = attn_forward(table, q_t, all_pairs, query_row)
+    states, attn_low = tie(states, attn_low)
     gain_row = gated_gain[None]
-    scan_out, gated_low = gated_forward(part, mixed, cum, states, projected, gain_row)
-
-    mamba_out = matmul(gated_low, full_out)
-    attn_out = matmul(attn_low, full_output_weight)
-    second = hidden + mamba_out + attn_out
+    scan_out, gated_low = gated_forward(part, mixed, cum, states, gate_z, gain_row)
+
+    second = hidden + matmul(branch_columns(gated_low, attn_low), full_branch)
     scale_two = norm_scale(second)
     normed_two = (second * scale_two * feed_gain).astype(bf16)
     gate_rows = matmul(normed_two, full_gu)
@@ -911,64 +939,52 @@
     result = second + matmul(activated, full_down)
 
     down_grad = out_grad.astype(bf16)
-    down_part = row_contract(activated, down_grad)
+    d_model = hidden.shape[1]
+    down_part = rows_by_owner(row_contract(activated, down_grad))
     act_grad = backward_product(down_grad, full_down)
     gate_grad = act_grad * up_part * sig_gate * (1.0 + gate_part * (1.0 - sig_gate))
     up_grad = act_grad * silu_gate
     gu_grad = jnp.concatenate([gate_grad, up_grad], axis=1).astype(bf16)
-    gu_part = rows_by_owner(row_contract(normed_two, gu_grad))
-    d_model = hidden.shape[1]
-    sum_1 = sum_core(
-        [gu_part[..., k : k + d_model] for k in range(0, 2 * FF, d_model)] + [rows_by_owner(down_part)]
-    )
+    gu_parts = [
+        rows_by_owner(row_contract(normed_two, gu_grad[:, k : k + d_model])) for k in range(0, 2 * FF, d_model)
+    ]
     normed_two_grad = backward_product(gu_grad, full_gu)
     grad_feed = jnp.sum(normed_two_grad * second * scale_two, axis=0)
     resid_grad = out_grad + norm_backward(normed_two_grad * feed_gain, second, scale_two)
     branch_gradient = resid_grad.astype(bf16)
-    gated_grad = backward_product(branch_gradient, full_out)
+    gated_grad, attn_grad = branch_split(
+        backward_product(branch_gradient, full_branch), DI, QUERY_HEADS * HEAD_WIDTH
+    )
     scan_grad, z_grad, gain_parts, direct = gated_backward(
-        gated_grad, scan_out, projected, gain_row, mixed, cum
+        gated_grad, scan_out, gate_z, gain_row, mixed, cum
     )
     grad_gated = jnp.sum(gain_parts[:, 0], axis=0)
-    carries = exchange_states(order[:, ::-1], direct, fades)
-
-    attn_grad = backward_product(branch_gradient, full_output_weight).astype(bf16)
-    attn_grad, sum_1 = tie(attn_grad, sum_1)
-    sum_1 = sum_first(sum_1)
-    z_wide = row_contract(normed_one, z_grad[:, :d_model])
+    pieces = send_updates(direct)
+
+    attn_grad, pieces = tie(attn_grad.astype(bf16), pieces)
+    carries = return_states(run_states(order[::-1], pieces, fades))
+    z_part = rows_by_owner(row_contract(normed_one, z_grad[:, :d_model]))
     z_rest = rows_by_owner(row_contract(normed_one, z_grad[:, d_model:]))
-    rest_rows = z_rest.shape[4] // 2
-    sum_2 = sum_core(
-        [
-            rows_by_owner(row_contract(gated_low, branch_gradient)),
-            rows_by_owner(row_contract(attn_low, branch_gradient)),
-            rows_by_owner(z_wide),
-            jnp.concatenate([z_rest[..., :rest_rows, :], z_rest[..., rest_rows:, :]], axis=5),
-        ]
-    )
+    z_half = z_rest.shape[4] // 2
+    views = [
+        rows_by_owner(row_contract(gated_low, branch_gradient)),
+        rows_by_owner(row_contract(attn_low, branch_gradient)),
+        z_part,
+        jnp.concatenate([z_rest[..., :z_half, :], z_rest[..., z_half:, :]], axis=5),
+    ]
+    views = gu_parts + [down_part] + views
+    attn_grad, flat = tie(attn_grad, jnp.concatenate(views, axis=4))
+    sums = sum_all(flat)
     dq, d_pairs = attn_backward(
         table, q_t, all_pairs, attn_grad, attn_t, log_total, cosine, sine, query_row
     )
-    pair_grad = reduce_ctx(d_pairs.reshape(ctx_count, device_rows, 2 * kv_width))
-    key_grad = pair_grad[:, :kv_width]
-    quarter = HEAD_WIDTH // 2
-    key_swapped = jnp.concatenate(
-        [key_grad[:, k * quarter : (k + 1) * quarter] for k in (1, 0, 3, 2)], axis=1
-    )
-    qkv_grad = jnp.concatenate(
-        [dq, (key_grad * cosine - key_swapped * sine).astype(bf16), pair_grad[:, kv_width:].astype(bf16)],
-        axis=1,
-    )
-
-    scan_grad, sum_1, sum_2 = tie(scan_grad, sum_1, sum_2)
-    sum_1 = sum_second(*sum_1)
-    sum_2 = sum_first(sum_2)
+    d_pairs, carries = tie(d_pairs, carries)
+    d_pairs = d_pairs.reshape(ctx_count // 2, 2, device_rows, 2 * kv_width)
+    pairs_sent, scan_grad = tie(d_pairs[:, 1], scan_grad)
+    pairs_came = swap(pairs_sent, "ctx", 1)
     mixed_grad, d_cum, d_dt, skip_parts, last_parts = scan_backward(
         mixed, scan_grad, scan_out, dt, cum, cum_t, skip_row, states, carries
     )
-    mixed_grad, sum_1, sum_2 = tie(mixed_grad, sum_1, sum_2)
-    sum_1 = sum_last(sum_1)
-    sum_2 = sum_second(*sum_2)
     grad_skip = jnp.sum(skip_parts.reshape(2, MH, MP), axis=(0, 2))
     last = jnp.sum(last_parts.reshape(2, MH, MP), axis=2)
     log_grad = jnp.einsum("ts,bth->bsh", lower, d_cum, precision=highest) + last[:, None, :]
@@ -985,26 +1001,35 @@
         mixed_grad[half_rows:]
     )
     backs = jnp.concatenate([prev_early_grad, prev_late_grad], axis=0)
-    before_g, after_g = edge_exchange(backs.astype(bf16), lag_rows)
+    backs, pairs_came = tie(backs.astype(bf16), pairs_came)
+    own_pairs = (d_pairs[:, 0].astype(f32) + pairs_came.astype(f32)).astype(bf16)
+    pair_terms = [own_pairs[0]] + [swap(own_pairs[k // 2], "ctx", k) for k in range(2, ctx_count, 2)]
+    before_g, after_g = edge_exchange(backs, lag_rows)
     early_tail_grad = after_g.astype(f32) + jnp.where(is_last, prev_late_grad, 0.0)
     late_tail_grad = before_g.astype(f32)
     raw_early_grad = raw_early_grad.at[half_rows - lag_rows :].add(early_tail_grad)
     raw_late_grad = raw_late_grad.at[half_rows - lag_rows :].add(late_tail_grad)
     raw_grad = jnp.concatenate([raw_early_grad, raw_late_grad], axis=0)
-    raw_grad, sum_1, sum_2 = tie(raw_grad.astype(bf16), sum_1, sum_2)
-    sum_2 = sum_last(sum_2)
+    raw_grad, *pair_terms = tie(raw_grad.astype(bf16), *pair_terms)
+    pair_grad = sum(term.astype(f32) for term in pair_terms)
+    key_grad = pair_grad[:, :kv_width]
+    quarter = HEAD_WIDTH // 2
+    key_swapped = jnp.concatenate(
+        [key_grad[:, k * quarter : (k + 1) * quarter] for k in (1, 0, 3, 2)], axis=1
+    )
+    qkv_grad = jnp.concatenate(
+        [dq, (key_grad * cosine - key_swapped * sine).astype(bf16), pair_grad[:, kv_width:].astype(bf16)],
+        axis=1,
+    )
     tail_width = CONV + MH
     tail_grad = jnp.concatenate(
         [raw_grad, step_raw_grad.astype(bf16), jnp.zeros((device_rows, -tail_width % 128), bf16), qkv_grad],
         axis=1,
     )
     sum_3 = sum_core([rows_by_owner(row_contract(normed_one, tail_grad))])
-    sum_3 = sum_last(sum_second(*sum_first(sum_3)))
-    normed_one_grad = (
-        backward_product(qkv_grad, full_qkv)
-        + backward_product(z_grad, full_in[:, :DI])
-        + backward_product(tail_grad[:, :tail_width], full_in[:, DI:])
-    )
+    normed_one_grad = order_rows(
+        backward_product(qkv_grad, full_qkv) + backward_product(tail_grad[:, :tail_width], full_in)
+    ) + backward_product(z_grad, full_gate_in)
     grad_mixer = jnp.sum(normed_one_grad * hidden * scale_one, axis=0)
     input_grad = resid_grad + norm_backward(normed_one_grad * mixer_gain, hidden, scale_one)
 
@@ -1018,28 +1043,20 @@
         grad_decay,
         grad_skip,
     )
-    each = d_model // (ctx_count * lax.axis_size("fsdp"))
-    gu_blocks = 2 * FF // d_model
-    grad_gu = jnp.concatenate([sum_1[k * each : (k + 1) * each] for k in range(gu_blocks)], axis=1)
-    grad_down = sum_1[gu_blocks * each :]
-    cuts = []
-    for rows in (each * DI // d_model, each * QUERY_HEADS * HEAD_WIDTH // d_model, each, each // 2):
-        cuts.append(sum_2[:rows])
-        sum_2 = sum_2[rows:]
-    grad_out, grad_o = cuts[:2]
-    grad_in = jnp.concatenate(
-        [
-            cuts[2],
-            jnp.concatenate([cuts[3][:, : d_model // 2], cuts[3][:, d_model // 2 :]], axis=0),
-            sum_3[:, :tail_width],
-        ],
-        axis=1,
-    )
-    grad_qkv = sum_3[:, tail_width + -tail_width % 128 :]
     flat = jnp.concatenate(small)
     size = flat.shape[0]
     flat = jnp.pad(flat, (0, -size % 1024)).reshape(-1, 128)
-    flat = all_sum(flat).reshape(-1)
+    sum_3, flat = tail_sums(sum_3, flat)
+    flat = flat.reshape(-1)
+    pieces, start = [], 0
+    for view in views:
+        pieces.append(sums[start : start + view.shape[4]])
+        start += view.shape[4]
+    grad_gu = jnp.concatenate(pieces[: len(gu_parts)], axis=1)
+    grad_down, grad_out, grad_o, grad_z, z_rest = pieces[len(gu_parts) :]
+    z_rest = jnp.concatenate([z_rest[:, : d_model // 2], z_rest[:, d_model // 2 :]], axis=0)
+    grad_in = jnp.concatenate([grad_z, z_rest, sum_3[:, :tail_width]], axis=1)
+    grad_qkv = sum_3[:, tail_width + -tail_width % 128 :]
     sums, start = [], 0
     for piece in small:
         sums.append(flat[start : start + piece.shape[0]])

time: 677 us -> 566 us (0.84)
  local copies, waits for them, and re-layouts: 115 us -> 81.2 us
  waiting for transfers between devices: 172 us -> 139 us
  other arithmetic: 70.2 us -> 47.1 us
  starting transfers between devices: 118 us -> 102 us
    ppermute x51 -> x27, waiting for transfers between devices: 164 us -> 121 us  [swap(): return lax.ppermute(array, axis, xor_pairs(lax.axis_size(axis), distance))]
    ppermute x51 -> x27, starting transfers between devices: 87.7 us -> 58.2 us  [swap(): return lax.ppermute(array, axis, xor_pairs(lax.axis_size(axis), distance))]
    unnamed x264 -> x237, local copies, waits for them, and re-layouts: 23.8 us -> 42.9 us
    dynamic_update_slice x12 -> x0, local copies, waits for them, and re-layouts: 14.7 us -> none  [put(): return lax.dynamic_update_slice(buf, piece, (x, c, h, zero, zero))]
    all_to_all x4 -> x5, starting transfers between devices: 19.5 us -> 33 us  [the longest x2 14 us: send_updates(): return lax.all_to_all(parts, 'ctx', 0, 0).reshape(2 * count, share, DI)]
    convert_element_type x3 -> x1, other arithmetic: 15.8 us -> 3.32 us  [sum_core(): return (keep.astype(f32) + swap(send, 'fsdp', 1).astype(f32)).astype(bf16)]
    reshape x8 -> x2, local copies, waits for them, and re-layouts: 12.1 us -> 1.87 us  [send_updates(): parts = updates.reshape(2, count, share, DI).swapaxes(0, 1)]
    convert_element_type x15 -> x7, other arithmetic: 13.2 us -> 3.37 us  [the longest x1 1.45 us: local(): (d_pairs[:, 0].astype(f32) + pairs_came.astype(f32)).astype(bf16)]
  transfers between devices with their start and end apart: 63 -> 41, of which waited for: 30 -> 15; matrix products, arithmetic and copies ran while one was open for 28% -> 26% of each run, Pallas kernels for 12% -> 16%
where the time goes in v2:
time: 566 us; the launch traced here: 558 us
  waiting for transfers between devices  139 us (25%)
  starting transfers between devices  102 us (18%)
  Pallas kernels  93.9 us (17%)
  local copies, waits for them, and re-layouts  81.2 us (14%)
  matrix products  78.8 us (14%)
  other arithmetic  47.1 us (8%)
  between operations  16.7 us (3%)
    ppermute x27, waiting for transfers between devices, swap(): return lax.ppermute(array, axis, xor_pairs(lax.axis_size(axis), distance))  121 us
    ppermute x27, starting transfers between devices, swap(): return lax.ppermute(array, axis, xor_pairs(lax.axis_size(axis), distance))  58.2 us
    unnamed x237, local copies, waits for them, and re-layouts  42.9 us
    pallas_call x1, Pallas kernels, attn_backward(): pl.pallas_call(attn_backward_kernel, grid_spec=pltpu.PrefetchScalarGridSp...  34.5 us
    dot_general x6, matrix products, matmul(): return jnp.dot(left, right, preferred_element_type=f32)  29.2 us
    dot_general x10, matrix products, row_contract(): lax.dot_general(left, right, (((0,), (0,)), ((), ())), preferred_element_...  25.6 us
    dot_general x6, matrix products, backward_product(): lax.dot_general(grad_rows, weight, (((1,), (1,)), ((), ())), preferred_el...  23.1 us
    pallas_call x1, Pallas kernels, attn_forward(): pl.pallas_call(attn_forward_kernel, grid_spec=pltpu.PrefetchScalarGridSpe...  20.1 us
  transfers between devices with their start and end apart: 41, of which 15 were waited for; matrix products, arithmetic and copies ran while one was open for 26% of the time, Pallas kernels for 16%

profile of v2, /device:TPU:0, one launch (start us, length us, event | category | flops | bytes accessed | tf_op | source)
XLA Modules:
  0.0 558.3 jit_solution(8382869873420606922)
XLA Ops:
  11.3 3.0 collective-permute-start
  19.7 6.6 %collective-permute-done = bf16[256,768]{1,0:T(8,128)(2,1)S(1)} collective-permute-done((bf16[256,768]{1,0:T(8,128)(2,1)}, bf16[256,768]{1,0:T(8,128)(2,1)S(1)}, u32[]{:S(2)}, u32[]{:S(2)}) %collective-permute-start) | collective-permute-done | bytes 393248 | tf_op jit(solution)/shard_map/ppermute | solution.py:37
  33.4 27.2 %collective-permute-done.2 = bf16[256,1816]{0,1:T(8,128)(2,1)} collective-permute-done((bf16[256,1816]{0,1:T(8,128)(2,1)S(1)}, bf16[256,1816]{0,1:T(8,128)(2,1)}, u32[]{:S(2)}, u32[]{:S(2)}) %collective-permute-start.2) | collective-permute-done | bytes 929824 | tf_op jit(solution)/shard_map/ppermute | solution.py:37
  71.4 3.7 collective-permute-start.4
  76.7 4.0 collective-permute-done.5
  80.8 3.4 fusion.32
  87.1 4.7 collective-permute-start.11
  93.4 9.1 %all-to-all-start.1 = ((f32[8,2,24]{2,1,0:T(2,128)}), f32[8,2,24]{2,1,0:T(2,128)S(1)}, u32[]{:S(2)}, u32[]{:S(2)}) async-start(f32[8,2,24]{2,1,0:T(2,128)} %broadcast_in_dim.43), calls=%async_computation.1 | async-start | bytes 16384 | tf_op jit(solution)/shard_map/all_to_all | solution.py:911
  102.5 7.7 %scan_forward.1 = (f32[448,1536]{1,0:T(8,128)S(1)}, bf16[2,128,1536]{2,1,0:T(8,128)(2,1)S(1)}) custom-call(f32[448,1792]{1,0:T(8,128)} %pad_maximum_fusion.m_ref.c_ref, f32[2,224,24]{2,1,0:T(8,128)S(1)} %bitcast.175, f32[2,224,24]{2,1,0:T(8,128)S(1)} %bitcast.170, f32[2,24,224]{2,1,0:T(8,128)S(1)} %fusion.53.cumt_ref, ...), custom_call_target="tpu_custom_call" | custom-call | flops 616562688 | bytes 5505024 | tf_op jit(solution)/shard_map/scan_forward/pallas_call | solution.py:474
  113.6 8.1 %all-to-all-start = ((bf16[8,2,16,1536]{3,2,1,0:T(8,128)(2,1)}), bf16[8,2,16,1536]{3,2,1,0:T(8,128)(2,1)S(1)}, u32[]{:S(2)}, u32[]{:S(2)}) async-start(bf16[8,2,16,1536]{3,2,1,0:T(8,128)(2,1)} %bitcast.192), calls=%async_computation | async-start | bytes 1572864 | tf_op jit(solution)/shard_map/all_to_all | solution.py:534
  122.6 5.1 fusion.116.z_ref
  127.7 12.6 %all-to-all-done = bf16[8,2,16,1536]{3,2,1,0:T(8,128)(2,1)S(1)} async-done(((bf16[8,2,16,1536]{3,2,1,0:T(8,128)(2,1)}), bf16[8,2,16,1536]{3,2,1,0:T(8,128)(2,1)S(1)}, u32[]{:S(2)}, u32[]{:S(2)}) %all-to-all-start) | async-done | bytes 786464 | tf_op jit(solution)/shard_map/all_to_all | solution.py:534
  142.0 3.5 all-to-all-start.2
  149.2 20.1 %attn_forward.1 = (bf16[448,512]{1,0:T(8,128)(2,1)S(1)}, f32[2,2,64,896]{3,2,1,0:T(8,128)S(1)}, f32[2,2,1,896]{3,2,1,0:T(1,128)S(1)}) custom-call(s32[4,17]{1,0:T(4,128)S(1)} %pad_add_fusion.3.tab, bf16[2,2,64,896]{3,2,1,0:T(8,128)(2,1)S(1)} %copy-done.17, bf16[16,224,256]{2,1,0:T(8,128)(2,1)S(1)} %bitcast.180, s32[1,896]{1,0:T(1,128)S(1)} %broadcast_in_dim_tile.5.row_ref), custom_call_target="tpu_custom_call" | custom-call | flops 1746927616 | bytes 8388608 | tf_op jit(solution)/shard_map/attn_forward/pallas_call | solution.py:302
  172.9 4.4 gated_forward.1
  184.6 5.0 multiply_reduce_fusion.2
  191.9 10.7 %fusion.117 = f32[448,4096]{1,0:T(8,128)} fusion(bf16[448,1024]{1,0:T(8,128)(2,1)} %multiply_convert_fusion.3, bf16[1024,4096]{1,0:T(8,128)(2,1)} %all-gather.9.cloned.1.call-done), kind=kOutput, calls=%fused_computation.309 | convolution fusion | flops 3758096384 | bytes 16646144 | tf_op jit(solution)/shard_map/dot_general | solution.py:52
  202.6 8.7 %multiply_convert_fusion.1 = (bf16[448,2048]{1,0:T(8,128)(2,1)S(1)}, bf16[448,2048]{1,0:T(8,128)(2,1)S(1)}, bf16[448,2048]{1,0:T(8,128)(2,1)}) fusion(f32[448,4096]{1,0:T(8,128)} %fusion.117, bf16[2048,1024]{1,0:T(8,128)(2,1)} %all-gather.11.cloned.1.call-done, bf16[224,1024]{1,0:T(8,128)(2,1)S(1)} %copy-done.58, bf16[224,1024]{1,0:T(8,128)(2,1)S(1)} %copy-done.56), kind=kOutput, calls=%fused_computation.10 | convolution fusion | flops 1894645760 | bytes 17956864 | tf_op jit(solution)/shard_map/dot_general | solution.py:60
  214.0 2.7 convolution_convert_fusion.6
  216.7 2.6 convolution_convert_fusion.5
  222.8 5.8 %multiply_reduce_fusion = (f32[1024]{0:T(1024)S(1)}, f32[448]{0:T(512)S(1)}, f32[448,1024]{1,0:T(8,128)S(1)}) fusion(f32[448,1024]{1,0:T(8,128)S(1)} %copy-done.42, f32[448]{0:T(512)S(1)} %add_rsqrt_fusion, f32[1024]{0:T(1024)S(1)} %copy-done.88, bf16[1024,4096]{1,0:T(8,128)(2,1)S(1)} %bitcast.213, bf16[448,2048]{1,0:T(8,128)(2,1)} %copy-done.104, ...), kind=kOutput, calls=%fused_computation.52 | convolution fusion | flops 3768187392 | bytes 15740416 | tf_op jit(solution)/shard_map/dot_general | solution.py:60
  229.2 3.5 convolution_convert_fusion.2
  239.8 5.8 %gated_backward.1 = (f32[448,1536]{1,0:T(8,128)S(1)}, bf16[448,1536]{1,0:T(8,128)(2,1)S(1)}, f32[2,1,1536]{2,1,0:T(1,128)S(1)}, bf16[2,128,1536]{2,1,0:T(8,128)(2,1)S(1)}) custom-call(f32[448,1536]{1,0:T(8,128)} %pad_maximum_fusion.1.gg_ref, f32[448,1536]{1,0:T(8,128)} %copy-done, f32[448,1536]{1,0:T(8,128)} %fusion.116.z_ref, ...), custom_call_target="tpu_custom_call" | custom-call | flops 196804608 | bytes 13762560 | tf_op jit(solution)/shard_map/gated_backward/pallas_call | solution.py:626
  248.0 5.9 %all-to-all-start.3 = ((bf16[8,2,16,1536]{3,2,1,0:T(8,128)(2,1)}), bf16[8,2,16,1536]{3,2,1,0:T(8,128)(2,1)S(1)}, u32[]{:S(2)}, u32[]{:S(2)}) async-start(bf16[8,2,16,1536]{3,2,1,0:T(8,128)(2,1)} %bitcast.189), calls=%async_computation.3 | async-start | bytes 1572864 | tf_op jit(solution)/shard_map/all_to_all | solution.py:534
  254.0 3.3 constant_dynamic-update-slice_fusion.15
  279.6 6.4 %all-to-all-start.4 = ((bf16[8,2,16,1536]{3,2,1,0:T(8,128)(2,1)}), bf16[8,2,16,1536]{3,2,1,0:T(8,128)(2,1)S(1)}, u32[]{:S(2)}, u32[]{:S(2)}) async-start(bf16[8,2,16,1536]{3,2,1,0:T(8,128)(2,1)} %bitcast.39), calls=%async_computation.4 | async-start | bytes 1572864 | tf_op jit(solution)/shard_map/all_to_all | solution.py:539
  286.0 5.4 convolution_add_fusion.1
  292.4 34.5 %attn_backward.1 = (bf16[448,512]{1,0:T(8,128)(2,1)}, bf16[16,224,256]{2,1,0:T(8,128)(2,1)}) custom-call(s32[4,17]{1,0:T(4,128)} %copy-done.15, bf16[2,2,64,896]{3,2,1,0:T(8,128)(2,1)} %copy-done.16, bf16[16,224,256]{2,1,0:T(8,128)(2,1)} %bitcast.181, bf16[448,512]{1,0:T(8,128)(2,1)} %pad_maximum_fusion.12.do_ref, f32[2,2,64,896]{3,2,1,0:T(8,128)} %copy-done.18, ...), custom_call_target="tpu_custom_call" | custom-call | flops 4367319040 | bytes 16777216 | tf_op jit(solution)/shard_map/attn_backward/pallas_call | solution.py:387
  330.1 16.7 %scan_backward.1 = (f32[448,1792]{1,0:T(8,128)}, f32[2,224,24]{2,1,0:T(8,128)}, f32[2,224,24]{2,1,0:T(8,128)}, f32[2,1,1536]{2,1,0:T(1,128)}, f32[2,1,1536]{2,1,0:T(1,128)}) custom-call(f32[448,1792]{1,0:T(8,128)} %pad_maximum_fusion.m_ref.c_ref, f32[448,1536]{1,0:T(8,128)} %copy-done.5, f32[448,1536]{1,0:T(8,128)} %copy-done, f32[2,224,24]{2,1,0:T(8,128)} %bitcast.176, ...), custom_call_target="tpu_custom_call" | custom-call | flops 1849688064 | bytes 13762560 | tf_op jit(solution)/shard_map/scan_backward/pallas_call | solution.py:744
  349.8 7.0 %multiply_reduce_fusion.10 = (f32[1792]{0:T(1024)S(1)}, f32[1792]{0:T(1024)S(1)}, f32[1792]{0:T(1024)S(1)}, f32[1792]{0:T(1024)S(1)}, f32[1792]{0:T(1024)S(1)}, ...) fusion(f32[448,1816]{1,0:T(8,128)} %copy-done.31, ...), kind=kLoop, calls=%fused_computation.81 | loop fusion | flops 16841216 | bytes 16171008 | tf_op jit(solution)/shard_map/transpose(jvp())/reduce_sum | solution.py:798
  366.5 21.2 %collective-permute-done.12 = bf16[4,448,256]{2,1,0:T(8,128)(2,1)} collective-permute-done((bf16[4,448,256]{2,1,0:T(8,128)(2,1)}, bf16[4,448,256]{2,1,0:T(8,128)(2,1)}, u32[]{:S(2)}, u32[]{:S(2)}) %collective-permute-start.12) | collective-permute-done | bytes 917536 | tf_op jit(solution)/shard_map/ppermute | solution.py:37
  387.7 4.1 collective-permute-start.14
  395.7 3.4 collective-permute-start.15
  399.1 2.9 collective-permute-start.16
  405.7 2.6 pad_maximum_fusion.5
  408.9 11.5 %collective-permute-done.16 = bf16[448,256]{1,0:T(8,128)(2,1)} collective-permute-done((bf16[448,256]{1,0:T(8,128)(2,1)}, bf16[448,256]{1,0:T(8,128)(2,1)}, u32[]{:S(2)}, u32[]{:S(2)}) %collective-permute-start.16) | collective-permute-done | bytes 229408 | tf_op jit(solution)/shard_map/ppermute | solution.py:37
  424.4 4.9 concatenate.150
  429.3 5.4 convolution_convert_fusion
  445.6 3.2 fusion.16
  449.0 3.3 fusion
  453.1 11.0 %collective-permute-start.22 = (bf16[2,2,32,2688]{3,2,1,0:T(8,128)(2,1)S(1)}, bf16[2,2,32,2688]{3,2,1,0:T(8,128)(2,1)S(1)}, u32[]{:S(2)}, u32[]{:S(2)}) collective-permute-start(bf16[2,2,32,2688]{3,2,1,0:T(8,128)(2,1)S(1)} %bitcast.205), channel_id=1, source_target_pairs={{0,4},{4,0},{8,12},{12,8},{16,20},{20,16},{24,28},{28,24},{1,5},{5... | collective-permute-start | bytes 2064392 | tf_op jit(solution)/shard_map/ppermute | solution.py:37
  464.8 25.5 %collective-permute-done.19 = f32[104,128]{1,0:T(8,128)S(1)} collective-permute-done((f32[104,128]{1,0:T(8,128)S(1)}, f32[104,128]{1,0:T(8,128)S(1)}, u32[]{:S(2)}, u32[]{:S(2)}) %collective-permute-start.19) | collective-permute-done | bytes 53280 | tf_op jit(solution)/shard_map/ppermute | solution.py:37
  490.6 6.4 %collective-permute-start.24 = (bf16[2,32,2688]{2,1,0:T(8,128)(2,1)S(1)}, bf16[2,32,2688]{2,1,0:T(8,128)(2,1)S(1)}, u32[]{:S(2)}, u32[]{:S(2)}) collective-permute-start(bf16[2,32,2688]{2,1,0:T(8,128)(2,1)S(1)} %get-tuple-element.260), channel_id=1, source_target_pairs={{0,4},{4,0},{8,12},{12,8},{16,20},{20,16},{24,28},{28,24},{1,5},{5... | collective-permute-start | bytes 1032200 | tf_op jit(solution)/shard_map/ppermute | solution.py:37
  500.7 12.4 %collective-permute-done.23 = f32[104,128]{1,0:T(8,128)S(1)} collective-permute-done((f32[104,128]{1,0:T(8,128)S(1)}, f32[104,128]{1,0:T(8,128)S(1)}, u32[]{:S(2)}, u32[]{:S(2)}) %collective-permute-start.23) | collective-permute-done | bytes 53280 | tf_op jit(solution)/shard_map/ppermute | solution.py:37
  515.5 7.8 %collective-permute-start.26 = (f32[104,128]{1,0:T(8,128)S(1)}, f32[104,128]{1,0:T(8,128)S(1)}, u32[]{:S(2)}, u32[]{:S(2)}) collective-permute-start(f32[104,128]{1,0:T(8,128)S(1)} %add.392), channel_id=1, source_target_pairs={{0,8},{4,12},{8,0},{12,4},{16,24},{20,28},{24,16},{28,20},{1,9},{5... | collective-permute-start | bytes 159752 | tf_op jit(solution)/shard_map/ppermute | solution.py:37
  525.4 3.0 collective-permute-start.27
  530.2 2.9 collective-permute-start.28
  537.9 7.3 %collective-permute-done.29 = bf16[32,2688]{1,0:T(8,128)(2,1)S(1)} collective-permute-done((bf16[32,2688]{1,0:T(8,128)(2,1)S(1)}, bf16[32,2688]{1,0:T(8,128)(2,1)S(1)}, u32[]{:S(2)}, u32[]{:S(2)}) %collective-permute-start.29) | collective-permute-done | bytes 172064 | tf_op jit(solution)/shard_map/ppermute | solution.py:37
  (471 shorter events, 155.6 us)
Async XLA Ops:
  7.2 115.3 %all-gather.5.cloned.1.call-start = ((), (), s32[]{:S(2)}) async-start(), calls=%async_computation.6 | async-start | bytes 3932160 | tf_op jit(solution)/shard_map/all_gather | solution.py:84
  9.4 175.1 %all-gather.7.cloned.1.call-start = ((), (), s32[]{:S(2)}) async-start(), calls=%async_computation.7 | async-start | bytes 5242880 | tf_op jit(solution)/shard_map/all_gather | solution.py:84
  10.6 181.3 %all-gather.9.cloned.1.call-start = ((), (), s32[]{:S(2)}) async-start(), calls=%async_computation.8 | async-start | bytes 10485760 | tf_op jit(solution)/shard_map/all_gather | solution.py:84
  11.3 15.0 %collective-permute-start = (bf16[256,768]{1,0:T(8,128)(2,1)}, bf16[256,768]{1,0:T(8,128)(2,1)S(1)}, u32[]{:S(2)}, u32[]{:S(2)}) collective-permute-start(bf16[256,768]{1,0:T(8,128)(2,1)} %param.33), channel_id=1, source_target_pairs={{0,2},{1,3},{2,0},{3,1},{4,6},{5,7},{6,4},{7,5},{8,10},{9,11},{10,... | collective-permute-start | bytes 1179656 | tf_op jit(solution)/shard_map/ppermute | solution.py:37
  14.3 17.9 %collective-permute-start.6 = (bf16[256,768]{1,0:T(8,128)(2,1)}, bf16[256,768]{1,0:T(8,128)(2,1)}, u32[]{:S(2)}, u32[]{:S(2)}) collective-permute-start(bf16[256,768]{1,0:T(8,128)(2,1)} %param.33), channel_id=1, source_target_pairs={{0,1},{1,0},{2,3},{3,2},{4,5},{5,4},{6,7},{7,6},{8,9},{9,8},{10,11... | collective-permute-start | bytes 1179656 | tf_op jit(solution)/shard_map/ppermute | solution.py:37
  18.1 104.4 %copy-start.32 = (bf16[448,1024]{1,0:T(8,128)(2,1)}, bf16[448,1024]{1,0:T(8,128)(2,1)S(1)}, u32[]{:S(2)}) copy-start(bf16[448,1024]{1,0:T(8,128)(2,1)S(1)} %fusion.8) | copy-start | bytes 2752516
  18.5 43.0 %copy-start.7 = (f32[448,128]{1,0:T(8,128)}, f32[448,128]{1,0:T(8,128)S(1)}, u32[]{:S(2)}) copy-start(f32[448,128]{1,0:T(8,128)S(1)} %broadcast_multiply_fusion.8.sin_ref) | copy-start | bytes 688132
  26.3 34.2 %collective-permute-start.2 = (bf16[256,1816]{0,1:T(8,128)(2,1)S(1)}, bf16[256,1816]{0,1:T(8,128)(2,1)}, u32[]{:S(2)}, u32[]{:S(2)}) collective-permute-start(bf16[256,1816]{0,1:T(8,128)(2,1)S(1)} %slice.418), channel_id=1, source_target_pairs={{0,2},{1,3},{2,0},{3,1},{4,6},{5,7},{6,4},{7,5},{8,10},{9,11},{10,... | collective-permute-start | bytes 2789384 | tf_op jit(solution)/shard_map/ppermute | solution.py:37
  28.8 52.0 %copy-start.79 = (f32[1792]{0:T(1024)}, f32[1792]{0:T(1024)S(1)}, u32[]{:S(2)}) copy-start(f32[1792]{0:T(1024)S(1)} %get-tuple-element.182) | copy-start | bytes 21508
  28.8 52.0 %copy-start.81 = (f32[1792]{0:T(1024)}, f32[1792]{0:T(1024)S(1)}, u32[]{:S(2)}) copy-start(f32[1792]{0:T(1024)S(1)} %get-tuple-element.183) | copy-start | bytes 21508
  28.8 52.0 %copy-start.83 = (f32[1792]{0:T(1024)}, f32[1792]{0:T(1024)S(1)}, u32[]{:S(2)}) copy-start(f32[1792]{0:T(1024)S(1)} %get-tuple-element.184) | copy-start | bytes 21508
  29.1 73.4 %copy-start.13 = (f32[1,1536]{1,0:T(1,128)}, f32[1,1536]{1,0:T(1,128)S(1)}, u32[]{:S(2)}) copy-start(f32[1,1536]{1,0:T(1,128)S(1)} %broadcast_in_dim_reshape.3.skip_ref) | copy-start | bytes 18436
  31.6 36.0 %collective-permute-start.1 = (bf16[256,1816]{0,1:T(8,128)(2,1)S(1)}, bf16[256,1816]{0,1:T(8,128)(2,1)S(1)}, u32[]{:S(2)}, u32[]{:S(2)}) collective-permute-start(bf16[256,1816]{0,1:T(8,128)(2,1)S(1)} %slice.418), channel_id=1, source_target_pairs={{0,1},{1,0},{2,3},{3,2},{4,5},{5,4},{6,7},{7,6},{8,9},{9,8},{10,11... | collective-permute-start | bytes 2789384 | tf_op jit(solution)/shard_map/ppermute | solution.py:37
  31.7 28.9 %collective-permute-start.7 = (bf16[256,768]{1,0:T(8,128)(2,1)S(1)}, bf16[256,768]{1,0:T(8,128)(2,1)S(1)}, u32[]{:S(2)}, u32[]{:S(2)}) collective-permute-start(bf16[256,768]{1,0:T(8,128)(2,1)S(1)} %copy-done.69), channel_id=1, source_target_pairs={{0,1},{1,0},{2,3},{3,2},{4,5},{5,4},{6,7},{7,6},{8,9},{9,8},{10,11... | collective-permute-start | bytes 1179656 | tf_op jit(solution)/shard_map/ppermute | solution.py:37
  60.5 8.6 %collective-permute-start.3 = (bf16[256,1816]{0,1:T(8,128)(2,1)}, bf16[256,1816]{0,1:T(8,128)(2,1)S(1)}, u32[]{:S(2)}, u32[]{:S(2)}) collective-permute-start(bf16[256,1816]{0,1:T(8,128)(2,1)} %collective-permute-done.2), channel_id=1, source_target_pairs={{0,1},{1,0},{2,3},{3,2},{4,5},{5,4},{6,7},{7,6},{8,9},{9,8},{10,11... | collective-permute-start | bytes 2789384 | tf_op jit(solution)/shard_map/ppermute | solution.py:37
  63.1 22.9 %collective-permute-start.8 = (bf16[448,256]{1,0:T(8,128)(2,1)S(1)}, bf16[448,256]{1,0:T(8,128)(2,1)S(1)}, u32[]{:S(2)}, u32[]{:S(2)}) collective-permute-start(bf16[448,256]{1,0:T(8,128)(2,1)S(1)} %get-tuple-element.108), channel_id=1, source_target_pairs={{0,8},{4,12},{8,0},{12,4},{16,24},{20,28},{24,16},{28,20},{1,9},{5... | collective-permute-start | bytes 688136 | tf_op jit(solution)/shard_map/ppermute | solution.py:37
  65.0 21.1 %collective-permute-start.9 = (bf16[448,256]{1,0:T(8,128)(2,1)S(1)}, bf16[448,256]{1,0:T(8,128)(2,1)S(1)}, u32[]{:S(2)}, u32[]{:S(2)}) collective-permute-start(bf16[448,256]{1,0:T(8,128)(2,1)S(1)} %get-tuple-element.108), channel_id=1, source_target_pairs={{0,16},{4,20},{8,24},{12,28},{16,0},{20,4},{24,8},{28,12},{1,17},{... | collective-permute-start | bytes 688136 | tf_op jit(solution)/shard_map/ppermute | solution.py:37
  67.6 18.5 %collective-permute-start.10 = (bf16[448,256]{1,0:T(8,128)(2,1)S(1)}, bf16[448,256]{1,0:T(8,128)(2,1)S(1)}, u32[]{:S(2)}, u32[]{:S(2)}) collective-permute-start(bf16[448,256]{1,0:T(8,128)(2,1)S(1)} %get-tuple-element.108), channel_id=1, source_target_pairs={{0,24},{4,28},{8,16},{12,20},{16,8},{20,12},{24,0},{28,4},{1,25},{... | collective-permute-start | bytes 688136 | tf_op jit(solution)/shard_map/ppermute | solution.py:37
  71.4 5.2 collective-permute-start.4
  75.1 5.6 %collective-permute-start.5 = (bf16[3,1792]{1,0:T(4,128)(2,1)S(1)}, bf16[3,1792]{1,0:T(4,128)(2,1)S(1)}, u32[]{:S(2)}, u32[]{:S(2)}) collective-permute-start(bf16[3,1792]{1,0:T(4,128)(2,1)S(1)} %get-tuple-element.206), channel_id=1, source_target_pairs={{4,0},{8,4},{12,8},{16,12},{20,16},{24,20},{28,24},{5,1},{9,5},{13... | collective-permute-start | bytes 32264 | tf_op jit(solution)/shard_map/ppermute | solution.py:68
  87.1 25.5 %collective-permute-start.11 = (bf16[4,448,256]{2,1,0:T(8,128)(2,1)}, bf16[4,448,256]{2,1,0:T(8,128)(2,1)}, u32[]{:S(2)}, u32[]{:S(2)}) collective-permute-start(bf16[4,448,256]{2,1,0:T(8,128)(2,1)} %get-tuple-element.246), channel_id=1, source_target_pairs={{0,4},{4,0},{8,12},{12,8},{16,20},{20,16},{24,28},{28,24},{1,5},{5... | collective-permute-start | bytes 2752520 | tf_op jit(solution)/shard_map/ppermute | solution.py:37
  92.7 147.1 %copy-start.2 = (f32[2,24,224]{1,2,0:T(8,128)}, f32[2,24,224]{1,2,0:T(8,128)S(1)}, u32[]{:S(2)}) copy-start(f32[2,24,224]{1,2,0:T(8,128)S(1)} %copy.83) | copy-start | bytes 129028
  93.4 20.2 %all-to-all-start.1 = ((f32[8,2,24]{2,1,0:T(2,128)}), f32[8,2,24]{2,1,0:T(2,128)S(1)}, u32[]{:S(2)}, u32[]{:S(2)}) async-start(f32[8,2,24]{2,1,0:T(2,128)} %broadcast_in_dim.43), calls=%async_computation.1 | async-start | bytes 16384 | tf_op jit(solution)/shard_map/all_to_all | solution.py:911
  113.6 26.7 %all-to-all-start = ((bf16[8,2,16,1536]{3,2,1,0:T(8,128)(2,1)}), bf16[8,2,16,1536]{3,2,1,0:T(8,128)(2,1)S(1)}, u32[]{:S(2)}, u32[]{:S(2)}) async-start(bf16[8,2,16,1536]{3,2,1,0:T(8,128)(2,1)} %bitcast.192), calls=%async_computation | async-start | bytes 1572864 | tf_op jit(solution)/shard_map/all_to_all | solution.py:534
  121.7 80.9 %all-gather.11.cloned.1.call-start = ((), (), s32[]{:S(2)}) async-start(), calls=%async_computation.9 | async-start | bytes 5242880 | tf_op jit(solution)/shard_map/all_gather | solution.py:84
  142.0 28.8 %all-to-all-start.2 = ((bf16[8,2,16,1536]{3,2,1,0:T(8,128)(2,1)}), bf16[8,2,16,1536]{3,2,1,0:T(8,128)(2,1)S(1)}, u32[]{:S(2)}, u32[]{:S(2)}) async-start(bf16[8,2,16,1536]{3,2,1,0:T(8,128)(2,1)} %bitcast.17), calls=%async_computation.2 | async-start | bytes 1572864 | tf_op jit(solution)/shard_map/all_to_all | solution.py:539
  248.0 29.7 %all-to-all-start.3 = ((bf16[8,2,16,1536]{3,2,1,0:T(8,128)(2,1)}), bf16[8,2,16,1536]{3,2,1,0:T(8,128)(2,1)S(1)}, u32[]{:S(2)}, u32[]{:S(2)}) async-start(bf16[8,2,16,1536]{3,2,1,0:T(8,128)(2,1)} %bitcast.189), calls=%async_computation.3 | async-start | bytes 1572864 | tf_op jit(solution)/shard_map/all_to_all | solution.py:534
  253.9 292.1 %reduce-scatter.2.cloned.1.call-start = ((), (), s32[]{:S(2)}) async-start(), calls=%async_computation.10 | async-start | bytes 20545536 | tf_op jit(solution)/shard_map/reduce_scatter | solution.py:102
  279.6 47.3 %all-to-all-start.4 = ((bf16[8,2,16,1536]{3,2,1,0:T(8,128)(2,1)}), bf16[8,2,16,1536]{3,2,1,0:T(8,128)(2,1)S(1)}, u32[]{:S(2)}, u32[]{:S(2)}) async-start(bf16[8,2,16,1536]{3,2,1,0:T(8,128)(2,1)} %bitcast.39), calls=%async_computation.4 | async-start | bytes 1572864 | tf_op jit(solution)/shard_map/all_to_all | solution.py:539
  347.8 39.9 %collective-permute-start.12 = (bf16[4,448,256]{2,1,0:T(8,128)(2,1)}, bf16[4,448,256]{2,1,0:T(8,128)(2,1)}, u32[]{:S(2)}, u32[]{:S(2)}) collective-permute-start(bf16[4,448,256]{2,1,0:T(8,128)(2,1)} %slice_bitcast_fusion.1), channel_id=1, source_target_pairs={{0,4},{4,0},{8,12},{12,8},{16,20},{20,16},{24,28},{28,24},{1,5},{5... | collective-permute-start | bytes 2752520 | tf_op jit(solution)/shard_map/ppermute | solution.py:37
  387.7 14.3 %collective-permute-start.14 = (bf16[3,1792]{1,0:T(4,128)(2,1)S(1)}, bf16[3,1792]{1,0:T(4,128)(2,1)S(1)}, u32[]{:S(2)}, u32[]{:S(2)}) collective-permute-start(bf16[3,1792]{1,0:T(4,128)(2,1)S(1)} %get-tuple-element.287), channel_id=1, source_target_pairs={{0,4},{4,8},{8,12},{12,16},{16,20},{20,24},{24,28},{1,5},{5,9},{9,... | collective-permute-start | bytes 32264 | tf_op jit(solution)/shard_map/ppermute | solution.py:67
  391.8 11.7 %collective-permute-start.13 = (bf16[3,1792]{1,0:T(4,128)(2,1)S(1)}, bf16[3,1792]{1,0:T(4,128)(2,1)S(1)}, u32[]{:S(2)}, u32[]{:S(2)}) collective-permute-start(bf16[3,1792]{1,0:T(4,128)(2,1)S(1)} %get-tuple-element.286), channel_id=1, source_target_pairs={{4,0},{8,4},{12,8},{16,12},{20,16},{24,20},{28,24},{5,1},{9,5},{13... | collective-permute-start | bytes 32264 | tf_op jit(solution)/shard_map/ppermute | solution.py:68
  395.7 13.2 %collective-permute-start.15 = (bf16[448,256]{1,0:T(8,128)(2,1)}, bf16[448,256]{1,0:T(8,128)(2,1)}, u32[]{:S(2)}, u32[]{:S(2)}) collective-permute-start(bf16[448,256]{1,0:T(8,128)(2,1)} %get-tuple-element.239), channel_id=1, source_target_pairs={{0,8},{4,12},{8,0},{12,4},{16,24},{20,28},{24,16},{28,20},{1,9},{5... | collective-permute-start | bytes 688136 | tf_op jit(solution)/shard_map/ppermute | solution.py:37
  399.1 21.3 %collective-permute-start.16 = (bf16[448,256]{1,0:T(8,128)(2,1)}, bf16[448,256]{1,0:T(8,128)(2,1)}, u32[]{:S(2)}, u32[]{:S(2)}) collective-permute-start(bf16[448,256]{1,0:T(8,128)(2,1)} %get-tuple-element.238), channel_id=1, source_target_pairs={{0,16},{4,20},{8,24},{12,28},{16,0},{20,4},{24,8},{28,12},{1,17},{... | collective-permute-start | bytes 688136 | tf_op jit(solution)/shard_map/ppermute | solution.py:37
  402.1 20.0 %collective-permute-start.17 = (bf16[448,256]{1,0:T(8,128)(2,1)}, bf16[448,256]{1,0:T(8,128)(2,1)}, u32[]{:S(2)}, u32[]{:S(2)}) collective-permute-start(bf16[448,256]{1,0:T(8,128)(2,1)} %get-tuple-element.237), channel_id=1, source_target_pairs={{0,24},{4,28},{8,16},{12,20},{16,8},{20,12},{24,0},{28,4},{1,25},{... | collective-permute-start | bytes 688136 | tf_op jit(solution)/shard_map/ppermute | solution.py:37
  438.4 10.6 %collective-permute-start.20 = (bf16[4,2,2,32,2688]{4,3,1,0,2:T(8,128)(2,1)}, bf16[4,2,2,32,2688]{4,3,1,0,2:T(8,128)(2,1)}, u32[]{:S(2)}, u32[]{:S(2)}) collective-permute-start(bf16[4,2,2,32,2688]{4,3,1,0,2:T(8,128)(2,1)} %bitcast.162), channel_id=1, source_target_pairs={{0,1},{1,0},{2,3},{3,2},{4,5},{5,4},{6,7},{7,6},{8,9},{9,8},{10,11... | collective-permute-start | bytes 8257544 | tf_op jit(solution)/shard_map/ppermute | solution.py:37
  449.0 15.1 %collective-permute-start.18 = (f32[104,128]{1,0:T(8,128)S(1)}, f32[104,128]{1,0:T(8,128)S(1)}, u32[]{:S(2)}, u32[]{:S(2)}) collective-permute-start(f32[104,128]{1,0:T(8,128)S(1)} %pad_bitcast_fusion), channel_id=1, source_target_pairs={{0,1},{1,0},{2,3},{3,2},{4,5},{5,4},{6,7},{7,6},{8,9},{9,8},{10,11... | collective-permute-start | bytes 159752 | tf_op jit(solution)/shard_map/ppermute | solution.py:37
  452.7 37.6 %collective-permute-start.21 = (bf16[2,2,32,2688]{3,2,1,0:T(8,128)(2,1)S(1)}, bf16[2,2,32,2688]{3,2,1,0:T(8,128)(2,1)S(1)}, u32[]{:S(2)}, u32[]{:S(2)}) collective-permute-start(bf16[2,2,32,2688]{3,2,1,0:T(8,128)(2,1)S(1)} %get-tuple-element.233), channel_id=1, source_target_pairs={{0,2},{1,3},{2,0},{3,1},{4,6},{5,7},{6,4},{7,5},{8,10},{9,11},{10,... | collective-permute-start | bytes 2064392 | tf_op jit(solution)/shard_map/ppermute | solution.py:37
  453.1 37.2 %collective-permute-start.22 = (bf16[2,2,32,2688]{3,2,1,0:T(8,128)(2,1)S(1)}, bf16[2,2,32,2688]{3,2,1,0:T(8,128)(2,1)S(1)}, u32[]{:S(2)}, u32[]{:S(2)}) collective-permute-start(bf16[2,2,32,2688]{3,2,1,0:T(8,128)(2,1)S(1)} %bitcast.205), channel_id=1, source_target_pairs={{0,4},{4,0},{8,12},{12,8},{16,20},{20,16},{24,28},{28,24},{1,5},{5... | collective-permute-start | bytes 2064392 | tf_op jit(solution)/shard_map/ppermute | solution.py:37
  464.1 26.2 %collective-permute-start.19 = (f32[104,128]{1,0:T(8,128)S(1)}, f32[104,128]{1,0:T(8,128)S(1)}, u32[]{:S(2)}, u32[]{:S(2)}) collective-permute-start(f32[104,128]{1,0:T(8,128)S(1)} %fusion.91), channel_id=1, source_target_pairs={{0,2},{1,3},{2,0},{3,1},{4,6},{5,7},{6,4},{7,5},{8,10},{9,11},{10,... | collective-permute-start | bytes 159752 | tf_op jit(solution)/shard_map/ppermute | solution.py:37
  490.6 22.6 %collective-permute-start.24 = (bf16[2,32,2688]{2,1,0:T(8,128)(2,1)S(1)}, bf16[2,32,2688]{2,1,0:T(8,128)(2,1)S(1)}, u32[]{:S(2)}, u32[]{:S(2)}) collective-permute-start(bf16[2,32,2688]{2,1,0:T(8,128)(2,1)S(1)} %get-tuple-element.260), channel_id=1, source_target_pairs={{0,4},{4,0},{8,12},{12,8},{16,20},{20,16},{24,28},{28,24},{1,5},{5... | collective-permute-start | bytes 1032200 | tf_op jit(solution)/shard_map/ppermute | solution.py:37
  497.3 18.2 %collective-permute-start.25 = (bf16[2,32,2688]{2,1,0:T(8,128)(2,1)S(1)}, bf16[2,32,2688]{2,1,0:T(8,128)(2,1)S(1)}, u32[]{:S(2)}, u32[]{:S(2)}) collective-permute-start(bf16[2,32,2688]{2,1,0:T(8,128)(2,1)S(1)} %get-tuple-element.258), channel_id=1, source_target_pairs={{0,2},{1,3},{2,0},{3,1},{4,6},{5,7},{6,4},{7,5},{8,10},{9,11},{10,... | collective-permute-start | bytes 1032200 | tf_op jit(solution)/shard_map/ppermute | solution.py:37
  499.3 13.9 %collective-permute-start.23 = (f32[104,128]{1,0:T(8,128)S(1)}, f32[104,128]{1,0:T(8,128)S(1)}, u32[]{:S(2)}, u32[]{:S(2)}) collective-permute-start(f32[104,128]{1,0:T(8,128)S(1)} %fusion.147), channel_id=1, source_target_pairs={{0,4},{4,0},{8,12},{12,8},{16,20},{20,16},{24,28},{28,24},{1,5},{5... | collective-permute-start | bytes 159752 | tf_op jit(solution)/shard_map/ppermute | solution.py:37
  515.5 9.9 %collective-permute-start.26 = (f32[104,128]{1,0:T(8,128)S(1)}, f32[104,128]{1,0:T(8,128)S(1)}, u32[]{:S(2)}, u32[]{:S(2)}) collective-permute-start(f32[104,128]{1,0:T(8,128)S(1)} %add.392), channel_id=1, source_target_pairs={{0,8},{4,12},{8,0},{12,4},{16,24},{20,28},{24,16},{28,20},{1,9},{5... | collective-permute-start | bytes 159752 | tf_op jit(solution)/shard_map/ppermute | solution.py:37
  525.4 7.7 %collective-permute-start.27 = (f32[104,128]{1,0:T(8,128)S(1)}, f32[104,128]{1,0:T(8,128)S(1)}, u32[]{:S(2)}, u32[]{:S(2)}) collective-permute-start(f32[104,128]{1,0:T(8,128)S(1)} %add.395), channel_id=1, source_target_pairs={{0,16},{4,20},{8,24},{12,28},{16,0},{20,4},{24,8},{28,12},{1,17},{... | collective-permute-start | bytes 159752 | tf_op jit(solution)/shard_map/ppermute | solution.py:37
  528.6 9.2 %collective-permute-start.30 = (bf16[32,2688]{1,0:T(8,128)(2,1)S(1)}, bf16[32,2688]{1,0:T(8,128)(2,1)S(1)}, u32[]{:S(2)}, u32[]{:S(2)}) collective-permute-start(bf16[32,2688]{1,0:T(8,128)(2,1)S(1)} %get-tuple-element.257), channel_id=1, source_target_pairs={{0,24},{4,28},{8,16},{12,20},{16,8},{20,12},{24,0},{28,4},{1,25},{... | collective-permute-start | bytes 516104 | tf_op jit(solution)/shard_map/ppermute | solution.py:37
  530.2 15.0 %collective-permute-start.29 = (bf16[32,2688]{1,0:T(8,128)(2,1)S(1)}, bf16[32,2688]{1,0:T(8,128)(2,1)S(1)}, u32[]{:S(2)}, u32[]{:S(2)}) collective-permute-start(bf16[32,2688]{1,0:T(8,128)(2,1)S(1)} %get-tuple-element.256), channel_id=1, source_target_pairs={{0,16},{4,20},{8,24},{12,28},{16,0},{20,4},{24,8},{28,12},{1,17},{... | collective-permute-start | bytes 516104 | tf_op jit(solution)/shard_map/ppermute | solution.py:37
  530.2 15.0 %collective-permute-start.28 = (bf16[32,2688]{1,0:T(8,128)(2,1)S(1)}, bf16[32,2688]{1,0:T(8,128)(2,1)S(1)}, u32[]{:S(2)}, u32[]{:S(2)}) collective-permute-start(bf16[32,2688]{1,0:T(8,128)(2,1)S(1)} %get-tuple-element.255), channel_id=1, source_target_pairs={{0,8},{4,12},{8,0},{12,4},{16,24},{20,28},{24,16},{28,20},{1,9},{5... | collective-permute-start | bytes 516104 | tf_op jit(solution)/shard_map/ppermute | solution.py:37
  (101 other events, 690.4 us)
Sparse Core Ops, SparseCore 0:
  10.2 45.3 all-gather.4
  57.1 35.6 all-gather.6
  94.3 58.2 all-gather.8
  154.1 34.5 all-gather.10
  277.8 241.0 reduce-scatter.1

commit v3 on v2

--- a/solution.py
+++ b/solution.py
@@ -133,12 +133,26 @@
     )
 
 
-def sum_core(views):
+def send_core(view):
     core = lax.axis_index("fsdp") % 2
-    keep, send = (
-        jnp.concatenate([pick(view, side, 3) for view in views], axis=3) for side in (core, 1 - core)
-    )
-    return (keep.astype(f32) + swap(send, "fsdp", 1).astype(f32)).astype(bf16)
+    return pick(view, core, 3), swap(pick(view, 1 - core, 3), "fsdp", 1)
+
+
+def first_terms(terms):
+    parts = add_up(terms).astype(bf16)
+    half = parts.shape[0] // 2
+    low = exchange(parts[:half], 2, "fsdp", 2, parts.shape[2])
+    return low + exchange(parts[half:], 1, "ctx", 1, 2)
+
+
+def second_terms(terms):
+    low, high = (add_up(part).astype(bf16) for part in (terms[:-2], terms[-2:]))
+    return exchange(low, 1, "ctx", 1, 2) + exchange(high, 1, "fsdp", 2, high.shape[1])
+
+
+def last_terms(terms):
+    both = jnp.concatenate([add_up(part).astype(bf16) for part in (terms[:2], terms[2:])], axis=0)
+    return exchange(both, 0, "ctx", 2, both.shape[0])
 
 
 def tie(*arrays):
@@ -150,20 +164,6 @@
         array = array + swap(array, axis, distance)
         distance *= 2
     return array
-
-
-def tail_sums(parts, small):
-    ctx_count, fs_count = lax.axis_size("ctx"), lax.axis_size("fsdp")
-    half, wide = parts.shape[0] // 2, fs_count // 2
-    low = exchange(parts[:half], 2, "fsdp", 2, wide)
-    high = exchange(parts[half:], 1, "ctx", 1, 2)
-    small, *terms = tie(all_sum(small, "fsdp", 1, fs_count), *low, *high)
-    low, high = (add_up(part).astype(bf16) for part in (terms[:wide], terms[wide:]))
-    low = exchange(low, 1, "ctx", 1, 2)
-    high = exchange(high, 1, "fsdp", 2, wide)
-    small, *terms = tie(all_sum(small, "ctx", 1, 2), *low, *high)
-    both = jnp.concatenate([add_up(part).astype(bf16) for part in (terms[:2], terms[2:])], axis=0)
-    return add_up(exchange(both, 0, "ctx", 2, ctx_count // 2)), all_sum(small, "ctx", 2, ctx_count)
 
 
 def pair_table(ctx_count, mine):
@@ -1001,17 +1001,25 @@
         mixed_grad[half_rows:]
     )
     backs = jnp.concatenate([prev_early_grad, prev_late_grad], axis=0)
-    backs, pairs_came = tie(backs.astype(bf16), pairs_came)
-    own_pairs = (d_pairs[:, 0].astype(f32) + pairs_came.astype(f32)).astype(bf16)
-    pair_terms = [own_pairs[0]] + [swap(own_pairs[k // 2], "ctx", k) for k in range(2, ctx_count, 2)]
-    before_g, after_g = edge_exchange(backs, lag_rows)
+    before_g, after_g = edge_exchange(backs.astype(bf16), lag_rows)
+    before_g, after_g, pairs_came = tie(before_g, after_g, pairs_came)
     early_tail_grad = after_g.astype(f32) + jnp.where(is_last, prev_late_grad, 0.0)
     late_tail_grad = before_g.astype(f32)
     raw_early_grad = raw_early_grad.at[half_rows - lag_rows :].add(early_tail_grad)
     raw_late_grad = raw_late_grad.at[half_rows - lag_rows :].add(late_tail_grad)
     raw_grad = jnp.concatenate([raw_early_grad, raw_late_grad], axis=0)
-    raw_grad, *pair_terms = tie(raw_grad.astype(bf16), *pair_terms)
-    pair_grad = sum(term.astype(f32) for term in pair_terms)
+    wide_grad = jnp.concatenate([raw_grad.astype(bf16), step_raw_grad.astype(bf16)], axis=1)
+    tail_width = CONV + MH
+    padded_grad = jnp.pad(wide_grad, ((0, 0), (0, -tail_width % 128)))
+
+    kept, came = send_core(rows_by_owner(row_contract(normed_one, padded_grad)))
+    own_pairs = (d_pairs[:, 0].astype(f32) + pairs_came.astype(f32)).astype(bf16)
+    pair_terms = [own_pairs[0]] + [swap(own_pairs[k // 2], "ctx", k) for k in range(2, ctx_count, 2)]
+    wide_terms = first_terms([kept, came])
+    count = len(pair_terms)
+    tied = tie(*pair_terms, *wide_terms)
+    pair_terms, wide_terms = tied[:count], tied[count:]
+    pair_grad = add_up(pair_terms)
     key_grad = pair_grad[:, :kv_width]
     quarter = HEAD_WIDTH // 2
     key_swapped = jnp.concatenate(
@@ -1021,14 +1029,11 @@
         [dq, (key_grad * cosine - key_swapped * sine).astype(bf16), pair_grad[:, kv_width:].astype(bf16)],
         axis=1,
     )
-    tail_width = CONV + MH
-    tail_grad = jnp.concatenate(
-        [raw_grad, step_raw_grad.astype(bf16), jnp.zeros((device_rows, -tail_width % 128), bf16), qkv_grad],
-        axis=1,
-    )
-    sum_3 = sum_core([rows_by_owner(row_contract(normed_one, tail_grad))])
+    kept, came = send_core(rows_by_owner(row_contract(normed_one, qkv_grad)))
+    wide_terms = second_terms(wide_terms)
+    came, *wide_terms = tie(came, *wide_terms)
     normed_one_grad = order_rows(
-        backward_product(qkv_grad, full_qkv) + backward_product(tail_grad[:, :tail_width], full_in)
+        backward_product(qkv_grad, full_qkv) + backward_product(wide_grad, full_in)
     ) + backward_product(z_grad, full_gate_in)
     grad_mixer = jnp.sum(normed_one_grad * hidden * scale_one, axis=0)
     input_grad = resid_grad + norm_backward(normed_one_grad * mixer_gain, hidden, scale_one)
@@ -1046,8 +1051,13 @@
     flat = jnp.concatenate(small)
     size = flat.shape[0]
     flat = jnp.pad(flat, (0, -size % 1024)).reshape(-1, 128)
-    sum_3, flat = tail_sums(sum_3, flat)
-    flat = flat.reshape(-1)
+    wide_terms, qkv_terms = last_terms(wide_terms), first_terms([kept, came])
+    count = len(wide_terms)
+    flat, *tied = tie(all_sum(flat, "fsdp", 1, lax.axis_size("fsdp")), *wide_terms, *qkv_terms)
+    grad_wide, qkv_terms = add_up(tied[:count]), second_terms(tied[count:])
+    flat, *qkv_terms = tie(all_sum(flat, "ctx", 1, 2), *qkv_terms)
+    grad_qkv = add_up(last_terms(qkv_terms))
+    flat = all_sum(flat, "ctx", 2, ctx_count).reshape(-1)
     pieces, start = [], 0
     for view in views:
         pieces.append(sums[start : start + view.shape[4]])
@@ -1055,8 +1065,7 @@
     grad_gu = jnp.concatenate(pieces[: len(gu_parts)], axis=1)
     grad_down, grad_out, grad_o, grad_z, z_rest = pieces[len(gu_parts) :]
     z_rest = jnp.concatenate([z_rest[:, : d_model // 2], z_rest[:, d_model // 2 :]], axis=0)
-    grad_in = jnp.concatenate([grad_z, z_rest, sum_3[:, :tail_width]], axis=1)
-    grad_qkv = sum_3[:, tail_width + -tail_width % 128 :]
+    grad_in = jnp.concatenate([grad_z, z_rest, grad_wide[:, :tail_width]], axis=1)
     sums, start = [], 0
     for piece in small:
         sums.append(flat[start : start + piece.shape[0]])

time: 566 us -> 546 us (0.965)
  starting transfers between devices: 102 us -> 95.1 us
    ppermute x27 -> x35, starting transfers between devices: 58.2 us -> 51.6 us  [swap(): return lax.ppermute(array, axis, xor_pairs(lax.axis_size(axis), distance))]
    ppermute x27 -> x35, waiting for transfers between devices: 121 us -> 118 us  [swap(): return lax.ppermute(array, axis, xor_pairs(lax.axis_size(axis), distance))]
    unnamed x237 -> x257, local copies, waits for them, and re-layouts: 42.9 us -> 44.6 us
    dot_general x10 -> x11, matrix products: 25.6 us -> 24.6 us  [row_contract(): lax.dot_general(left, right, (((0,), (0,)), ((), ())), preferred_element_...]
  transfers between devices with their start and end apart: 41 -> 49, of which waited for: 15 -> 20; matrix products, arithmetic and copies ran while one was open for 26% -> 24% of each run, Pallas kernels for 16% -> 16%
where the time goes in v3:
time: 546 us; the launch traced here: 536 us
  waiting for transfers between devices  136 us (25%)
  starting transfers between devices  95.1 us (17%)
  Pallas kernels  93.9 us (17%)
  local copies, waits for them, and re-layouts  76.1 us (14%)
  matrix products  74.5 us (14%)
  other arithmetic  43.5 us (8%)
  between operations  17 us (3%)
    ppermute x35, waiting for transfers between devices, swap(): return lax.ppermute(array, axis, xor_pairs(lax.axis_size(axis), distance))  118 us
    ppermute x35, starting transfers between devices, swap(): return lax.ppermute(array, axis, xor_pairs(lax.axis_size(axis), distance))  51.6 us
    unnamed x257, local copies, waits for them, and re-layouts  44.6 us
    pallas_call x1, Pallas kernels, attn_backward(): pl.pallas_call(attn_backward_kernel, grid_spec=pltpu.PrefetchScalarGridSp...  34.5 us
    dot_general x6, matrix products, matmul(): return jnp.dot(left, right, preferred_element_type=f32)  25.9 us
    dot_general x11, matrix products, row_contract(): lax.dot_general(left, right, (((0,), (0,)), ((), ())), preferred_element_...  24.6 us
    dot_general x6, matrix products, backward_product(): lax.dot_general(grad_rows, weight, (((1,), (1,)), ((), ())), preferred_el...  23.1 us
    pallas_call x1, Pallas kernels, attn_forward(): pl.pallas_call(attn_forward_kernel, grid_spec=pltpu.PrefetchScalarGridSpe...  20 us
  transfers between devices with their start and end apart: 49, of which 20 were waited for; matrix products, arithmetic and copies ran while one was open for 24% of the time, Pallas kernels for 16%

profile of v3, /device:TPU:0, one launch (start us, length us, event | category | flops | bytes accessed | tf_op | source)
XLA Modules:
  0.0 536.1 jit_solution(8439036987302323059)
XLA Ops:
  11.3 3.0 collective-permute-start
  19.7 6.6 %collective-permute-done = bf16[256,768]{1,0:T(8,128)(2,1)S(1)} collective-permute-done((bf16[256,768]{1,0:T(8,128)(2,1)}, bf16[256,768]{1,0:T(8,128)(2,1)S(1)}, u32[]{:S(2)}, u32[]{:S(2)}) %collective-permute-start) | collective-permute-done | bytes 393248 | tf_op jit(solution)/shard_map/ppermute | solution.py:37
  33.4 27.2 %collective-permute-done.2 = bf16[256,1816]{0,1:T(8,128)(2,1)} collective-permute-done((bf16[256,1816]{0,1:T(8,128)(2,1)S(1)}, bf16[256,1816]{0,1:T(8,128)(2,1)}, u32[]{:S(2)}, u32[]{:S(2)}) %collective-permute-start.2) | collective-permute-done | bytes 929824 | tf_op jit(solution)/shard_map/ppermute | solution.py:37
  64.9 2.6 collective-permute-start.9
  71.4 3.7 collective-permute-start.4
  76.7 4.0 collective-permute-done.5
  80.8 3.3 fusion.29
  87.1 4.7 collective-permute-start.11
  93.3 9.1 %all-to-all-start.1 = ((f32[8,2,24]{2,1,0:T(2,128)}), f32[8,2,24]{2,1,0:T(2,128)S(1)}, u32[]{:S(2)}, u32[]{:S(2)}) async-start(f32[8,2,24]{2,1,0:T(2,128)} %broadcast_in_dim.41), calls=%async_computation.1 | async-start | bytes 16384 | tf_op jit(solution)/shard_map/all_to_all | solution.py:911
  102.5 7.8 %scan_forward.1 = (f32[448,1536]{1,0:T(8,128)S(1)}, bf16[2,128,1536]{2,1,0:T(8,128)(2,1)S(1)}) custom-call(f32[448,1792]{1,0:T(8,128)} %pad_maximum_fusion.m_ref.c_ref, f32[2,224,24]{2,1,0:T(8,128)S(1)} %bitcast.205, f32[2,224,24]{2,1,0:T(8,128)S(1)} %bitcast.200, f32[2,24,224]{2,1,0:T(8,128)S(1)} %fusion.44.cumt_ref, ...), custom_call_target="tpu_custom_call" | custom-call | flops 616562688 | bytes 5505024 | tf_op jit(solution)/shard_map/scan_forward/pallas_call | solution.py:474
  113.5 8.1 %all-to-all-start = ((bf16[8,2,16,1536]{3,2,1,0:T(8,128)(2,1)}), bf16[8,2,16,1536]{3,2,1,0:T(8,128)(2,1)S(1)}, u32[]{:S(2)}, u32[]{:S(2)}) async-start(bf16[8,2,16,1536]{3,2,1,0:T(8,128)(2,1)} %bitcast.223), calls=%async_computation | async-start | bytes 1572864 | tf_op jit(solution)/shard_map/all_to_all | solution.py:534
  122.5 5.1 fusion.119.z_ref
  127.5 12.7 %all-to-all-done = bf16[8,2,16,1536]{3,2,1,0:T(8,128)(2,1)S(1)} async-done(((bf16[8,2,16,1536]{3,2,1,0:T(8,128)(2,1)}), bf16[8,2,16,1536]{3,2,1,0:T(8,128)(2,1)S(1)}, u32[]{:S(2)}, u32[]{:S(2)}) %all-to-all-start) | async-done | bytes 786464 | tf_op jit(solution)/shard_map/all_to_all | solution.py:534
  142.0 3.5 all-to-all-start.2
  149.2 20.0 %attn_forward.1 = (bf16[448,512]{1,0:T(8,128)(2,1)S(1)}, f32[2,2,64,896]{3,2,1,0:T(8,128)S(1)}, f32[2,2,1,896]{3,2,1,0:T(1,128)S(1)}) custom-call(s32[4,17]{1,0:T(4,128)S(1)} %pad_add_fusion.3.tab, bf16[2,2,64,896]{3,2,1,0:T(8,128)(2,1)S(1)} %copy-done.17, bf16[16,224,256]{2,1,0:T(8,128)(2,1)S(1)} %bitcast.210, s32[1,896]{1,0:T(1,128)S(1)} %broadcast_in_dim_tile.5.row_ref), custom_call_target="tpu_custom_call" | custom-call | flops 1746927616 | bytes 8388608 | tf_op jit(solution)/shard_map/attn_forward/pallas_call | solution.py:302
  172.8 4.4 gated_forward.1
  184.5 5.0 multiply_reduce_fusion.2
  191.8 10.7 %fusion.120 = f32[448,4096]{1,0:T(8,128)} fusion(bf16[448,1024]{1,0:T(8,128)(2,1)} %multiply_convert_fusion.3, bf16[1024,4096]{1,0:T(8,128)(2,1)} %all-gather.9.cloned.1.call-done), kind=kOutput, calls=%fused_computation.336 | convolution fusion | flops 3758096384 | bytes 16646144 | tf_op jit(solution)/shard_map/dot_general | solution.py:52
  202.6 8.8 %multiply_convert_fusion.1 = (bf16[448,2048]{1,0:T(8,128)(2,1)S(1)}, bf16[448,2048]{1,0:T(8,128)(2,1)S(1)}, bf16[448,2048]{1,0:T(8,128)(2,1)}) fusion(f32[448,4096]{1,0:T(8,128)} %fusion.120, bf16[2048,1024]{1,0:T(8,128)(2,1)} %all-gather.11.cloned.1.call-done, bf16[224,1024]{1,0:T(8,128)(2,1)S(1)} %copy-done.60, bf16[224,1024]{1,0:T(8,128)(2,1)S(1)} %copy-done.58), kind=kOutput, calls=%fused_computation.10 | convolution fusion | flops 1894645760 | bytes 17956864 | tf_op jit(solution)/shard_map/dot_general | solution.py:60
  211.4 2.6 convolution_convert_fusion.7
  214.0 2.7 convolution_convert_fusion.6
  216.6 2.6 convolution_convert_fusion.5
  219.2 2.6 convolution_convert_fusion.4
  222.7 5.8 %multiply_reduce_fusion = (f32[1024]{0:T(1024)S(1)}, f32[448]{0:T(512)S(1)}, f32[448,1024]{1,0:T(8,128)S(1)}) fusion(f32[448,1024]{1,0:T(8,128)S(1)} %copy-done.40, f32[448]{0:T(512)S(1)} %add_rsqrt_fusion, f32[1024]{0:T(1024)S(1)} %copy-done.96, bf16[1024,4096]{1,0:T(8,128)(2,1)S(1)} %bitcast.246, bf16[448,2048]{1,0:T(8,128)(2,1)} %copy-done.113, ...), kind=kOutput, calls=%fused_computation.51 | convolution fusion | flops 3768187392 | bytes 15740416 | tf_op jit(solution)/shard_map/dot_general | solution.py:60
  229.2 3.5 convolution_convert_fusion.2
  239.7 5.8 %gated_backward.1 = (f32[448,1536]{1,0:T(8,128)S(1)}, bf16[448,1536]{1,0:T(8,128)(2,1)S(1)}, f32[2,1,1536]{2,1,0:T(1,128)S(1)}, bf16[2,128,1536]{2,1,0:T(8,128)(2,1)S(1)}) custom-call(f32[448,1536]{1,0:T(8,128)} %pad_maximum_fusion.1.gg_ref, f32[448,1536]{1,0:T(8,128)} %copy-done, f32[448,1536]{1,0:T(8,128)} %fusion.119.z_ref, ...), custom_call_target="tpu_custom_call" | custom-call | flops 196804608 | bytes 13762560 | tf_op jit(solution)/shard_map/gated_backward/pallas_call | solution.py:626
  247.9 5.9 %all-to-all-start.3 = ((bf16[8,2,16,1536]{3,2,1,0:T(8,128)(2,1)}), bf16[8,2,16,1536]{3,2,1,0:T(8,128)(2,1)S(1)}, u32[]{:S(2)}, u32[]{:S(2)}) async-start(bf16[8,2,16,1536]{3,2,1,0:T(8,128)(2,1)} %bitcast.221), calls=%async_computation.3 | async-start | bytes 1572864 | tf_op jit(solution)/shard_map/all_to_all | solution.py:534
  253.9 3.4 constant_dynamic-update-slice_fusion.15
  279.8 6.4 %all-to-all-start.4 = ((bf16[8,2,16,1536]{3,2,1,0:T(8,128)(2,1)}), bf16[8,2,16,1536]{3,2,1,0:T(8,128)(2,1)S(1)}, u32[]{:S(2)}, u32[]{:S(2)}) async-start(bf16[8,2,16,1536]{3,2,1,0:T(8,128)(2,1)} %bitcast.39), calls=%async_computation.4 | async-start | bytes 1572864 | tf_op jit(solution)/shard_map/all_to_all | solution.py:539
  286.4 34.5 %attn_backward.1 = (bf16[448,512]{1,0:T(8,128)(2,1)}, bf16[16,224,256]{2,1,0:T(8,128)(2,1)}) custom-call(s32[4,17]{1,0:T(4,128)} %copy-done.15, bf16[2,2,64,896]{3,2,1,0:T(8,128)(2,1)} %copy-done.16, bf16[16,224,256]{2,1,0:T(8,128)(2,1)} %bitcast.211, bf16[448,512]{1,0:T(8,128)(2,1)} %pad_maximum_fusion.13.do_ref, f32[2,2,64,896]{3,2,1,0:T(8,128)} %copy-done.18, ...), custom_call_target="tpu_custom_call" | custom-call | flops 4367319040 | bytes 16777216 | tf_op jit(solution)/shard_map/attn_backward/pallas_call | solution.py:387
  324.0 16.7 %scan_backward.1 = (f32[448,1792]{1,0:T(8,128)}, f32[2,224,24]{2,1,0:T(8,128)}, f32[2,224,24]{2,1,0:T(8,128)}, f32[2,1,1536]{2,1,0:T(1,128)}, f32[2,1,1536]{2,1,0:T(1,128)}) custom-call(f32[448,1792]{1,0:T(8,128)} %pad_maximum_fusion.m_ref.c_ref, f32[448,1536]{1,0:T(8,128)} %copy-done.5, f32[448,1536]{1,0:T(8,128)} %copy-done, f32[2,224,24]{2,1,0:T(8,128)} %bitcast.206, ...), custom_call_target="tpu_custom_call" | custom-call | flops 1849688064 | bytes 13762560 | tf_op jit(solution)/shard_map/scan_backward/pallas_call | solution.py:744
  341.7 6.7 %multiply_reduce_fusion.10 = (f32[1792]{0:T(1024)S(1)}, f32[1792]{0:T(1024)S(1)}, f32[1792]{0:T(1024)S(1)}, f32[1792]{0:T(1024)S(1)}, f32[1792]{0:T(1024)S(1)}, ...) fusion(f32[448,1816]{1,0:T(8,128)} %copy-done.28, ...), kind=kLoop, calls=%fused_computation.78 | loop fusion | flops 16841216 | bytes 16171008 | tf_op jit(solution)/shard_map/transpose(jvp())/reduce_sum | solution.py:798
  349.5 3.9 collective-permute-start.12
  355.3 2.7 collective-permute-start.14
  362.4 33.5 %collective-permute-done.14 = bf16[4,448,256]{2,1,0:T(8,128)(2,1)S(1)} collective-permute-done((bf16[4,448,256]{2,1,0:T(8,128)(2,1)S(1)}, bf16[4,448,256]{2,1,0:T(8,128)(2,1)S(1)}, u32[]{:S(2)}, u32[]{:S(2)}) %collective-permute-start.14) | collective-permute-done | bytes 917536 | tf_op jit(solution)/shard_map/ppermute | solution.py:37
  414.5 2.6 collective-permute-start.15
  429.8 4.6 collective-permute-done.16
  434.3 6.9 %collective-permute-done.17 = bf16[448,256]{1,0:T(8,128)(2,1)S(1)} collective-permute-done((bf16[448,256]{1,0:T(8,128)(2,1)S(1)}, bf16[448,256]{1,0:T(8,128)(2,1)S(1)}, u32[]{:S(2)}, u32[]{:S(2)}) %collective-permute-start.17) | collective-permute-done | bytes 229408 | tf_op jit(solution)/shard_map/ppermute | solution.py:37
  441.2 9.5 %collective-permute-done.19 = bf16[2,2,32,1920]{3,2,1,0:T(8,128)(2,1)S(1)} collective-permute-done((bf16[2,2,32,1920]{3,2,1,0:T(8,128)(2,1)S(1)}, bf16[2,2,32,1920]{3,2,1,0:T(8,128)(2,1)S(1)}, u32[]{:S(2)}, u32[]{:S(2)}) %collective-permute-start.19) | collective-permute-done | bytes 491552 | tf_op jit(solution)/shard_map/ppermute | solution.py:37
  456.5 3.2 fusion.16
  463.7 3.6 collective-permute-start.25
  469.7 6.2 %collective-permute-done.24 = bf16[2,32,1920]{2,1,0:T(8,128)(2,1)S(1)} collective-permute-done((bf16[2,32,1920]{2,1,0:T(8,128)(2,1)S(1)}, bf16[2,32,1920]{2,1,0:T(8,128)(2,1)S(1)}, u32[]{:S(2)}, u32[]{:S(2)}) %collective-permute-start.24) | collective-permute-done | bytes 245792 | tf_op jit(solution)/shard_map/ppermute | solution.py:37
  475.9 3.5 collective-permute-done.25
  479.8 3.0 collective-permute-start.27
  488.6 4.3 collective-permute-done.27
  493.8 4.3 collective-permute-done.29
  500.8 2.8 collective-permute-start.33
  516.2 2.5 collective-permute-done.37
  (515 shorter events, 172.9 us)
Async XLA Ops:
  7.2 115.3 %all-gather.5.cloned.1.call-start = ((), (), s32[]{:S(2)}) async-start(), calls=%async_computation.6 | async-start | bytes 3932160 | tf_op jit(solution)/shard_map/all_gather | solution.py:84
  9.4 175.1 %all-gather.7.cloned.1.call-start = ((), (), s32[]{:S(2)}) async-start(), calls=%async_computation.7 | async-start | bytes 5242880 | tf_op jit(solution)/shard_map/all_gather | solution.py:84
  10.6 181.3 %all-gather.9.cloned.1.call-start = ((), (), s32[]{:S(2)}) async-start(), calls=%async_computation.8 | async-start | bytes 10485760 | tf_op jit(solution)/shard_map/all_gather | solution.py:84
  11.3 15.0 %collective-permute-start = (bf16[256,768]{1,0:T(8,128)(2,1)}, bf16[256,768]{1,0:T(8,128)(2,1)S(1)}, u32[]{:S(2)}, u32[]{:S(2)}) collective-permute-start(bf16[256,768]{1,0:T(8,128)(2,1)} %param.33), channel_id=1, source_target_pairs={{0,2},{1,3},{2,0},{3,1},{4,6},{5,7},{6,4},{7,5},{8,10},{9,11},{10,... | collective-permute-start | bytes 1179656 | tf_op jit(solution)/shard_map/ppermute | solution.py:37
  14.3 17.9 %collective-permute-start.6 = (bf16[256,768]{1,0:T(8,128)(2,1)}, bf16[256,768]{1,0:T(8,128)(2,1)}, u32[]{:S(2)}, u32[]{:S(2)}) collective-permute-start(bf16[256,768]{1,0:T(8,128)(2,1)} %param.33), channel_id=1, source_target_pairs={{0,1},{1,0},{2,3},{3,2},{4,5},{5,4},{6,7},{7,6},{8,9},{9,8},{10,11... | collective-permute-start | bytes 1179656 | tf_op jit(solution)/shard_map/ppermute | solution.py:37
  26.3 34.2 %collective-permute-start.2 = (bf16[256,1816]{0,1:T(8,128)(2,1)S(1)}, bf16[256,1816]{0,1:T(8,128)(2,1)}, u32[]{:S(2)}, u32[]{:S(2)}) collective-permute-start(bf16[256,1816]{0,1:T(8,128)(2,1)S(1)} %slice.417), channel_id=1, source_target_pairs={{0,2},{1,3},{2,0},{3,1},{4,6},{5,7},{6,4},{7,5},{8,10},{9,11},{10,... | collective-permute-start | bytes 2789384 | tf_op jit(solution)/shard_map/ppermute | solution.py:37
  31.6 36.0 %collective-permute-start.1 = (bf16[256,1816]{0,1:T(8,128)(2,1)S(1)}, bf16[256,1816]{0,1:T(8,128)(2,1)S(1)}, u32[]{:S(2)}, u32[]{:S(2)}) collective-permute-start(bf16[256,1816]{0,1:T(8,128)(2,1)S(1)} %slice.417), channel_id=1, source_target_pairs={{0,1},{1,0},{2,3},{3,2},{4,5},{5,4},{6,7},{7,6},{8,9},{9,8},{10,11... | collective-permute-start | bytes 2789384 | tf_op jit(solution)/shard_map/ppermute | solution.py:37
  31.7 28.9 %collective-permute-start.7 = (bf16[256,768]{1,0:T(8,128)(2,1)S(1)}, bf16[256,768]{1,0:T(8,128)(2,1)S(1)}, u32[]{:S(2)}, u32[]{:S(2)}) collective-permute-start(bf16[256,768]{1,0:T(8,128)(2,1)S(1)} %copy-done.77), channel_id=1, source_target_pairs={{0,1},{1,0},{2,3},{3,2},{4,5},{5,4},{6,7},{7,6},{8,9},{9,8},{10,11... | collective-permute-start | bytes 1179656 | tf_op jit(solution)/shard_map/ppermute | solution.py:37
  60.5 8.5 %collective-permute-start.3 = (bf16[256,1816]{0,1:T(8,128)(2,1)}, bf16[256,1816]{0,1:T(8,128)(2,1)S(1)}, u32[]{:S(2)}, u32[]{:S(2)}) collective-permute-start(bf16[256,1816]{0,1:T(8,128)(2,1)} %collective-permute-done.2), channel_id=1, source_target_pairs={{0,1},{1,0},{2,3},{3,2},{4,5},{5,4},{6,7},{7,6},{8,9},{9,8},{10,11... | collective-permute-start | bytes 2789384 | tf_op jit(solution)/shard_map/ppermute | solution.py:37
  63.1 22.9 %collective-permute-start.8 = (bf16[448,256]{1,0:T(8,128)(2,1)S(1)}, bf16[448,256]{1,0:T(8,128)(2,1)S(1)}, u32[]{:S(2)}, u32[]{:S(2)}) collective-permute-start(bf16[448,256]{1,0:T(8,128)(2,1)S(1)} %get-tuple-element.121), channel_id=1, source_target_pairs={{0,8},{4,12},{8,0},{12,4},{16,24},{20,28},{24,16},{28,20},{1,9},{5... | collective-permute-start | bytes 688136 | tf_op jit(solution)/shard_map/ppermute | solution.py:37
  64.9 21.0 %collective-permute-start.9 = (bf16[448,256]{1,0:T(8,128)(2,1)S(1)}, bf16[448,256]{1,0:T(8,128)(2,1)S(1)}, u32[]{:S(2)}, u32[]{:S(2)}) collective-permute-start(bf16[448,256]{1,0:T(8,128)(2,1)S(1)} %get-tuple-element.121), channel_id=1, source_target_pairs={{0,16},{4,20},{8,24},{12,28},{16,0},{20,4},{24,8},{28,12},{1,17},{... | collective-permute-start | bytes 688136 | tf_op jit(solution)/shard_map/ppermute | solution.py:37
  67.5 18.5 %collective-permute-start.10 = (bf16[448,256]{1,0:T(8,128)(2,1)S(1)}, bf16[448,256]{1,0:T(8,128)(2,1)S(1)}, u32[]{:S(2)}, u32[]{:S(2)}) collective-permute-start(bf16[448,256]{1,0:T(8,128)(2,1)S(1)} %get-tuple-element.121), channel_id=1, source_target_pairs={{0,24},{4,28},{8,16},{12,20},{16,8},{20,12},{24,0},{28,4},{1,25},{... | collective-permute-start | bytes 688136 | tf_op jit(solution)/shard_map/ppermute | solution.py:37
  75.1 5.6 %collective-permute-start.5 = (bf16[3,1792]{1,0:T(4,128)(2,1)S(1)}, bf16[3,1792]{1,0:T(4,128)(2,1)S(1)}, u32[]{:S(2)}, u32[]{:S(2)}) collective-permute-start(bf16[3,1792]{1,0:T(4,128)(2,1)S(1)} %get-tuple-element.230), channel_id=1, source_target_pairs={{4,0},{8,4},{12,8},{16,12},{20,16},{24,20},{28,24},{5,1},{9,5},{13... | collective-permute-start | bytes 32264 | tf_op jit(solution)/shard_map/ppermute | solution.py:68
  87.1 25.5 %collective-permute-start.11 = (bf16[4,448,256]{2,1,0:T(8,128)(2,1)}, bf16[4,448,256]{2,1,0:T(8,128)(2,1)}, u32[]{:S(2)}, u32[]{:S(2)}) collective-permute-start(bf16[4,448,256]{2,1,0:T(8,128)(2,1)} %get-tuple-element.272), channel_id=1, source_target_pairs={{0,4},{4,0},{8,12},{12,8},{16,20},{20,16},{24,28},{28,24},{1,5},{5... | collective-permute-start | bytes 2752520 | tf_op jit(solution)/shard_map/ppermute | solution.py:37
  93.3 20.2 %all-to-all-start.1 = ((f32[8,2,24]{2,1,0:T(2,128)}), f32[8,2,24]{2,1,0:T(2,128)S(1)}, u32[]{:S(2)}, u32[]{:S(2)}) async-start(f32[8,2,24]{2,1,0:T(2,128)} %broadcast_in_dim.41), calls=%async_computation.1 | async-start | bytes 16384 | tf_op jit(solution)/shard_map/all_to_all | solution.py:911
  113.5 26.7 %all-to-all-start = ((bf16[8,2,16,1536]{3,2,1,0:T(8,128)(2,1)}), bf16[8,2,16,1536]{3,2,1,0:T(8,128)(2,1)S(1)}, u32[]{:S(2)}, u32[]{:S(2)}) async-start(bf16[8,2,16,1536]{3,2,1,0:T(8,128)(2,1)} %bitcast.223), calls=%async_computation | async-start | bytes 1572864 | tf_op jit(solution)/shard_map/all_to_all | solution.py:534
  121.6 80.9 %all-gather.11.cloned.1.call-start = ((), (), s32[]{:S(2)}) async-start(), calls=%async_computation.9 | async-start | bytes 5242880 | tf_op jit(solution)/shard_map/all_gather | solution.py:84
  142.0 28.8 %all-to-all-start.2 = ((bf16[8,2,16,1536]{3,2,1,0:T(8,128)(2,1)}), bf16[8,2,16,1536]{3,2,1,0:T(8,128)(2,1)S(1)}, u32[]{:S(2)}, u32[]{:S(2)}) async-start(bf16[8,2,16,1536]{3,2,1,0:T(8,128)(2,1)} %bitcast.17), calls=%async_computation.2 | async-start | bytes 1572864 | tf_op jit(solution)/shard_map/all_to_all | solution.py:539
  247.9 30.1 %all-to-all-start.3 = ((bf16[8,2,16,1536]{3,2,1,0:T(8,128)(2,1)}), bf16[8,2,16,1536]{3,2,1,0:T(8,128)(2,1)S(1)}, u32[]{:S(2)}, u32[]{:S(2)}) async-start(bf16[8,2,16,1536]{3,2,1,0:T(8,128)(2,1)} %bitcast.221), calls=%async_computation.3 | async-start | bytes 1572864 | tf_op jit(solution)/shard_map/all_to_all | solution.py:534
  253.8 270.0 %reduce-scatter.2.cloned.1.call-start = ((), (), s32[]{:S(2)}) async-start(), calls=%async_computation.10 | async-start | bytes 20545536 | tf_op jit(solution)/shard_map/reduce_scatter | solution.py:102
  279.8 41.0 %all-to-all-start.4 = ((bf16[8,2,16,1536]{3,2,1,0:T(8,128)(2,1)}), bf16[8,2,16,1536]{3,2,1,0:T(8,128)(2,1)S(1)}, u32[]{:S(2)}, u32[]{:S(2)}) async-start(bf16[8,2,16,1536]{3,2,1,0:T(8,128)(2,1)} %bitcast.39), calls=%async_computation.4 | async-start | bytes 1572864 | tf_op jit(solution)/shard_map/all_to_all | solution.py:539
  349.5 12.9 %collective-permute-start.12 = (bf16[3,1792]{1,0:T(4,128)(2,1)S(1)}, bf16[3,1792]{1,0:T(4,128)(2,1)S(1)}, u32[]{:S(2)}, u32[]{:S(2)}) collective-permute-start(bf16[3,1792]{1,0:T(4,128)(2,1)S(1)} %get-tuple-element.216), channel_id=1, source_target_pairs={{0,4},{4,8},{8,12},{12,16},{16,20},{20,24},{24,28},{1,5},{5,9},{9,... | collective-permute-start | bytes 32264 | tf_op jit(solution)/shard_map/ppermute | solution.py:67
  354.0 8.4 %collective-permute-start.13 = (bf16[3,1792]{1,0:T(4,128)(2,1)S(1)}, bf16[3,1792]{1,0:T(4,128)(2,1)S(1)}, u32[]{:S(2)}, u32[]{:S(2)}) collective-permute-start(bf16[3,1792]{1,0:T(4,128)(2,1)S(1)} %split.21), channel_id=1, source_target_pairs={{4,0},{8,4},{12,8},{16,12},{20,16},{24,20},{28,24},{5,1},{9,5},{13... | collective-permute-start | bytes 32264 | tf_op jit(solution)/shard_map/ppermute | solution.py:68
  355.3 40.6 %collective-permute-start.14 = (bf16[4,448,256]{2,1,0:T(8,128)(2,1)S(1)}, bf16[4,448,256]{2,1,0:T(8,128)(2,1)S(1)}, u32[]{:S(2)}, u32[]{:S(2)}) collective-permute-start(bf16[4,448,256]{2,1,0:T(8,128)(2,1)S(1)} %copy-done.64), channel_id=1, source_target_pairs={{0,4},{4,0},{8,12},{12,8},{16,20},{20,16},{24,28},{28,24},{1,5},{5... | collective-permute-start | bytes 2752520 | tf_op jit(solution)/shard_map/ppermute | solution.py:37
  407.7 11.8 %collective-permute-start.18 = (bf16[4,2,2,32,1920]{4,3,2,1,0:T(8,128)(2,1)}, bf16[4,2,2,32,1920]{4,3,2,1,0:T(8,128)(2,1)}, u32[]{:S(2)}, u32[]{:S(2)}) collective-permute-start(bf16[4,2,2,32,1920]{4,3,2,1,0:T(8,128)(2,1)} %dynamic-slice_bitcast_fusion), channel_id=1, source_target_pairs={{0,1},{1,0},{2,3},{3,2},{4,5},{5,4},{6,7},{7,6},{8,9},{9,8},{10,11... | collective-permute-start | bytes 5898248 | tf_op jit(solution)/shard_map/ppermute | solution.py:37
  414.5 15.3 %collective-permute-start.15 = (bf16[448,256]{1,0:T(8,128)(2,1)S(1)}, bf16[448,256]{1,0:T(8,128)(2,1)S(1)}, u32[]{:S(2)}, u32[]{:S(2)}) collective-permute-start(bf16[448,256]{1,0:T(8,128)(2,1)S(1)} %get-tuple-element.265), channel_id=1, source_target_pairs={{0,8},{4,12},{8,0},{12,4},{16,24},{20,28},{24,16},{28,20},{1,9},{5... | collective-permute-start | bytes 688136 | tf_op jit(solution)/shard_map/ppermute | solution.py:37
  417.1 17.2 %collective-permute-start.16 = (bf16[448,256]{1,0:T(8,128)(2,1)S(1)}, bf16[448,256]{1,0:T(8,128)(2,1)S(1)}, u32[]{:S(2)}, u32[]{:S(2)}) collective-permute-start(bf16[448,256]{1,0:T(8,128)(2,1)S(1)} %get-tuple-element.264), channel_id=1, source_target_pairs={{0,16},{4,20},{8,24},{12,28},{16,0},{20,4},{24,8},{28,12},{1,17},{... | collective-permute-start | bytes 688136 | tf_op jit(solution)/shard_map/ppermute | solution.py:37
  418.8 22.5 %collective-permute-start.17 = (bf16[448,256]{1,0:T(8,128)(2,1)S(1)}, bf16[448,256]{1,0:T(8,128)(2,1)S(1)}, u32[]{:S(2)}, u32[]{:S(2)}) collective-permute-start(bf16[448,256]{1,0:T(8,128)(2,1)S(1)} %get-tuple-element.263), channel_id=1, source_target_pairs={{0,24},{4,28},{8,16},{12,20},{16,8},{20,12},{24,0},{28,4},{1,25},{... | collective-permute-start | bytes 688136 | tf_op jit(solution)/shard_map/ppermute | solution.py:37
  422.7 28.0 %collective-permute-start.19 = (bf16[2,2,32,1920]{3,2,1,0:T(8,128)(2,1)S(1)}, bf16[2,2,32,1920]{3,2,1,0:T(8,128)(2,1)S(1)}, u32[]{:S(2)}, u32[]{:S(2)}) collective-permute-start(bf16[2,2,32,1920]{3,2,1,0:T(8,128)(2,1)S(1)} %get-tuple-element.261), channel_id=1, source_target_pairs={{0,2},{1,3},{2,0},{3,1},{4,6},{5,7},{6,4},{7,5},{8,10},{9,11},{10,... | collective-permute-start | bytes 1474568 | tf_op jit(solution)/shard_map/ppermute | solution.py:37
  425.0 25.8 %collective-permute-start.20 = (bf16[2,2,32,1920]{3,2,1,0:T(8,128)(2,1)S(1)}, bf16[2,2,32,1920]{3,2,1,0:T(8,128)(2,1)S(1)}, u32[]{:S(2)}, u32[]{:S(2)}) collective-permute-start(bf16[2,2,32,1920]{3,2,1,0:T(8,128)(2,1)S(1)} %get-tuple-element.259), channel_id=1, source_target_pairs={{0,4},{4,0},{8,12},{12,8},{16,20},{20,16},{24,28},{28,24},{1,5},{5... | collective-permute-start | bytes 1474568 | tf_op jit(solution)/shard_map/ppermute | solution.py:37
  459.8 8.2 %collective-permute-start.21 = (f32[104,128]{1,0:T(8,128)S(1)}, f32[104,128]{1,0:T(8,128)S(1)}, u32[]{:S(2)}, u32[]{:S(2)}) collective-permute-start(f32[104,128]{1,0:T(8,128)S(1)} %pad_bitcast_fusion), channel_id=1, source_target_pairs={{0,1},{1,0},{2,3},{3,2},{4,5},{5,4},{6,7},{7,6},{8,9},{9,8},{10,11... | collective-permute-start | bytes 159752 | tf_op jit(solution)/shard_map/ppermute | solution.py:37
  462.3 17.0 %collective-permute-start.23 = (bf16[4,2,2,32,768]{4,3,1,0,2:T(8,128)(2,1)S(1)}, bf16[4,2,2,32,768]{4,3,1,0,2:T(8,128)(2,1)S(1)}, u32[]{:S(2)}, u32[]{:S(2)}) collective-permute-start(bf16[4,2,2,32,768]{4,3,1,0,2:T(8,128)(2,1)S(1)} %bitcast.236), channel_id=1, source_target_pairs={{0,1},{1,0},{2,3},{3,2},{4,5},{5,4},{6,7},{7,6},{8,9},{9,8},{10,11... | collective-permute-start | bytes 2359304 | tf_op jit(solution)/shard_map/ppermute | solution.py:37
  463.3 12.6 %collective-permute-start.24 = (bf16[2,32,1920]{2,1,0:T(8,128)(2,1)S(1)}, bf16[2,32,1920]{2,1,0:T(8,128)(2,1)S(1)}, u32[]{:S(2)}, u32[]{:S(2)}) collective-permute-start(bf16[2,32,1920]{2,1,0:T(8,128)(2,1)S(1)} %get-tuple-element.296), channel_id=1, source_target_pairs={{0,4},{4,0},{8,12},{12,8},{16,20},{20,16},{24,28},{28,24},{1,5},{5... | collective-permute-start | bytes 737288 | tf_op jit(solution)/shard_map/ppermute | solution.py:37
  463.7 15.6 %collective-permute-start.25 = (bf16[2,32,1920]{2,1,0:T(8,128)(2,1)S(1)}, bf16[2,32,1920]{2,1,0:T(8,128)(2,1)S(1)}, u32[]{:S(2)}, u32[]{:S(2)}) collective-permute-start(bf16[2,32,1920]{2,1,0:T(8,128)(2,1)S(1)} %get-tuple-element.294), channel_id=1, source_target_pairs={{0,2},{1,3},{2,0},{3,1},{4,6},{5,7},{6,4},{7,5},{8,10},{9,11},{10,... | collective-permute-start | bytes 737288 | tf_op jit(solution)/shard_map/ppermute | solution.py:37
  468.0 18.3 %collective-permute-start.22 = (f32[104,128]{1,0:T(8,128)S(1)}, f32[104,128]{1,0:T(8,128)S(1)}, u32[]{:S(2)}, u32[]{:S(2)}) collective-permute-start(f32[104,128]{1,0:T(8,128)S(1)} %fusion.93), channel_id=1, source_target_pairs={{0,2},{1,3},{2,0},{3,1},{4,6},{5,7},{6,4},{7,5},{8,10},{9,11},{10,... | collective-permute-start | bytes 159752 | tf_op jit(solution)/shard_map/ppermute | solution.py:37
  479.7 8.9 %collective-permute-start.26 = (bf16[32,1920]{1,0:T(8,128)(2,1)S(1)}, bf16[32,1920]{1,0:T(8,128)(2,1)S(1)}, u32[]{:S(2)}, u32[]{:S(2)}) collective-permute-start(bf16[32,1920]{1,0:T(8,128)(2,1)S(1)} %get-tuple-element.292), channel_id=1, source_target_pairs={{0,8},{4,12},{8,0},{12,4},{16,24},{20,28},{24,16},{28,20},{1,9},{5... | collective-permute-start | bytes 368648 | tf_op jit(solution)/shard_map/ppermute | solution.py:37
  479.8 13.1 %collective-permute-start.27 = (bf16[32,1920]{1,0:T(8,128)(2,1)S(1)}, bf16[32,1920]{1,0:T(8,128)(2,1)S(1)}, u32[]{:S(2)}, u32[]{:S(2)}) collective-permute-start(bf16[32,1920]{1,0:T(8,128)(2,1)S(1)} %get-tuple-element.293), channel_id=1, source_target_pairs={{0,16},{4,20},{8,24},{12,28},{16,0},{20,4},{24,8},{28,12},{1,17},{... | collective-permute-start | bytes 368648 | tf_op jit(solution)/shard_map/ppermute | solution.py:37
  482.8 11.0 %collective-permute-start.28 = (bf16[32,1920]{1,0:T(8,128)(2,1)S(1)}, bf16[32,1920]{1,0:T(8,128)(2,1)S(1)}, u32[]{:S(2)}, u32[]{:S(2)}) collective-permute-start(bf16[32,1920]{1,0:T(8,128)(2,1)S(1)} %get-tuple-element.290), channel_id=1, source_target_pairs={{0,24},{4,28},{8,16},{12,20},{16,8},{20,12},{24,0},{28,4},{1,25},{... | collective-permute-start | bytes 368648 | tf_op jit(solution)/shard_map/ppermute | solution.py:37
  484.5 13.5 %collective-permute-start.29 = (bf16[2,2,32,768]{3,2,1,0:T(8,128)(2,1)S(1)}, bf16[2,2,32,768]{3,2,1,0:T(8,128)(2,1)S(1)}, u32[]{:S(2)}, u32[]{:S(2)}) collective-permute-start(bf16[2,2,32,768]{3,2,1,0:T(8,128)(2,1)S(1)} %get-tuple-element.304), channel_id=1, source_target_pairs={{0,2},{1,3},{2,0},{3,1},{4,6},{5,7},{6,4},{7,5},{8,10},{9,11},{10,... | collective-permute-start | bytes 589832 | tf_op jit(solution)/shard_map/ppermute | solution.py:37
  486.4 11.7 %collective-permute-start.30 = (bf16[2,2,32,768]{3,2,1,0:T(8,128)(2,1)S(1)}, bf16[2,2,32,768]{3,2,1,0:T(8,128)(2,1)S(1)}, u32[]{:S(2)}, u32[]{:S(2)}) collective-permute-start(bf16[2,2,32,768]{3,2,1,0:T(8,128)(2,1)S(1)} %bitcast.242), channel_id=1, source_target_pairs={{0,4},{4,0},{8,12},{12,8},{16,20},{20,16},{24,28},{28,24},{1,5},{5... | collective-permute-start | bytes 589832 | tf_op jit(solution)/shard_map/ppermute | solution.py:37
  498.0 6.9 %collective-permute-start.31 = (f32[104,128]{1,0:T(8,128)S(1)}, f32[104,128]{1,0:T(8,128)S(1)}, u32[]{:S(2)}, u32[]{:S(2)}) collective-permute-start(f32[104,128]{1,0:T(8,128)S(1)} %fusion.150), channel_id=1, source_target_pairs={{0,4},{4,0},{8,12},{12,8},{16,20},{20,16},{24,28},{28,24},{1,5},{5... | collective-permute-start | bytes 159752 | tf_op jit(solution)/shard_map/ppermute | solution.py:37
  500.6 6.3 %collective-permute-start.32 = (bf16[2,32,768]{2,1,0:T(8,128)(2,1)S(1)}, bf16[2,32,768]{2,1,0:T(8,128)(2,1)S(1)}, u32[]{:S(2)}, u32[]{:S(2)}) collective-permute-start(bf16[2,32,768]{2,1,0:T(8,128)(2,1)S(1)} %get-tuple-element.313), channel_id=1, source_target_pairs={{0,4},{4,0},{8,12},{12,8},{16,20},{20,16},{24,28},{28,24},{1,5},{5... | collective-permute-start | bytes 294920 | tf_op jit(solution)/shard_map/ppermute | solution.py:37
  500.8 7.9 %collective-permute-start.33 = (bf16[2,32,768]{2,1,0:T(8,128)(2,1)S(1)}, bf16[2,32,768]{2,1,0:T(8,128)(2,1)S(1)}, u32[]{:S(2)}, u32[]{:S(2)}) collective-permute-start(bf16[2,32,768]{2,1,0:T(8,128)(2,1)S(1)} %get-tuple-element.311), channel_id=1, source_target_pairs={{0,2},{1,3},{2,0},{3,1},{4,6},{5,7},{6,4},{7,5},{8,10},{9,11},{10,... | collective-permute-start | bytes 294920 | tf_op jit(solution)/shard_map/ppermute | solution.py:37
  508.7 5.3 collective-permute-start.34
  509.5 6.7 %collective-permute-start.38 = (bf16[32,768]{1,0:T(8,128)(2,1)S(1)}, bf16[32,768]{1,0:T(8,128)(2,1)S(1)}, u32[]{:S(2)}, u32[]{:S(2)}) collective-permute-start(bf16[32,768]{1,0:T(8,128)(2,1)S(1)} %get-tuple-element.310), channel_id=1, source_target_pairs={{0,24},{4,28},{8,16},{12,20},{16,8},{20,12},{24,0},{28,4},{1,25},{... | collective-permute-start | bytes 147464 | tf_op jit(solution)/shard_map/ppermute | solution.py:37
  511.7 7.0 %collective-permute-start.37 = (bf16[32,768]{1,0:T(8,128)(2,1)S(1)}, bf16[32,768]{1,0:T(8,128)(2,1)S(1)}, u32[]{:S(2)}, u32[]{:S(2)}) collective-permute-start(bf16[32,768]{1,0:T(8,128)(2,1)S(1)} %get-tuple-element.309), channel_id=1, source_target_pairs={{0,16},{4,20},{8,24},{12,28},{16,0},{20,4},{24,8},{28,12},{1,17},{... | collective-permute-start | bytes 147464 | tf_op jit(solution)/shard_map/ppermute | solution.py:37
  512.4 6.3 %collective-permute-start.36 = (bf16[32,768]{1,0:T(8,128)(2,1)S(1)}, bf16[32,768]{1,0:T(8,128)(2,1)S(1)}, u32[]{:S(2)}, u32[]{:S(2)}) collective-permute-start(bf16[32,768]{1,0:T(8,128)(2,1)S(1)} %get-tuple-element.308), channel_id=1, source_target_pairs={{0,8},{4,12},{8,0},{12,4},{16,24},{20,28},{24,16},{28,20},{1,9},{5... | collective-permute-start | bytes 147464 | tf_op jit(solution)/shard_map/ppermute | solution.py:37
  514.0 6.8 %collective-permute-start.35 = (f32[104,128]{1,0:T(8,128)S(1)}, f32[104,128]{1,0:T(8,128)S(1)}, u32[]{:S(2)}, u32[]{:S(2)}) collective-permute-start(f32[104,128]{1,0:T(8,128)S(1)} %add.456), channel_id=1, source_target_pairs={{0,16},{4,20},{8,24},{12,28},{16,0},{20,4},{24,8},{28,12},{1,17},{... | collective-permute-start | bytes 159752 | tf_op jit(solution)/shard_map/ppermute | solution.py:37
  (119 other events, 1159.3 us)
Sparse Core Ops, SparseCore 0:
  10.2 45.3 all-gather.4
  57.1 35.6 all-gather.6
  94.3 58.2 all-gather.8
  154.1 34.5 all-gather.10
  278.1 241.1 reduce-scatter.1
